TPU v7x, 512 devices: a whole 4x8x8 slice. The times are simulated.
512 devices in a mesh: seq: 128 (over z, y, core), chan: 4 (over x).
Axes of the slice: x: 4, y: 8, z: 8, core: 2. Of those that a mesh axis runs over, the one named last changes fastest.
Arguments:
- tokens: bfloat16 [32768, 8192], P('seq', 'chan'), may hold values from -6 to 6
- in_weight: bfloat16 [8192, 3, 256], P('chan'), may hold values from -0.0625 to 0.0625
- short_weight: float32 [3, 3, 256], P(None, None, 'chan'), may hold values from -3 to 3
- residue: float32 [256, 16], P('chan'), may hold values from -2 to 2
- rates: float32 [256, 16], P('chan'), may hold values from 7.6293945e-06 to 0.05
- skip: float32 [256], P('chan'), may hold values from -4 to 4
Outputs:
- mixed: bfloat16 [32768, 256], P('seq', 'chan')
All inputs are finite; a program needn't handle non-finite values.
Results may differ from a plain program's by a relative error of at most 0.005.
Values sent between devices are 32-bit elements; how exact they have to be, the bound alone decides.
No kernel may reach another device: no remote copies, remote signals or barrier semaphores. Data moves between devices by JAX's collectives and lax.ppermute only.
A program may use at most 64 MiB of HBM per device.

v0:
```python
import math

import jax
import jax.numpy as jnp
from jax import lax
from jax.sharding import PartitionSpec as P

highest = lax.Precision.HIGHEST


def from_behind(block, axis, distance):
    devices = range(lax.axis_size(axis))
    route = [(i - distance, i) for i in devices if i - distance in devices]
    return lax.ppermute(block, axis, route)


def rotation(counts, period):
    reduced = counts % period
    centred = jnp.where(reduced > period // 2, reduced - period, reduced)
    phase_angle = centred.astype(jnp.float32) * (2.0 * math.pi / period)
    return (jnp.cos(phase_angle), jnp.sin(phase_angle))


def fourier_table(length_dft):
    steps_in = jnp.arange(length_dft, dtype=jnp.int32)
    return rotation(steps_in[:, None] * steps_in[None, :], length_dft)


def fold_table(count_seq):
    freq_fold = jnp.arange(2 * count_seq, dtype=jnp.int32)
    shard_pos = jnp.arange(count_seq, dtype=jnp.int32)
    return rotation(freq_fold[:, None] * shard_pos[None, :], 2 * count_seq)


def twist(values, cos_tw, sin_tw):
    real_part = values[0] * cos_tw + values[1] * sin_tw
    imag_part = values[1] * cos_tw - values[0] * sin_tw
    return jnp.stack([real_part, imag_part])


def along_rows(received):
    cos_rows, sin_rows = fourier_table(received.shape[2])
    real_part = received[0]
    imag_part = received[1]
    out_real = jnp.einsum("km,emc->ekc", cos_rows, real_part, precision=highest) + jnp.einsum(
        "km,emc->ekc", sin_rows, imag_part, precision=highest
    )
    out_imag = jnp.einsum("km,emc->ekc", cos_rows, imag_part, precision=highest) - jnp.einsum(
        "km,emc->ekc", sin_rows, real_part, precision=highest
    )
    return jnp.stack([out_real, out_imag])


def forward(signal):
    count_seq = lax.axis_size("seq")
    device_pos = lax.axis_index("seq")
    local_rows, channels = signal.shape
    length_fft = 2 * count_seq * local_rows
    block_rows = local_rows // count_seq
    cos_fold, sin_fold = fold_table(count_seq)
    portion = lax.all_to_all(
        signal.reshape(count_seq, block_rows, channels),
        "seq",
        split_axis=0,
        concat_axis=0,
        tiled=True,
    )
    real_part = jnp.einsum("ka,arc->krc", cos_fold, portion, precision=highest)
    imag_part = -jnp.einsum("ka,arc->krc", sin_fold, portion, precision=highest)
    spread = jnp.stack([real_part, imag_part])
    rows_here = device_pos * block_rows + jnp.arange(block_rows, dtype=jnp.int32)
    freq_fold = jnp.arange(2 * count_seq, dtype=jnp.int32)
    cos_tw, sin_tw = rotation(freq_fold[:, None] * rows_here[None, :], length_fft)
    spread = twist(spread, cos_tw[:, :, None], sin_tw[:, :, None])
    values = along_rows(lax.all_to_all(spread, "seq", split_axis=1, concat_axis=2, tiled=True))
    return (values, device_pos)


def inverse(spectrum, spectral_pos):
    count_seq = lax.axis_size("seq")
    local_rows = spectrum.shape[2]
    channels = spectrum.shape[3]
    length_fft = 2 * count_seq * local_rows
    cos_rows, sin_rows = fourier_table(local_rows)
    real_part = spectrum[0]
    imag_part = spectrum[1]
    back_real = jnp.einsum("mk,ekc->emc", cos_rows, real_part, precision=highest) - jnp.einsum(
        "mk,ekc->emc", sin_rows, imag_part, precision=highest
    )
    back_imag = jnp.einsum("mk,ekc->emc", cos_rows, imag_part, precision=highest) + jnp.einsum(
        "mk,ekc->emc", sin_rows, real_part, precision=highest
    )
    freq_low = 2 * spectral_pos + jnp.arange(2, dtype=jnp.int32)
    cos_tw, sin_tw = rotation(
        freq_low[:, None] * jnp.arange(local_rows, dtype=jnp.int32)[None, :], length_fft
    )
    values = twist(jnp.stack([back_real, back_imag]), cos_tw[:, :, None], -sin_tw[:, :, None])
    cos_fold, sin_fold = fold_table(count_seq)
    received = lax.all_to_all(values, "seq", split_axis=2, concat_axis=1, tiled=True)
    gathered = jnp.einsum("ka,krc->arc", cos_fold, received[0], precision=highest) - jnp.einsum(
        "ka,krc->arc", sin_fold, received[1], precision=highest
    )
    placed = lax.all_to_all(gathered / length_fft, "seq", split_axis=0, concat_axis=1, tiled=True)
    return placed.reshape(local_rows, channels)


def per_device(tokens, in_weight, short_weight, residue, rates, skip):
    partials = jnp.einsum("td,djc->tjc", tokens, in_weight, preferred_element_type=jnp.float32)
    projected = lax.psum_scatter(partials, "chan", scatter_dimension=2, tiled=True)
    earlier = from_behind(projected[-2:], "seq", 1)
    extended = jnp.concatenate([earlier, projected], axis=0)
    features = (
        short_weight[0] * projected
        + short_weight[1] * extended[1:-1]
        + short_weight[2] * extended[:-2]
    )
    queries = features[:, 0, :]
    mixed_in = features[:, 1, :] * features[:, 2, :]
    local_rows, channels = mixed_in.shape
    device_pos = lax.axis_index("seq")
    positions = (device_pos * local_rows + jnp.arange(local_rows, dtype=jnp.int32)).astype(
        jnp.float32
    )
    pole_weight = residue * jnp.sqrt(2.0 * rates)
    impulse = jnp.sum(pole_weight[None] * jnp.exp(-rates[None] * positions[:, None, None]), axis=-1)
    both_spectra, spectral_pos = forward(jnp.concatenate([mixed_in, impulse], axis=1))
    spectrum = both_spectra[..., :channels]
    response = both_spectra[..., channels:]
    real_part = spectrum[0] * response[0] - spectrum[1] * response[1]
    imag_part = spectrum[0] * response[1] + spectrum[1] * response[0]
    convolved = inverse(jnp.stack([real_part, imag_part]), spectral_pos)
    return (queries * (convolved + skip[None, :] * mixed_in)).astype(jnp.bfloat16)


def solution(mesh):
    in_specs = (
        P("seq", "chan"),
        P("chan", None, None),
        P(None, None, "chan"),
        P("chan", None),
        P("chan", None),
        P("chan"),
    )
    out_specs = P("seq", "chan")
    return jax.shard_map(
        per_device, mesh=mesh, in_specs=in_specs, out_specs=out_specs, check_vma=False
    )
```

profile of v0, /device:TPU:1, one launch (start us, length us, event | category | flops | bytes accessed | tf_op | source)
XLA Modules:
  0.0 194.7 jit_solution(10196828993539564431)
XLA Ops:
  6.6 1.8 copy-done
  8.4 3.4 %fusion.2 = f32[256,3,256]{0,2,1:T(8,128)} fusion(bf16[2048,3,256]{2,0,1:T(8,128)(2,1)S(1)} %copy-done, bf16[256,2048]{1,0:T(8,128)(2,1)} %param.6), kind=kOutput, calls=%fused_computation.7 | convolution fusion | flops 805306368 | bytes 4980736 | tf_op jit(solution)/shard_map/td,djc->tjc/dot_general | solution.py:108
  12.1 32.1 %reduce-scatter.2.cloned.1.call-done = f32[256,3,64]{0,2,1:T(8,128)} async-done(((f32[256,3,256]{0,2,1:T(8,128)}), f32[256,3,64]{0,2,1:T(8,128)}) %reduce-scatter.2.cloned.1.call-update) | async-done | bytes 196624 | tf_op jit(solution)/shard_map/reduce_scatter | solution.py:109
  45.2 4.7 %collective-permute-start = (f32[2,3,64]{0,2,1:T(8,128)S(1)}, f32[2,3,64]{0,2,1:T(8,128)S(1)}, u32[]{:S(2)}, u32[]{:S(2)}) collective-permute-start(f32[2,3,64]{0,2,1:T(8,128)S(1)} %slice.86), channel_id=1, source_target_pairs={{0,4},{4,8},{8,12},{12,16},{16,20},{20,24},{24,28},{28,32},{32,36}... | collective-permute-start | bytes 4616 | tf_op jit(solution)/shard_map/ppermute | solution.py:14
  52.2 1.5 fusion.25
  54.5 1.8 pad_maximum_fusion.3
  56.2 16.1 %all-to-all-start = ((f32[128,2,128]{2,1,0:T(2,128)}), f32[128,2,128]{2,1,0:T(2,128)S(1)}, u32[]{:S(2)}, u32[]{:S(2)}) async-start(f32[128,2,128]{2,1,0:T(2,128)} %pad_maximum_fusion.3), calls=%async_computation.1 | async-start | bytes 262144 | tf_op jit(solution)/shard_map/all_to_all | solution.py:61
  72.5 12.6 %all-to-all-done = f32[128,2,128]{2,1,0:T(2,128)S(1)} async-done(((f32[128,2,128]{2,1,0:T(2,128)}), f32[128,2,128]{2,1,0:T(2,128)S(1)}, u32[]{:S(2)}, u32[]{:S(2)}) %all-to-all-start) | async-done | bytes 131104 | tf_op jit(solution)/shard_map/all_to_all | solution.py:61
  88.1 6.8 %all-to-all-start.1 = ((f32[2,256,2,128]{3,2,0,1:T(2,128)}), f32[2,256,2,128]{3,2,0,1:T(2,128)}, u32[]{:S(2)}, u32[]{:S(2)}) async-start(f32[2,256,2,128]{3,2,0,1:T(2,128)} %copy.61), calls=%async_computation.2 | async-start | bytes 1048576 | tf_op jit(solution)/shard_map/all_to_all | solution.py:75
  95.0 20.0 %all-to-all-done.1 = f32[2,256,2,128]{3,2,0,1:T(2,128)} async-done(((f32[2,256,2,128]{3,2,0,1:T(2,128)}), f32[2,256,2,128]{3,2,0,1:T(2,128)}, u32[]{:S(2)}, u32[]{:S(2)}) %all-to-all-start.1) | async-done | bytes 524320 | tf_op jit(solution)/shard_map/all_to_all | solution.py:75
  116.3 1.5 fusion.17
  117.8 1.5 fusion.15
  119.3 1.5 fusion.1
  120.8 1.5 fusion
  125.1 1.4 convolution_add_fusion.1
  126.5 1.4 add_bitcast_fusion.1
  128.6 1.9 copy.67
  130.5 2.5 %reshape.167 = f32[128,1,512]{2,1,0:T(1,128)} reshape(f32[256,2,2,64]{3,2,1,0:T(2,128)} %bitcast.108) | data formatting | bytes 524288
  133.1 21.0 %all_to_all.44 = f32[128,1,512]{2,1,0:T(1,128)} all-to-all(f32[128,1,512]{2,1,0:T(1,128)} %reshape.167), channel_id=1, replica_groups=mesh['seq'=128,'chan'=4] {'seq'}, dimensions={0} | all-to-all | bytes 524288 | tf_op jit(solution)/shard_map/all_to_all | solution.py:99
  154.6 2.9 %reduce = f32[128,512]{1,0:T(8,128)} reduce(f32[128,1,512]{2,1,0:T(1,128)} %all_to_all.44, f32[]{:T(128)} %broadcast.440), dimensions={1}, to_apply=%all_to_all.36.reduce_sub_computation | reduce | bytes 524292 | tf_op jit(solution)/shard_map/all_to_all | solution.py:99
  157.5 2.1 %reshape.168 = f32[256,2,2,64]{3,2,1,0:T(2,128)} reshape(f32[128,512]{1,0:T(8,128)} %reduce) | data formatting | bytes 524288
  163.4 1.4 fusion.57
  164.8 1.8 copy.71
  169.7 16.4 %all_to_all.45 = f32[128,1,128]{2,1,0:T(1,128)S(1)} all-to-all(f32[128,1,128]{2,1,0:T(1,128)S(1)} %reshape.169), channel_id=1, replica_groups=mesh['seq'=128,'chan'=4] {'seq'}, dimensions={0} | all-to-all | bytes 131072 | tf_op jit(solution)/shard_map/all_to_all | solution.py:103
  (51 shorter events, 21.2 us)
Async XLA Ops:
  6.5 1.9 copy-start
  6.5 5.4 %copy-start.3 = (f32[64,16]{0,1:T(8,128)S(1)}, f32[64,16]{0,1:T(8,128)}, u32[]{:S(2)}) copy-start(f32[64,16]{0,1:T(8,128)} %param.10) | copy-start | bytes 12292
  6.5 5.4 %copy-start.2 = (f32[64,16]{0,1:T(8,128)S(1)}, f32[64,16]{0,1:T(8,128)}, u32[]{:S(2)}) copy-start(f32[64,16]{0,1:T(8,128)} %param.9) | copy-start | bytes 12292
  6.5 5.6 %copy-start.4 = (f32[3,3,64]{2,1,0:T(4,128)S(1)}, f32[3,3,64]{2,1,0:T(4,128)}, u32[]{:S(2)}) copy-start(f32[3,3,64]{2,1,0:T(4,128)} %param.8) | copy-start | bytes 6916
  6.5 37.7 %reduce-scatter.2.cloned.1.call-start = ((), (), s32[]{:S(2)}) async-start(), calls=%async_computation.5 | async-start | bytes 983040 | tf_op jit(solution)/shard_map/reduce_scatter | solution.py:109
  45.2 6.4 %collective-permute-start = (f32[2,3,64]{0,2,1:T(8,128)S(1)}, f32[2,3,64]{0,2,1:T(8,128)S(1)}, u32[]{:S(2)}, u32[]{:S(2)}) collective-permute-start(f32[2,3,64]{0,2,1:T(8,128)S(1)} %slice.86), channel_id=1, source_target_pairs={{0,4},{4,8},{8,12},{12,16},{16,20},{20,24},{24,28},{28,32},{32,36}... | collective-permute-start | bytes 4616 | tf_op jit(solution)/shard_map/ppermute | solution.py:14
  51.6 0.6 copy-start.1
  56.2 28.9 %all-to-all-start = ((f32[128,2,128]{2,1,0:T(2,128)}), f32[128,2,128]{2,1,0:T(2,128)S(1)}, u32[]{:S(2)}, u32[]{:S(2)}) async-start(f32[128,2,128]{2,1,0:T(2,128)} %pad_maximum_fusion.3), calls=%async_computation.1 | async-start | bytes 262144 | tf_op jit(solution)/shard_map/all_to_all | solution.py:61
  88.1 26.9 %all-to-all-start.1 = ((f32[2,256,2,128]{3,2,0,1:T(2,128)}), f32[2,256,2,128]{3,2,0,1:T(2,128)}, u32[]{:S(2)}, u32[]{:S(2)}) async-start(f32[2,256,2,128]{3,2,0,1:T(2,128)} %copy.61), calls=%async_computation.2 | async-start | bytes 1048576 | tf_op jit(solution)/shard_map/all_to_all | solution.py:75
  159.6 27.5 %copy-start.5 = (f32[64]{0:T(128)S(1)}, f32[64]{0:T(128)}, u32[]{:S(2)}) copy-start(f32[64]{0:T(128)} %param.11) | copy-start | bytes 772
Sparse Core Ops, SparseCore 0:
  12.0 32.1 reduce-scatter.1
where the time goes:
time: 196 us; the launch traced here: 195 us
  waiting for transfers between devices  65.8 us (34%)
  blocking collectives  37.5 us (19%)
  starting transfers between devices  27.7 us (14%)
  local copies, waits for them, and re-layouts  21.2 us (11%)
  matrix products  18.9 us (10%)
  between operations  13.7 us (7%)
  other arithmetic  10 us (5%)
    reduce_scatter x1, waiting for transfers between devices, per_device(): lax.psum_scatter(partials, 'chan', scatter_dimension=2, tiled=True)  32.1 us
    all_to_all x1, blocking collectives, inverse(): lax.all_to_all(values, 'seq', split_axis=2, concat_axis=1, tiled=True)  21 us
    all_to_all x1, waiting for transfers between devices, forward(): lax.all_to_all(spread, 'seq', split_axis=1, concat_axis=2, tiled=True)  20 us
    all_to_all x1, blocking collectives, inverse(): lax.all_to_all(gathered / length_fft, 'seq', split_axis=0, concat_axis=1,...  16.4 us
    all_to_all x1, starting transfers between devices, forward(): lax.all_to_all(signal.reshape(count_seq, block_rows, channels), 'seq', sp...  16.1 us
    all_to_all x1, waiting for transfers between devices, forward(): lax.all_to_all(signal.reshape(count_seq, block_rows, channels), 'seq', sp...  12.6 us
    unnamed x16, local copies, waits for them, and re-layouts  7.4 us
    all_to_all x1, starting transfers between devices, forward(): lax.all_to_all(spread, 'seq', split_axis=1, concat_axis=2, tiled=True)  6.78 us
  transfers between devices with their start and end apart: 4, of which 4 were waited for; matrix products, arithmetic and copies ran while one was open for 0% of the time, Pallas kernels for 0%

commit v1 on v0

v1 whole, which is shorter than its diff:
```python
import functools

import jax
import jax.numpy as jnp
from jax import lax
from jax.experimental import pallas as pl
from jax.experimental.pallas import tpu as pltpu
from jax.sharding import Mesh, PartitionSpec as P

NEAR = 16
STEP = 8
F32 = jnp.float32


def lanes_of(shape):
    return lax.broadcasted_iota(jnp.int32, shape, 1)


def rows_of(shape):
    return lax.broadcasted_iota(jnp.int32, shape, 0)


def swap(tile):
    return pltpu.roll(tile, tile.shape[1] // 2, 1)


def twice(row):
    return jnp.concatenate([row, row], axis=1)


def folded(poles):
    half = poles.shape[0] // 2
    return jnp.concatenate([poles[:half], poles[half:]], axis=1)


def project_kernel(tok_ref, w_ref, out_ref):
    acc = jnp.dot(tok_ref[...], w_ref[0], preferred_element_type=F32)
    rows = acc.shape[0] // 2
    for pair in range(acc.shape[1] // 128):
        early = acc[:rows, 128 * pair : 128 * (pair + 1)]
        late = acc[rows:, 128 * pair : 128 * (pair + 1)]
        left = lanes_of(early.shape) < 64
        out_ref[2 * pair, 0] = jnp.where(left, early, swap(late))
        out_ref[2 * pair + 1, 0] = jnp.where(left, swap(early), late)


def project(tokens, weight):
    rows, depth = tokens.shape
    streams, _, width = weight.shape
    chan = width // 64
    return pl.pallas_call(
        project_kernel,
        grid=(streams,),
        in_specs=[
            pl.BlockSpec((rows, depth), lambda s: (0, 0)),
            pl.BlockSpec((1, depth, width), lambda s: (s, 0, 0)),
        ],
        out_specs=pl.BlockSpec((chan, 1, rows // 2, 128), lambda s: (0, s, 0, 0)),
        out_shape=jax.ShapeDtypeStruct((chan, streams, rows // 2, 128), F32),
        compiler_params=pltpu.CompilerParams(vmem_limit_bytes=32 * 2**20),
        name="project",
    )(tokens, weight)


def local_kernel(part_ref, short_ref, residue_ref, rates_ref, send_ref, q_ref, x_ref, y_ref, half_ref, own_ref):
    count = part_ref.shape[0]
    rows, width = q_ref.shape
    lane = lanes_of((1, width))
    right = lane >= width // 2
    row = rows_of((rows, width))
    feats, edges = [], []
    for s in range(3):
        p = part_ref[0, s]
        for i in range(1, count):
            p = p + part_ref[i, s]
        tap = [twice(short_ref[k, s : s + 1, :]) for k in range(3)]
        before = jnp.where(right, swap(p[rows - 8 :]), 0.0)
        one = jnp.where(row < 1, before[7:8], pltpu.roll(p, 1, 0))
        two = pltpu.roll(p, 2, 0)
        two = jnp.where(row == 0, before[6:7], jnp.where(row == 1, before[7:8], two))
        feats.append(tap[0] * p + tap[1] * one + tap[2] * two)
        edges.append((tap[1] * p[rows - 1 :] + tap[2] * p[rows - 2 : rows - 1], tap[2] * p[rows - 1 :]))
    q, a, b = feats
    q_ref[...] = q
    x = jnp.where(jnp.logical_and(row < 2, jnp.logical_not(right)), 0.0, a * b)
    x_ref[...] = x
    tile = [
        jnp.where(right, swap(b[0:1]), a[0:1]),
        jnp.where(right, swap(b[1:2]), a[1:2]),
        jnp.where(right, edges[2][0], swap(edges[1][0])),
        jnp.where(right, edges[2][1], swap(edges[1][1])),
        jnp.where(right, edges[0][1], swap(edges[0][0])),
    ]
    own = jnp.concatenate(tile + [jnp.zeros((3, width), F32)], axis=0)
    own_ref[...] = own

    rates = twice(rates_ref[...])
    weight = twice(residue_ref[...]) * jnp.sqrt(2.0 * rates)
    poles = rates.shape[0]
    inner = rows_of((STEP, width))
    step_pos = inner.astype(F32)
    impulse = [jnp.sum(weight * jnp.exp(-rates * float(u)), axis=0, keepdims=True) for u in range(STEP)]
    near = [jnp.where(inner >= u, impulse[u], 0.0) for u in range(STEP)]
    decay = jnp.exp(-float(STEP) * rates)
    into, outof, fade = [], [], []
    for r in range(poles):
        rate = rates[r : r + 1]
        into.append(jnp.exp(-rate * (STEP - 1.0 - step_pos)))
        outof.append(weight[r : r + 1] * jnp.exp(-rate * (step_pos + 1.0)))
        fade.append(decay[r : r + 1])
    state = [None] * poles
    for k in range(rows // STEP):
        xk = x[k * STEP : (k + 1) * STEP]
        yk = near[0] * xk
        for u in range(1, STEP):
            yk = yk + near[u] * pltpu.roll(xk, u, 0)
        for r in range(poles):
            gain = jnp.sum(into[r] * xk, axis=0, keepdims=True)
            if k > 0:
                yk = yk + outof[r] * state[r]
                gain = gain + fade[r] * state[r]
            state[r] = gain
        y_ref[k * STEP : (k + 1) * STEP, :] = yk
    half = jnp.concatenate(state, axis=0)
    half_ref[...] = half
    total = half + jnp.exp(-float(rows) * rates) * swap(half)
    h = poles // 2
    packed = jnp.where(right, total[h:], swap(total[:h]))
    for i in range(send_ref.shape[0]):
        send_ref[i, 0:8, :] = packed
        send_ref[i, 8:16, :] = own


def local(parts, short_weight, residue, rates):
    _, _, rows, width = parts.shape
    tile = jax.ShapeDtypeStruct((rows, width), F32)
    return pl.pallas_call(
        local_kernel,
        out_shape=(
            jax.ShapeDtypeStruct((NEAR, 16, width), F32),
            tile,
            tile,
            tile,
            jax.ShapeDtypeStruct((rates.shape[0], width), F32),
            jax.ShapeDtypeStruct((8, width), F32),
        ),
        compiler_params=pltpu.CompilerParams(vmem_limit_bytes=32 * 2**20),
        name="local",
    )(parts, short_weight, residue, rates)


def gate_of(tile, before):
    a = tile[0:2]
    if before is not None:
        a = a + before[2:4]
    return a * swap(a)


def near_kernel(shard_rows, place_ref, got_ref, rates_ref, send_ref, prefix_ref, before_ref):
    near = place_ref[0]
    rates = folded(rates_ref[...])
    fade = jnp.exp(-float(shard_rows) * rates)
    first = jnp.exp(-(shard_rows - 1.0) * rates)
    second = jnp.exp(-(shard_rows - 2.0) * rates)
    total = got_ref[0, 0:8, :]
    prefix = jnp.where(near > 0, total, 0.0)
    before = jnp.zeros_like(total)
    for i in range(1, NEAR):
        edge = got_ref[i - 1, 8:16, :]
        gate = gate_of(got_ref[i, 8:16, :], edge)
        grown = total * fade + (got_ref[i, 0:8, :] + first * gate[0:1] + second * gate[1:2])
        before = jnp.where(near == i, edge, before)
        total = grown
        prefix = jnp.where(near > i, grown, prefix)
    prefix_ref[...] = prefix
    before_ref[...] = before
    head = got_ref[0, 8:16, :]
    tail = got_ref[NEAR - 1, 8:16, :]
    ends = jnp.where(rows_of(head.shape) < 2, head, tail)
    for i in range(send_ref.shape[0]):
        send_ref[i, 0:8, :] = total
        send_ref[i, 8:16, :] = ends


def near_sums(place, got, rates, shard_rows, far_count):
    width = got.shape[2]
    tile = jax.ShapeDtypeStruct((8, width), F32)
    vmem = pl.BlockSpec(memory_space=pltpu.VMEM)
    return pl.pallas_call(
        functools.partial(near_kernel, shard_rows),
        in_specs=[pl.BlockSpec(memory_space=pltpu.SMEM), vmem, vmem],
        out_shape=(jax.ShapeDtypeStruct((far_count, 16, width), F32), tile, tile),
        name="near_sums",
    )(place, got, rates)


def finish_kernel(
    shard_rows, place_ref, got_ref, prefix_ref, before_ref, own_ref, half_ref, q_ref, x_ref, y_ref,
    residue_ref, rates_ref, skip_ref, out_ref,
):
    near, far = place_ref[0], place_ref[1]
    rows, width = q_ref.shape
    rates = folded(rates_ref[...])
    first = jnp.exp(-(shard_rows - 1.0) * rates)
    second = jnp.exp(-(shard_rows - 2.0) * rates)
    last = jnp.exp(-float((NEAR - 1) * shard_rows) * rates)
    row_fade = jnp.exp(-float(NEAR * shard_rows) * rates)
    before = before_ref[...]
    carry = jnp.zeros_like(rates)
    opening = jnp.zeros_like(rates)
    edge = None
    for z in range(got_ref.shape[0]):
        gate = gate_of(got_ref[z, 8:16, :], edge)
        start = first * gate[0:1] + second * gate[1:2]
        opening = jnp.where(far == z, start, opening)
        if edge is not None:
            before = jnp.where(jnp.logical_and(near == 0, far == z), edge, before)
        grown = carry * row_fade + (got_ref[z, 0:8, :] + last * start)
        carry = jnp.where(far > z, grown, carry)
        edge = got_ref[z, 8:16, :]
    place = near.astype(F32) * float(shard_rows)
    state = prefix_ref[...] + jnp.exp(-place * rates) * carry
    beyond = jnp.exp(-jnp.maximum(place - shard_rows, 0.0) * rates) * opening
    state = state + jnp.where(near > 0, beyond, 0.0)
    gate = gate_of(own_ref[...], before)
    state = state + jnp.exp(rates) * gate[0:1] + jnp.exp(2.0 * rates) * gate[1:2]

    rates = twice(rates_ref[...])
    weight = twice(residue_ref[...]) * jnp.sqrt(2.0 * rates)
    poles = rates.shape[0]
    left = lanes_of((1, width)) < width // 2
    other = swap(state)
    whole = jnp.concatenate([jnp.where(left, state, other), jnp.where(left, other, state)], axis=0)
    whole = jnp.where(left, whole, swap(half_ref[...]) + jnp.exp(-float(rows) * rates) * whole)
    skip = twice(skip_ref[...])
    step_pos = rows_of((STEP, width)).astype(F32)
    decay = jnp.exp(-float(STEP) * rates)
    states, outof, fade = [], [], []
    for r in range(poles):
        states.append(jnp.broadcast_to(whole[r : r + 1], (STEP, width)))
        outof.append(weight[r : r + 1] * jnp.exp(-rates[r : r + 1] * (step_pos + 1.0)))
        fade.append(jnp.broadcast_to(decay[r : r + 1], (STEP, width)))
    states = [s * o for s, o in zip(states, outof)]
    for k in range(rows // STEP):
        at = slice(k * STEP, (k + 1) * STEP)
        xk, qk, yk = x_ref[at, :], q_ref[at, :], y_ref[at, :]
        if k == 0:
            inner = rows_of((STEP, width))
            ahead = jnp.sum(weight * jnp.exp(rates), axis=0, keepdims=True)
            top = jnp.logical_and(left, inner == 0)
            next_ = jnp.logical_and(left, inner == 1)
            xk = jnp.where(top, gate[0:1], jnp.where(next_, gate[1:2], xk))
            yk = yk - jnp.where(top, ahead * gate[1:2], 0.0)
            q_edge = before[4:5]
            qk = qk + jnp.where(top, q_edge, jnp.where(next_, swap(q_edge), 0.0))
        for r in range(poles):
            yk = yk + states[r]
            states[r] = states[r] * fade[r]
        mixed = qk * (yk + skip * xk)
        out_ref[at, :] = mixed[:, : width // 2].astype(out_ref.dtype)
        out_ref[rows + k * STEP : rows + (k + 1) * STEP, :] = mixed[:, width // 2 :].astype(out_ref.dtype)


def finish(shard_rows, place, got, prefix, before, own, half, q, x, y, residue, rates, skip):
    rows, width = q.shape
    vmem = pl.BlockSpec(memory_space=pltpu.VMEM)
    return pl.pallas_call(
        functools.partial(finish_kernel, shard_rows),
        in_specs=[pl.BlockSpec(memory_space=pltpu.SMEM)] + [vmem] * 11,
        out_shape=jax.ShapeDtypeStruct((2 * rows, width // 2), jnp.bfloat16),
        name="finish",
    )(place, got, prefix, before, own, half, q, x, y, residue, rates, skip)


def per_device(tokens, in_weight, short_weight, residue, rates, skip):
    shard_rows = tokens.shape[0]
    place = jnp.stack([lax.axis_index("near"), lax.axis_index("far")]).astype(jnp.int32)
    residue, rates = residue.T, rates.T
    partials = project(tokens, in_weight.transpose(1, 0, 2))
    parts = lax.all_to_all(partials, "chan", 0, 0, tiled=True)
    send, q, x, y, half, own = local(parts, short_weight, residue, rates)
    got = lax.all_to_all(send, "near", 0, 0, tiled=True)
    send, prefix, before = near_sums(place, got, rates, shard_rows, lax.axis_size("far"))
    got = lax.all_to_all(send, "far", 0, 0, tiled=True)
    return finish(shard_rows, place, got, prefix, before, own, half, q, x, y, residue, rates, skip[None, :])


def solution(mesh):
    seq, chan = mesh.devices.shape
    mesh = Mesh(mesh.devices.reshape(seq // NEAR, NEAR, chan), ("far", "near", "chan"))
    whole = ("far", "near")
    in_specs = (
        P(whole, "chan"),
        P("chan", None, None),
        P(None, None, "chan"),
        P("chan", None),
        P("chan", None),
        P("chan"),
    )
    return jax.shard_map(
        per_device, mesh=mesh, in_specs=in_specs, out_specs=P(whole, "chan"), check_vma=False
    )
```

time: 196 us -> 67.1 us (0.34)
  waiting for transfers between devices: 65.8 us -> 8.56 us
  matrix products: 18.9 us -> 0 us
  starting transfers between devices: 27.7 us -> 12 us
  between operations: 13.7 us -> 0.03 us
  local copies, waits for them, and re-layouts: 21.2 us -> 8.37 us
  other arithmetic: 10 us -> 0.61 us
  blocking collectives: 37.5 us -> 30.6 us
  Pallas kernels: 0 us -> 6.53 us
    reduce_scatter x1 -> x0, waiting for transfers between devices: 32.1 us -> none  [per_device(): lax.psum_scatter(partials, 'chan', scatter_dimension=2, tiled=True)]
    all_to_all x2 -> x1, waiting for transfers between devices: 32.6 us -> 8.56 us  [per_device(): got = lax.all_to_all(send, 'near', 0, 0, tiled=True)]
    dot_general x11 -> x0, matrix products: 16.7 us -> none  [the longest x1 3.45 us: per_device(): jnp.einsum('td,djc->tjc', tokens, in_weight, preferred_element_type=jnp.f...]
    all_to_all x2 -> x1, starting transfers between devices: 22.9 us -> 12 us  [per_device(): got = lax.all_to_all(send, 'near', 0, 0, tiled=True)]
    all_to_all x2, blocking collectives: 37.5 us -> 30.6 us  [the longest x1 17.6 us: per_device(): got = lax.all_to_all(send, 'far', 0, 0, tiled=True)]
    pallas_call x0 -> x4, Pallas kernels: none -> 6.53 us  [the longest x1 1.96 us: finish(): pl.pallas_call(functools.partial(finish_kernel, shard_rows), in_specs=[pl...]
    ppermute x1 -> x0, starting transfers between devices: 4.74 us -> none  [from_behind(): return lax.ppermute(block, axis, route)]
    slice x5 -> x0, local copies, waits for them, and re-layouts: 4.5 us -> none  [the longest x2 2.59 us: inverse(): received[1]]
  transfers between devices with their start and end apart: 4 -> 1, of which waited for: 4 -> 1; matrix products, arithmetic and copies ran while one was open for 0% -> 1% of each run, Pallas kernels for 0% -> 0%
where the time goes in v1:
time: 67.1 us; the launch traced here: 66.7 us
  blocking collectives  30.6 us (46%)
  starting transfers between devices  12 us (18%)
  waiting for transfers between devices  8.56 us (13%)
  local copies, waits for them, and re-layouts  8.37 us (12%)
  Pallas kernels  6.53 us (10%)
    all_to_all x1, blocking collectives, per_device(): got = lax.all_to_all(send, 'far', 0, 0, tiled=True)  17.6 us
    all_to_all x1, blocking collectives, per_device(): parts = lax.all_to_all(partials, 'chan', 0, 0, tiled=True)  13 us
    all_to_all x1, starting transfers between devices, per_device(): got = lax.all_to_all(send, 'near', 0, 0, tiled=True)  12 us
    all_to_all x1, waiting for transfers between devices, per_device(): got = lax.all_to_all(send, 'near', 0, 0, tiled=True)  8.56 us
    unnamed x22, local copies, waits for them, and re-layouts  6.83 us
    pallas_call x1, Pallas kernels, finish(): pl.pallas_call(functools.partial(finish_kernel, shard_rows), in_specs=[pl...  1.96 us
    pallas_call x1, Pallas kernels, near_sums(): pl.pallas_call(functools.partial(near_kernel, shard_rows), in_specs=[pl.B...  1.67 us
    pallas_call x1, Pallas kernels, project(): pl.pallas_call(project_kernel, grid=(streams,), in_specs=[pl.BlockSpec((r...  1.61 us
  transfers between devices with their start and end apart: 1, of which 1 were waited for; matrix products, arithmetic and copies ran while one was open for 1% of the time, Pallas kernels for 0%

profile of v1, /device:TPU:1, one launch (start us, length us, event | category | flops | bytes accessed | tf_op | source)
XLA Modules:
  0.0 66.7 jit_solution(20229613681654124)
XLA Ops:
  0.0 0.0 copy-start
  0.0 1.9 %copy-done = bf16[2048,3,256]{2,0,1:T(8,128)(2,1)S(1)} copy-done((bf16[2048,3,256]{2,0,1:T(8,128)(2,1)S(1)}, bf16[2048,3,256]{2,0,1:T(8,128)(2,1)}, u32[]{:S(2)}) %copy-start) | copy-done | bytes 3145752
  1.9 0.0 copy-start.1
  1.9 1.2 %copy-done.1 = bf16[256,2048]{1,0:T(8,128)(2,1)S(1)} copy-done((bf16[256,2048]{1,0:T(8,128)(2,1)S(1)}, bf16[256,2048]{1,0:T(8,128)(2,1)}, u32[]{:S(2)}) %copy-start.1) | copy-done | bytes 1048600
  3.1 0.0 copy-start.2
  3.1 1.6 %project.1 = f32[4,3,128,128]{3,2,1,0:T(8,128)S(1)} custom-call(bf16[256,2048]{1,0:T(8,128)(2,1)S(1)} %copy-done.1, bf16[3,2048,256]{2,1,0:T(8,128)(2,1)S(1)} %bitcast.6), custom_call_target="tpu_custom_call" | custom-call | tf_op jit(solution)/shard_map/project/pallas_call | solution.py:51
  4.7 13.0 %all_to_all.15.part_ref = f32[4,3,128,128]{3,2,1,0:T(8,128)S(1)} all-to-all(f32[4,3,128,128]{3,2,1,0:T(8,128)S(1)} %project.1), channel_id=1, replica_groups=mesh['far'=8,'near'=16,'chan'=4] {'chan'}, dimensions={0} | all-to-all | bytes 1572864 | tf_op jit(solution)/shard_map/all_to_all | solution.py:280
  17.7 0.0 copy-done.2
  17.7 0.0 copy-done.6
  17.7 0.0 copy-done.8
  17.7 1.3 %local.1 = (f32[16,16,128]{2,1,0:T(8,128)}, f32[128,128]{1,0:T(8,128)S(1)}, f32[128,128]{1,0:T(8,128)S(1)}, f32[128,128]{1,0:T(8,128)S(1)}, f32[16,128]{1,0:T(8,128)S(1)}, /*index=5*/f32[8,128]{1,0:T(8,128)S(1)}) custom-call(f32[4,3,128,128]{3,2,1,0:T(8,128)S(1)} %all_to_all.15.part_ref, f32[3,3,64]{2,1,0:T(4,128)S(1)} %copy-done.8, f32[16,64]{1,0:T(8,128)S(1)} %bitcast.11, ...), custom_call_target="tpu_custom_call" | custom-call | tf_op jit(solution)/shard_map/local/pallas_call | solution.py:137
  19.0 0.6 copy-done.3
  19.6 0.6 copy-done.4
  20.3 0.6 copy-done.5
  20.9 0.6 copy-done.7
  21.5 0.6 copy-done.9
  22.1 12.0 %all-to-all-start.1 = ((f32[16,16,128]{2,1,0:T(8,128)}), f32[16,16,128]{2,1,0:T(8,128)S(1)}, u32[]{:S(2)}, u32[]{:S(2)}) async-start(f32[16,16,128]{2,1,0:T(8,128)} %get-tuple-element.14), calls=%async_computation.1 | async-start | bytes 262144 | tf_op jit(solution)/shard_map/all_to_all | solution.py:282
  34.1 0.6 pad_add_fusion.place_ref
  34.7 8.6 %all-to-all-done.1.got_ref = f32[16,16,128]{2,1,0:T(8,128)S(1)} async-done(((f32[16,16,128]{2,1,0:T(8,128)}), f32[16,16,128]{2,1,0:T(8,128)S(1)}, u32[]{:S(2)}, u32[]{:S(2)}) %all-to-all-start.1) | async-done | bytes 131104 | tf_op jit(solution)/shard_map/all_to_all | solution.py:282
  43.3 0.6 copy-done.10
  43.9 1.7 %near_sums.1 = (f32[8,16,128]{2,1,0:T(8,128)}, f32[8,128]{1,0:T(8,128)}, f32[8,128]{1,0:T(8,128)}) custom-call(s32[2]{0:T(128)} %pad_add_fusion.place_ref, f32[16,16,128]{2,1,0:T(8,128)} %copy-done.10, f32[16,64]{1,0:T(8,128)} %bitcast.7), custom_call_target="tpu_custom_call" | custom-call | tf_op jit(solution)/shard_map/near_sums/pallas_call | solution.py:189
  45.6 17.6 %all_to_all.16.got_ref = f32[8,16,128]{2,1,0:T(8,128)} all-to-all(f32[8,16,128]{2,1,0:T(8,128)} %get-tuple-element.15), channel_id=1, replica_groups=mesh['far'=8,'near'=16,'chan'=4] {'far'}, dimensions={0} | all-to-all | bytes 131072 | tf_op jit(solution)/shard_map/all_to_all | solution.py:284
  63.2 2.0 %finish.1 = bf16[256,64]{1,0:T(8,128)(2,1)} custom-call(s32[2]{0:T(128)} %pad_add_fusion.place_ref, f32[8,16,128]{2,1,0:T(8,128)} %all_to_all.16.got_ref, f32[8,128]{1,0:T(8,128)} %get-tuple-element.16.prefix_ref, f32[8,128]{1,0:T(8,128)} %get-tuple-element.17.before_ref, f32[8,128]{1,0:T(8,128)} %copy-done.9, f32[16,128]{1,0:T(8,128)} %copy-done.7, ...), custom_call_target="tpu_custom_call" | custom-call | tf_op jit(solution)/shard_map/finish/pallas_call | solution.py:267
  65.1 1.5 %copy.7 = bf16[256,64]{0,1:T(8,128)(2,1)} copy(bf16[256,64]{1,0:T(8,128)(2,1)} %finish.1) | data formatting | bytes 65536 | tf_op jit(solution)/shard_map/finish/pallas_call | solution.py:267
  (8 shorter events, 0.0 us)
Async XLA Ops:
  0.0 1.9 %copy-start = (bf16[2048,3,256]{2,0,1:T(8,128)(2,1)S(1)}, bf16[2048,3,256]{2,0,1:T(8,128)(2,1)}, u32[]{:S(2)}) copy-start(bf16[2048,3,256]{2,0,1:T(8,128)(2,1)} %param.7) | copy-start | bytes 9437188
  1.9 1.2 %copy-start.1 = (bf16[256,2048]{1,0:T(8,128)(2,1)S(1)}, bf16[256,2048]{1,0:T(8,128)(2,1)}, u32[]{:S(2)}) copy-start(bf16[256,2048]{1,0:T(8,128)(2,1)} %tok_ref.1) | copy-start | bytes 3145732
  3.1 14.6 %copy-start.2 = (f32[64,16]{0,1:T(8,128)S(1)}, f32[64,16]{0,1:T(8,128)}, u32[]{:S(2)}) copy-start(f32[64,16]{0,1:T(8,128)} %param.10) | copy-start | bytes 12292
  3.1 14.6 %copy-start.6 = (f32[64,16]{0,1:T(8,128)S(1)}, f32[64,16]{0,1:T(8,128)}, u32[]{:S(2)}) copy-start(f32[64,16]{0,1:T(8,128)} %param.9) | copy-start | bytes 12292
  3.1 14.6 %copy-start.8 = (f32[3,3,64]{2,1,0:T(4,128)S(1)}, f32[3,3,64]{2,1,0:T(4,128)}, u32[]{:S(2)}) copy-start(f32[3,3,64]{2,1,0:T(4,128)} %short_ref.1) | copy-start | bytes 6916
  19.0 0.6 copy-start.3
  19.6 0.6 copy-start.4
  20.3 0.6 copy-start.5
  20.9 0.6 copy-start.7
  21.5 0.6 copy-start.9
  22.1 21.2 %all-to-all-start.1 = ((f32[16,16,128]{2,1,0:T(8,128)}), f32[16,16,128]{2,1,0:T(8,128)S(1)}, u32[]{:S(2)}, u32[]{:S(2)}) async-start(f32[16,16,128]{2,1,0:T(8,128)} %get-tuple-element.14), calls=%async_computation.1 | async-start | bytes 262144 | tf_op jit(solution)/shard_map/all_to_all | solution.py:282
  43.3 0.7 copy-start.10

commit v2 on v1

v2 whole, which is shorter than its diff:
```python
import functools

import jax
import jax.numpy as jnp
from jax import lax
from jax.experimental import pallas as pl
from jax.experimental.pallas import tpu as pltpu
from jax.sharding import Mesh, PartitionSpec as P

NEAR = 16
STEP = 8
F32 = jnp.float32
HBM = pl.BlockSpec(memory_space=pl.ANY)
VMEM = pl.BlockSpec(memory_space=pltpu.VMEM)
ROOMY = pltpu.CompilerParams(vmem_limit_bytes=56 * 2**20)


def lanes_of(shape):
    return lax.broadcasted_iota(jnp.int32, shape, 1)


def rows_of(shape):
    return lax.broadcasted_iota(jnp.int32, shape, 0)


def swap(tile):
    return pltpu.roll(tile, tile.shape[1] // 2, 1)


def twice(row):
    return jnp.concatenate([row, row], axis=1)


def folded(poles):
    half = poles.shape[0] // 2
    return jnp.concatenate([poles[:half], poles[half:]], axis=1)


def project_kernel(tok_hbm, w_hbm, out_ref, tok_ref, w_ref, tok_sem, w_sem):
    streams = w_ref.shape[0]
    tok_copy = pltpu.make_async_copy(tok_hbm, tok_ref, tok_sem)
    tok_copy.start()
    w_copies = [pltpu.make_async_copy(w_hbm.at[s], w_ref.at[s], w_sem.at[s]) for s in range(streams)]
    for copy in w_copies:
        copy.start()
    tok_copy.wait()
    for s in range(streams):
        w_copies[s].wait()
        acc = jnp.dot(tok_ref[...], w_ref[s], preferred_element_type=F32)
        rows = acc.shape[0] // 2
        for pair in range(acc.shape[1] // 128):
            early = acc[:rows, 128 * pair : 128 * (pair + 1)]
            late = acc[rows:, 128 * pair : 128 * (pair + 1)]
            left = lanes_of(early.shape) < 64
            out_ref[2 * pair, s] = jnp.where(left, early, swap(late))
            out_ref[2 * pair + 1, s] = jnp.where(left, swap(early), late)


def project(tokens, weight):
    rows, depth = tokens.shape
    streams, _, width = weight.shape
    chan = width // 64
    return pl.pallas_call(
        project_kernel,
        in_specs=[HBM, HBM],
        out_shape=jax.ShapeDtypeStruct((chan, streams, rows // 2, 128), F32),
        scratch_shapes=[
            pltpu.VMEM(tokens.shape, tokens.dtype),
            pltpu.VMEM(weight.shape, weight.dtype),
            pltpu.SemaphoreType.DMA(()),
            pltpu.SemaphoreType.DMA((streams,)),
        ],
        compiler_params=ROOMY,
        name="project",
    )(tokens, weight)


def local_kernel(part_ref, short_ref, residue_ref, rates_ref, send_ref, keep_ref):
    count = part_ref.shape[0]
    rows, width = part_ref.shape[2:]
    right = lanes_of((1, width)) >= width // 2
    row = rows_of((rows, width))
    feats, edges = [], []
    for s in range(3):
        p = part_ref[0, s]
        for i in range(1, count):
            p = p + part_ref[i, s]
        tap = [twice(short_ref[k, s : s + 1, :]) for k in range(3)]
        before = jnp.where(right, swap(p[rows - 8 :]), 0.0)
        one = jnp.where(row < 1, before[7:8], pltpu.roll(p, 1, 0))
        two = pltpu.roll(p, 2, 0)
        two = jnp.where(row == 0, before[6:7], jnp.where(row == 1, before[7:8], two))
        feats.append(tap[0] * p + tap[1] * one + tap[2] * two)
        edges.append((tap[1] * p[rows - 1 :] + tap[2] * p[rows - 2 : rows - 1], tap[2] * p[rows - 1 :]))
    q, a, b = feats
    keep_ref[0:rows, :] = q
    x = jnp.where(jnp.logical_and(row < 2, jnp.logical_not(right)), 0.0, a * b)
    keep_ref[rows : 2 * rows, :] = x
    tile = [
        jnp.where(right, swap(b[0:1]), a[0:1]),
        jnp.where(right, swap(b[1:2]), a[1:2]),
        jnp.where(right, edges[2][0], swap(edges[1][0])),
        jnp.where(right, edges[2][1], swap(edges[1][1])),
        jnp.where(right, edges[0][1], swap(edges[0][0])),
    ]
    own = jnp.concatenate(tile + [jnp.zeros((3, width), F32)], axis=0)
    keep_ref[3 * rows : 3 * rows + 8, :] = own

    rates = twice(rates_ref[...])
    weight = twice(residue_ref[...]) * jnp.sqrt(2.0 * rates)
    poles = rates.shape[0]
    inner = rows_of((STEP, width))
    step_pos = inner.astype(F32)
    impulse = [jnp.sum(weight * jnp.exp(-rates * float(u)), axis=0, keepdims=True) for u in range(STEP)]
    near = [jnp.where(inner >= u, impulse[u], 0.0) for u in range(STEP)]
    decay = jnp.exp(-float(STEP) * rates)
    into, outof, fade = [], [], []
    for r in range(poles):
        rate = rates[r : r + 1]
        into.append(jnp.exp(-rate * (STEP - 1.0 - step_pos)))
        outof.append(weight[r : r + 1] * jnp.exp(-rate * (step_pos + 1.0)))
        fade.append(decay[r : r + 1])
    state = [None] * poles
    for k in range(rows // STEP):
        xk = x[k * STEP : (k + 1) * STEP]
        yk = near[0] * xk
        for u in range(1, STEP):
            yk = yk + near[u] * pltpu.roll(xk, u, 0)
        for r in range(poles):
            gain = jnp.sum(into[r] * xk, axis=0, keepdims=True)
            if k > 0:
                yk = yk + outof[r] * state[r]
                gain = gain + fade[r] * state[r]
            state[r] = gain
        keep_ref[2 * rows + k * STEP : 2 * rows + (k + 1) * STEP, :] = yk
    half = jnp.concatenate(state, axis=0)
    keep_ref[3 * rows + 8 :, :] = half
    total = half + jnp.exp(-float(rows) * rates) * swap(half)
    h = poles // 2
    packed = jnp.where(right, total[h:], swap(total[:h]))
    for i in range(send_ref.shape[0]):
        send_ref[i, 0:8, :] = packed
        send_ref[i, 8:16, :] = own


def local(parts, short_weight, residue, rates):
    _, _, rows, width = parts.shape
    return pl.pallas_call(
        local_kernel,
        out_shape=(
            jax.ShapeDtypeStruct((NEAR, 16, width), F32),
            jax.ShapeDtypeStruct((3 * rows + 8 + rates.shape[0], width), F32),
        ),
        compiler_params=ROOMY,
        name="local",
    )(parts, short_weight, residue, rates)


def gate_of(tile, before):
    a = tile[0:2]
    if before is not None:
        a = a + before[2:4]
    return a * swap(a)


def near_kernel(shard_rows, got_hbm, rates_ref, send_ref, keep_ref, got_ref, sem):
    copy = pltpu.make_async_copy(got_hbm, got_ref, sem)
    copy.start()
    near = lax.axis_index("near")
    rates = folded(rates_ref[...])
    fade = jnp.exp(-float(shard_rows) * rates)
    first = jnp.exp(-(shard_rows - 1.0) * rates)
    second = jnp.exp(-(shard_rows - 2.0) * rates)
    copy.wait()
    total = got_ref[0, 0:8, :]
    prefix = jnp.where(near > 0, total, 0.0)
    before = jnp.zeros_like(total)
    for i in range(1, NEAR):
        edge = got_ref[i - 1, 8:16, :]
        gate = gate_of(got_ref[i, 8:16, :], edge)
        grown = total * fade + (got_ref[i, 0:8, :] + first * gate[0:1] + second * gate[1:2])
        before = jnp.where(near == i, edge, before)
        total = grown
        prefix = jnp.where(near > i, grown, prefix)
    keep_ref[0:8, :] = prefix
    keep_ref[8:16, :] = before
    head = got_ref[0, 8:16, :]
    tail = got_ref[NEAR - 1, 8:16, :]
    ends = jnp.where(rows_of(head.shape) < 2, head, tail)
    for i in range(send_ref.shape[0]):
        send_ref[i, 0:8, :] = total
        send_ref[i, 8:16, :] = ends


def near_sums(got, rates, shard_rows, far_count):
    width = got.shape[2]
    return pl.pallas_call(
        functools.partial(near_kernel, shard_rows),
        in_specs=[HBM, VMEM],
        out_shape=(jax.ShapeDtypeStruct((far_count, 16, width), F32), jax.ShapeDtypeStruct((16, width), F32)),
        scratch_shapes=[pltpu.VMEM(got.shape, F32), pltpu.SemaphoreType.DMA(())],
        compiler_params=ROOMY,
        name="near_sums",
    )(got, rates)


def finish_kernel(
    shard_rows, got_hbm, near_hbm, keep_hbm, residue_ref, rates_ref, skip_ref, out_ref, got_ref, near_ref, keep_ref, sems
):
    copies = [
        pltpu.make_async_copy(source, target, sems.at[i])
        for i, (source, target) in enumerate([(got_hbm, got_ref), (near_hbm, near_ref), (keep_hbm, keep_ref)])
    ]
    for copy in copies:
        copy.start()
    near, far = lax.axis_index("near"), lax.axis_index("far")
    rows, width = out_ref.shape[1] // 2, keep_ref.shape[1]
    rates = twice(rates_ref[...])
    weight = twice(residue_ref[...]) * jnp.sqrt(2.0 * rates)
    poles = rates.shape[0]
    skip = twice(skip_ref[...])
    step_pos = rows_of((STEP, width)).astype(F32)
    decay = jnp.exp(-float(STEP) * rates)
    half_decay = jnp.exp(-float(rows) * rates)
    ahead = jnp.sum(weight * jnp.exp(rates), axis=0, keepdims=True)
    outof, fade = [], []
    for r in range(poles):
        outof.append(weight[r : r + 1] * jnp.exp(-rates[r : r + 1] * (step_pos + 1.0)))
        fade.append(jnp.broadcast_to(decay[r : r + 1], (STEP, width)))

    rates = folded(rates_ref[...])
    first = jnp.exp(-(shard_rows - 1.0) * rates)
    second = jnp.exp(-(shard_rows - 2.0) * rates)
    last = jnp.exp(-float((NEAR - 1) * shard_rows) * rates)
    row_fade = jnp.exp(-float(NEAR * shard_rows) * rates)
    place = near.astype(F32) * float(shard_rows)
    place_fade = jnp.exp(-place * rates)
    beyond_fade = jnp.where(near > 0, jnp.exp(-jnp.maximum(place - shard_rows, 0.0) * rates), 0.0)
    ahead_one, ahead_two = jnp.exp(rates), jnp.exp(2.0 * rates)
    for copy in copies:
        copy.wait()
    before = near_ref[8:16, :]
    carry = jnp.zeros_like(rates)
    opening = jnp.zeros_like(rates)
    edge = None
    for z in range(got_ref.shape[0]):
        gate = gate_of(got_ref[z, 8:16, :], edge)
        start = first * gate[0:1] + second * gate[1:2]
        opening = jnp.where(far == z, start, opening)
        if edge is not None:
            before = jnp.where(jnp.logical_and(near == 0, far == z), edge, before)
        grown = carry * row_fade + (got_ref[z, 0:8, :] + last * start)
        carry = jnp.where(far > z, grown, carry)
        edge = got_ref[z, 8:16, :]
    state = near_ref[0:8, :] + place_fade * carry + beyond_fade * opening
    gate = gate_of(keep_ref[3 * rows : 3 * rows + 8, :], before)
    state = state + ahead_one * gate[0:1] + ahead_two * gate[1:2]

    left = lanes_of((1, width)) < width // 2
    other = swap(state)
    whole = jnp.concatenate([jnp.where(left, state, other), jnp.where(left, other, state)], axis=0)
    whole = jnp.where(left, whole, swap(keep_ref[3 * rows + 8 :, :]) + half_decay * whole)
    states = [jnp.broadcast_to(whole[r : r + 1], (STEP, width)) * outof[r] for r in range(poles)]
    steps = []
    for k in range(rows // STEP):
        at = k * STEP
        qk = keep_ref[at : at + STEP, :]
        xk = keep_ref[rows + at : rows + at + STEP, :]
        yk = keep_ref[2 * rows + at : 2 * rows + at + STEP, :]
        if k == 0:
            inner = rows_of((STEP, width))
            top = jnp.logical_and(left, inner == 0)
            next_ = jnp.logical_and(left, inner == 1)
            xk = jnp.where(top, gate[0:1], jnp.where(next_, gate[1:2], xk))
            yk = yk - jnp.where(top, ahead * gate[1:2], 0.0)
            q_edge = before[4:5]
            qk = qk + jnp.where(top, q_edge, jnp.where(next_, swap(q_edge), 0.0))
        for r in range(poles):
            yk = yk + states[r]
            states[r] = states[r] * fade[r]
        steps.append(qk * (yk + skip * xk))
    mixed = jnp.concatenate(steps, axis=0).T
    out_ref[:, :rows] = mixed[: width // 2].astype(out_ref.dtype)
    out_ref[:, rows:] = mixed[width // 2 :].astype(out_ref.dtype)


def finish(shard_rows, got, near, keep, residue, rates, skip):
    width = keep.shape[1]
    return pl.pallas_call(
        functools.partial(finish_kernel, shard_rows),
        in_specs=[HBM] * 3 + [VMEM] * 3,
        out_shape=jax.ShapeDtypeStruct((width // 2, shard_rows), jnp.bfloat16),
        scratch_shapes=[pltpu.VMEM(a.shape, F32) for a in (got, near, keep)] + [pltpu.SemaphoreType.DMA((3,))],
        compiler_params=ROOMY,
        name="finish",
    )(got, near, keep, residue, rates, skip)


def per_device(tokens, in_weight, short_weight, residue, rates, skip):
    shard_rows = tokens.shape[0]
    residue, rates = residue.T, rates.T
    partials = project(tokens, in_weight.transpose(1, 0, 2))
    parts = lax.all_to_all(partials, "chan", 0, 0, tiled=True)
    send, keep = local(parts, short_weight, residue, rates)
    got = lax.all_to_all(send, "near", 0, 0, tiled=True)
    send, near = near_sums(got, rates, shard_rows, lax.axis_size("far"))
    got = lax.all_to_all(send, "far", 0, 0, tiled=True)
    return finish(shard_rows, got, near, keep, residue, rates, skip[None, :]).T


def solution(mesh):
    seq, chan = mesh.devices.shape
    mesh = Mesh(mesh.devices.reshape(seq // NEAR, NEAR, chan), ("far", "near", "chan"))
    whole = ("far", "near")
    in_specs = (
        P(whole, "chan"),
        P("chan", None, None),
        P(None, None, "chan"),
        P("chan", None),
        P("chan", None),
        P("chan"),
    )
    return jax.shard_map(
        per_device, mesh=mesh, in_specs=in_specs, out_specs=P(whole, "chan"), check_vma=False
    )
```

time: 67.1 us -> 65.1 us (0.970)
  blocking collectives: 30.6 us -> 52.3 us
  starting transfers between devices: 12 us -> 0 us
  waiting for transfers between devices: 8.56 us -> 0 us
  local copies, waits for them, and re-layouts: 8.37 us -> 0 us
  Pallas kernels: 6.53 us -> 12.3 us
    all_to_all x0 -> x1, blocking collectives: none -> 21.4 us  [per_device(): got = lax.all_to_all(send, 'near', 0, 0, tiled=True)]
    all_to_all x1 -> x0, starting transfers between devices: 12 us -> none  [per_device(): got = lax.all_to_all(send, 'near', 0, 0, tiled=True)]
    all_to_all x1 -> x0, waiting for transfers between devices: 8.56 us -> none  [per_device(): got = lax.all_to_all(send, 'near', 0, 0, tiled=True)]
    unnamed x22 -> x0, local copies, waits for them, and re-layouts: 6.83 us -> none
    pallas_call x3, Pallas kernels: 5.24 us -> 9.82 us  [the longest x1 4.82 us: project(): pl.pallas_call(project_kernel, in_specs=[HBM, HBM], out_shape=jax.ShapeDt...]
    pallas_call x1 -> x0, local copies, waits for them, and re-layouts: 1.54 us -> none  [finish(): pl.pallas_call(functools.partial(finish_kernel, shard_rows), in_specs=[pl...]
    pallas_call x1, Pallas kernels: 1.29 us -> 2.52 us  [local(): pl.pallas_call(local_kernel, out_shape=(jax.ShapeDtypeStruct((NEAR, 16, w...]
  transfers between devices with their start and end apart: 1 -> 0, of which waited for: 1 -> 0; matrix products, arithmetic and copies ran while one was open for 1% -> 0% of each run, Pallas kernels for 0% -> 0%
where the time goes in v2:
time: 65.1 us; the launch traced here: 64.6 us
  blocking collectives  52.3 us (80%)
  Pallas kernels  12.3 us (19%)
    all_to_all x1, blocking collectives, per_device(): got = lax.all_to_all(send, 'near', 0, 0, tiled=True)  21.4 us
    all_to_all x1, blocking collectives, per_device(): got = lax.all_to_all(send, 'far', 0, 0, tiled=True)  17.6 us
    all_to_all x1, blocking collectives, per_device(): parts = lax.all_to_all(partials, 'chan', 0, 0, tiled=True)  13.3 us
    pallas_call x1, Pallas kernels, project(): pl.pallas_call(project_kernel, in_specs=[HBM, HBM], out_shape=jax.ShapeDt...  4.82 us
    pallas_call x1, Pallas kernels, finish(): pl.pallas_call(functools.partial(finish_kernel, shard_rows), in_specs=[HB...  2.66 us
    pallas_call x1, Pallas kernels, local(): pl.pallas_call(local_kernel, out_shape=(jax.ShapeDtypeStruct((NEAR, 16, w...  2.52 us
    pallas_call x1, Pallas kernels, near_sums(): pl.pallas_call(functools.partial(near_kernel, shard_rows), in_specs=[HBM,...  2.34 us

profile of v2, /device:TPU:1, one launch (start us, length us, event | category | flops | bytes accessed | tf_op | source)
XLA Modules:
  0.0 64.6 jit_solution(1832279630078845399)
XLA Ops:
  0.0 4.8 %project.1 = f32[4,3,128,128]{3,2,1,0:T(8,128)} custom-call(bf16[256,2048]{1,0:T(8,128)(2,1)} %tok_hbm.1, bf16[3,2048,256]{2,1,0:T(8,128)(2,1)} %bitcast.5), custom_call_target="tpu_custom_call" | custom-call | tf_op jit(solution)/shard_map/project/pallas_call | solution.py:63
  4.8 13.3 %all_to_all.15.part_ref = f32[4,3,128,128]{3,2,1,0:T(8,128)} all-to-all(f32[4,3,128,128]{3,2,1,0:T(8,128)} %project.1), channel_id=1, replica_groups=mesh['far'=8,'near'=16,'chan'=4] {'chan'}, dimensions={0} | all-to-all | bytes 1572864 | tf_op jit(solution)/shard_map/all_to_all | solution.py:303
  18.1 2.5 %local.1 = (f32[16,16,128]{2,1,0:T(8,128)}, f32[408,128]{1,0:T(8,128)}) custom-call(f32[4,3,128,128]{3,2,1,0:T(8,128)} %all_to_all.15.part_ref, f32[3,3,64]{2,1,0:T(4,128)} %short_ref.1, f32[16,64]{1,0:T(8,128)} %bitcast.9, f32[16,64]{1,0:T(8,128)} %bitcast.6), custom_call_target="tpu_custom_call" | custom-call | tf_op jit(solution)/shard_map/local/pallas_call | solution.py:148
  20.6 21.4 %all_to_all.16.got_hbm = f32[16,16,128]{2,1,0:T(8,128)} all-to-all(f32[16,16,128]{2,1,0:T(8,128)} %get-tuple-element.9), channel_id=1, replica_groups=mesh['far'=8,'near'=16,'chan'=4] {'near'}, dimensions={0} | all-to-all | bytes 262144 | tf_op jit(solution)/shard_map/all_to_all | solution.py:305
  42.0 2.3 %near_sums.1 = (f32[8,16,128]{2,1,0:T(8,128)}, f32[16,128]{1,0:T(8,128)}) custom-call(f32[16,16,128]{2,1,0:T(8,128)} %all_to_all.16.got_hbm, f32[16,64]{1,0:T(8,128)} %bitcast.7), custom_call_target="tpu_custom_call" | custom-call | tf_op jit(solution)/shard_map/near_sums/pallas_call | solution.py:197
  44.4 17.6 %all_to_all.17.got_hbm = f32[8,16,128]{2,1,0:T(8,128)} all-to-all(f32[8,16,128]{2,1,0:T(8,128)} %get-tuple-element.10), channel_id=1, replica_groups=mesh['far'=8,'near'=16,'chan'=4] {'far'}, dimensions={0} | all-to-all | bytes 131072 | tf_op jit(solution)/shard_map/all_to_all | solution.py:307
  62.0 2.7 %finish.1 = bf16[64,256]{1,0:T(8,128)(2,1)} custom-call(f32[8,16,128]{2,1,0:T(8,128)} %all_to_all.17.got_hbm, f32[16,128]{1,0:T(8,128)} %get-tuple-element.11.near_hbm, f32[408,128]{1,0:T(8,128)} %get-tuple-element.12.keep_hbm, f32[16,64]{1,0:T(8,128)} %bitcast.10, f32[16,64]{1,0:T(8,128)} %bitcast.8, f32[1,64]{1,0:T(1,128)} %bitcast.11), custom_call_target="tpu_custom_call" | custom-call | tf_op jit(solution)/shard_map/finish/pallas_call | solution.py:289

commit v3 on v2

--- a/solution.py
+++ b/solution.py
@@ -11,8 +11,15 @@
 STEP = 8
 F32 = jnp.float32
 HBM = pl.BlockSpec(memory_space=pl.ANY)
-VMEM = pl.BlockSpec(memory_space=pltpu.VMEM)
-ROOMY = pltpu.CompilerParams(vmem_limit_bytes=56 * 2**20)
+ROOMY = pltpu.CompilerParams(vmem_limit_bytes=24 * 2**20)
+
+
+def in_vmem(array):
+    return pltpu.with_memory_space_constraint(array, pltpu.VMEM)
+
+
+def in_hbm(array):
+    return pltpu.with_memory_space_constraint(array, pltpu.HBM)
 
 
 def lanes_of(shape):
@@ -36,21 +43,35 @@
     return jnp.concatenate([poles[:half], poles[half:]], axis=1)
 
 
-def project_kernel(tok_hbm, w_hbm, out_ref, tok_ref, w_ref, tok_sem, w_sem):
-    streams = w_ref.shape[0]
-    tok_copy = pltpu.make_async_copy(tok_hbm, tok_ref, tok_sem)
-    tok_copy.start()
-    w_copies = [pltpu.make_async_copy(w_hbm.at[s], w_ref.at[s], w_sem.at[s]) for s in range(streams)]
-    for copy in w_copies:
-        copy.start()
-    tok_copy.wait()
+def project_kernel(tok_hbm, w_hbm, out_ref, tok_ref, w_ref, acc_ref, tok_sems, w_sems):
+    streams, depth, _ = w_ref.shape
+    pieces = tok_sems.shape[0]
+    deep = depth // pieces
+    parts = [pl.ds(i * deep, deep) for i in range(pieces)]
+    tok_copies = [
+        pltpu.make_async_copy(tok_hbm.at[:, part], tok_ref.at[:, part], tok_sems.at[i]) for i, part in enumerate(parts)
+    ]
+    w_copies = [
+        [pltpu.make_async_copy(w_hbm.at[s, part], w_ref.at[s, part], w_sems.at[s, i]) for i, part in enumerate(parts)]
+        for s in range(streams)
+    ]
+    for i in range(pieces):
+        tok_copies[i].start()
+        w_copies[0][i].start()
+    for s in range(1, streams):
+        for copy in w_copies[s]:
+            copy.start()
     for s in range(streams):
-        w_copies[s].wait()
-        acc = jnp.dot(tok_ref[...], w_ref[s], preferred_element_type=F32)
-        rows = acc.shape[0] // 2
-        for pair in range(acc.shape[1] // 128):
-            early = acc[:rows, 128 * pair : 128 * (pair + 1)]
-            late = acc[rows:, 128 * pair : 128 * (pair + 1)]
+        for i, part in enumerate(parts):
+            if s == 0:
+                tok_copies[i].wait()
+            w_copies[s][i].wait()
+            term = jnp.dot(tok_ref[:, part], w_ref[s, part, :], preferred_element_type=F32)
+            acc_ref[...] = term if i == 0 else acc_ref[...] + term
+        rows = acc_ref.shape[0] // 2
+        for pair in range(acc_ref.shape[1] // 128):
+            early = acc_ref[:rows, 128 * pair : 128 * (pair + 1)]
+            late = acc_ref[rows:, 128 * pair : 128 * (pair + 1)]
             left = lanes_of(early.shape) < 64
             out_ref[2 * pair, s] = jnp.where(left, early, swap(late))
             out_ref[2 * pair + 1, s] = jnp.where(left, swap(early), late)
@@ -60,19 +81,21 @@
     rows, depth = tokens.shape
     streams, _, width = weight.shape
     chan = width // 64
+    pieces = 4
     return pl.pallas_call(
         project_kernel,
         in_specs=[HBM, HBM],
-        out_shape=jax.ShapeDtypeStruct((chan, streams, rows // 2, 128), F32),
+        out_shape=pltpu.VMEM((chan, streams, rows // 2, 128), F32),
         scratch_shapes=[
             pltpu.VMEM(tokens.shape, tokens.dtype),
             pltpu.VMEM(weight.shape, weight.dtype),
-            pltpu.SemaphoreType.DMA(()),
-            pltpu.SemaphoreType.DMA((streams,)),
+            pltpu.VMEM((rows, width), F32),
+            pltpu.SemaphoreType.DMA((pieces,)),
+            pltpu.SemaphoreType.DMA((streams, pieces)),
         ],
         compiler_params=ROOMY,
         name="project",
-    )(tokens, weight)
+    )(in_hbm(tokens), in_hbm(weight))
 
 
 def local_kernel(part_ref, short_ref, residue_ref, rates_ref, send_ref, keep_ref):
@@ -148,12 +171,12 @@
     return pl.pallas_call(
         local_kernel,
         out_shape=(
-            jax.ShapeDtypeStruct((NEAR, 16, width), F32),
-            jax.ShapeDtypeStruct((3 * rows + 8 + rates.shape[0], width), F32),
+            pltpu.VMEM((NEAR, 16, width), F32),
+            pltpu.VMEM((3 * rows + 8 + rates.shape[0], width), F32),
         ),
         compiler_params=ROOMY,
         name="local",
-    )(parts, short_weight, residue, rates)
+    )(in_vmem(parts), short_weight, residue, rates)
 
 
 def gate_of(tile, before):
@@ -163,15 +186,12 @@
     return a * swap(a)
 
 
-def near_kernel(shard_rows, got_hbm, rates_ref, send_ref, keep_ref, got_ref, sem):
-    copy = pltpu.make_async_copy(got_hbm, got_ref, sem)
-    copy.start()
+def near_kernel(shard_rows, got_ref, rates_ref, send_ref, keep_ref):
     near = lax.axis_index("near")
     rates = folded(rates_ref[...])
     fade = jnp.exp(-float(shard_rows) * rates)
     first = jnp.exp(-(shard_rows - 1.0) * rates)
     second = jnp.exp(-(shard_rows - 2.0) * rates)
-    copy.wait()
     total = got_ref[0, 0:8, :]
     prefix = jnp.where(near > 0, total, 0.0)
     before = jnp.zeros_like(total)
@@ -196,23 +216,12 @@
     width = got.shape[2]
     return pl.pallas_call(
         functools.partial(near_kernel, shard_rows),
-        in_specs=[HBM, VMEM],
-        out_shape=(jax.ShapeDtypeStruct((far_count, 16, width), F32), jax.ShapeDtypeStruct((16, width), F32)),
-        scratch_shapes=[pltpu.VMEM(got.shape, F32), pltpu.SemaphoreType.DMA(())],
-        compiler_params=ROOMY,
+        out_shape=(pltpu.VMEM((far_count, 16, width), F32), pltpu.VMEM((16, width), F32)),
         name="near_sums",
-    )(got, rates)
-
-
-def finish_kernel(
-    shard_rows, got_hbm, near_hbm, keep_hbm, residue_ref, rates_ref, skip_ref, out_ref, got_ref, near_ref, keep_ref, sems
-):
-    copies = [
-        pltpu.make_async_copy(source, target, sems.at[i])
-        for i, (source, target) in enumerate([(got_hbm, got_ref), (near_hbm, near_ref), (keep_hbm, keep_ref)])
-    ]
-    for copy in copies:
-        copy.start()
+    )(in_vmem(got), rates)
+
+
+def finish_kernel(shard_rows, got_ref, near_ref, keep_ref, residue_ref, rates_ref, skip_ref, out_ref):
     near, far = lax.axis_index("near"), lax.axis_index("far")
     rows, width = out_ref.shape[1] // 2, keep_ref.shape[1]
     rates = twice(rates_ref[...])
@@ -237,8 +246,6 @@
     place_fade = jnp.exp(-place * rates)
     beyond_fade = jnp.where(near > 0, jnp.exp(-jnp.maximum(place - shard_rows, 0.0) * rates), 0.0)
     ahead_one, ahead_two = jnp.exp(rates), jnp.exp(2.0 * rates)
-    for copy in copies:
-        copy.wait()
     before = near_ref[8:16, :]
     carry = jnp.zeros_like(rates)
     opening = jnp.zeros_like(rates)
@@ -288,12 +295,9 @@
     width = keep.shape[1]
     return pl.pallas_call(
         functools.partial(finish_kernel, shard_rows),
-        in_specs=[HBM] * 3 + [VMEM] * 3,
         out_shape=jax.ShapeDtypeStruct((width // 2, shard_rows), jnp.bfloat16),
-        scratch_shapes=[pltpu.VMEM(a.shape, F32) for a in (got, near, keep)] + [pltpu.SemaphoreType.DMA((3,))],
-        compiler_params=ROOMY,
         name="finish",
-    )(got, near, keep, residue, rates, skip)
+    )(in_vmem(got), in_vmem(near), in_vmem(keep), residue, rates, skip)
 
 
 def per_device(tokens, in_weight, short_weight, residue, rates, skip):

time: 65.1 us -> 59.1 us (0.908)
  Pallas kernels: 12.3 us -> 7.58 us
  blocking collectives: 52.3 us -> 51.2 us
    pallas_call x4, Pallas kernels: 12.3 us -> 7.58 us  [the longest x1 4.48 us: project(): pl.pallas_call(project_kernel, in_specs=[HBM, HBM], out_shape=pltpu.VMEM(...]
where the time goes in v3:
time: 59.1 us; the launch traced here: 58.8 us
  blocking collectives  51.2 us (87%)
  Pallas kernels  7.58 us (13%)
    all_to_all x1, blocking collectives, per_device(): got = lax.all_to_all(send, 'near', 0, 0, tiled=True)  21 us
    all_to_all x1, blocking collectives, per_device(): got = lax.all_to_all(send, 'far', 0, 0, tiled=True)  17.3 us
    all_to_all x1, blocking collectives, per_device(): parts = lax.all_to_all(partials, 'chan', 0, 0, tiled=True)  13 us
    pallas_call x1, Pallas kernels, project(): pl.pallas_call(project_kernel, in_specs=[HBM, HBM], out_shape=pltpu.VMEM(...  4.48 us
    pallas_call x1, Pallas kernels, finish(): pl.pallas_call(functools.partial(finish_kernel, shard_rows), out_shape=ja...  1.66 us

profile of v3, /device:TPU:1, one launch (start us, length us, event | category | flops | bytes accessed | tf_op | source)
XLA Modules:
  0.0 58.8 jit_solution(16204139798819778451)
XLA Ops:
  0.0 0.0 copy-start
  0.0 0.0 copy-start.1
  0.0 0.0 copy-start.2
  0.0 4.5 %project.1 = f32[4,3,128,128]{3,2,1,0:T(8,128)S(1)} custom-call(bf16[256,2048]{1,0:T(8,128)(2,1)} %tok_hbm.1, bf16[3,2048,256]{2,1,0:T(8,128)(2,1)} %bitcast.10), custom_call_target="tpu_custom_call" | custom-call | tf_op jit(solution)/shard_map/project/pallas_call | solution.py:85
  4.5 13.0 %all_to_all.15.part_ref = f32[4,3,128,128]{3,2,1,0:T(8,128)S(1)} all-to-all(f32[4,3,128,128]{3,2,1,0:T(8,128)S(1)} %project.1), channel_id=1, replica_groups=mesh['far'=8,'near'=16,'chan'=4] {'chan'}, dimensions={0} | all-to-all | bytes 1572864 | tf_op jit(solution)/shard_map/all_to_all | solution.py:307
  17.5 0.0 copy-done
  17.5 0.0 copy-done.1
  17.5 0.0 copy-done.2
  17.5 0.6 %local.1 = (f32[16,16,128]{2,1,0:T(8,128)S(1)}, f32[408,128]{1,0:T(8,128)S(1)}) custom-call(f32[4,3,128,128]{3,2,1,0:T(8,128)S(1)} %all_to_all.15.part_ref, f32[3,3,64]{2,1,0:T(4,128)S(1)} %copy-done.2, f32[16,64]{1,0:T(8,128)S(1)} %bitcast.9, f32[16,64]{1,0:T(8,128)S(1)} %bitcast.7), custom_call_target="tpu_custom_call" | custom-call | tf_op jit(solution)/shard_map/local/pallas_call | solution.py:171
  18.1 21.0 %all_to_all.16.got_ref = f32[16,16,128]{2,1,0:T(8,128)S(1)} all-to-all(f32[16,16,128]{2,1,0:T(8,128)S(1)} %get-tuple-element.9), channel_id=1, replica_groups=mesh['far'=8,'near'=16,'chan'=4] {'near'}, dimensions={0} | all-to-all | bytes 262144 | tf_op jit(solution)/shard_map/all_to_all | solution.py:309
  39.1 0.8 %near_sums.1 = (f32[8,16,128]{2,1,0:T(8,128)S(1)}, f32[16,128]{1,0:T(8,128)S(1)}) custom-call(f32[16,16,128]{2,1,0:T(8,128)S(1)} %all_to_all.16.got_ref, f32[16,64]{1,0:T(8,128)} %bitcast.5), custom_call_target="tpu_custom_call" | custom-call | tf_op jit(solution)/shard_map/near_sums/pallas_call | solution.py:217
  39.9 17.3 %all_to_all.17.got_ref = f32[8,16,128]{2,1,0:T(8,128)S(1)} all-to-all(f32[8,16,128]{2,1,0:T(8,128)S(1)} %get-tuple-element.10), channel_id=1, replica_groups=mesh['far'=8,'near'=16,'chan'=4] {'far'}, dimensions={0} | all-to-all | bytes 131072 | tf_op jit(solution)/shard_map/all_to_all | solution.py:311
  57.2 1.7 %finish.1 = bf16[64,256]{1,0:T(8,128)(2,1)} custom-call(f32[8,16,128]{2,1,0:T(8,128)S(1)} %all_to_all.17.got_ref, f32[16,128]{1,0:T(8,128)S(1)} %get-tuple-element.11.near_ref, f32[408,128]{1,0:T(8,128)S(1)} %get-tuple-element.12.keep_ref, f32[16,64]{1,0:T(8,128)} %bitcast.8, f32[16,64]{1,0:T(8,128)} %bitcast.6, f32[1,64]{1,0:T(1,128)} %bitcast.11), custom_call_target="tpu_custom_call" | custom-call | tf_op jit(solution)/shard_map/finish/pallas_call | solution.py:296
Async XLA Ops:
  0.0 17.5 %copy-start = (f32[64,16]{0,1:T(8,128)S(1)}, f32[64,16]{0,1:T(8,128)}, u32[]{:S(2)}) copy-start(f32[64,16]{0,1:T(8,128)} %param.10) | copy-start | bytes 12292
  0.0 17.5 %copy-start.1 = (f32[64,16]{0,1:T(8,128)S(1)}, f32[64,16]{0,1:T(8,128)}, u32[]{:S(2)}) copy-start(f32[64,16]{0,1:T(8,128)} %param.9) | copy-start | bytes 12292
  0.0 17.5 %copy-start.2 = (f32[3,3,64]{2,1,0:T(4,128)S(1)}, f32[3,3,64]{2,1,0:T(4,128)}, u32[]{:S(2)}) copy-start(f32[3,3,64]{2,1,0:T(4,128)} %short_ref.1) | copy-start | bytes 6916

commit v4 on v3

--- a/solution.py
+++ b/solution.py
@@ -48,30 +48,25 @@
     pieces = tok_sems.shape[0]
     deep = depth // pieces
     parts = [pl.ds(i * deep, deep) for i in range(pieces)]
-    tok_copies = [
-        pltpu.make_async_copy(tok_hbm.at[:, part], tok_ref.at[:, part], tok_sems.at[i]) for i, part in enumerate(parts)
-    ]
-    w_copies = [
-        [pltpu.make_async_copy(w_hbm.at[s, part], w_ref.at[s, part], w_sems.at[s, i]) for i, part in enumerate(parts)]
-        for s in range(streams)
-    ]
-    for i in range(pieces):
-        tok_copies[i].start()
-        w_copies[0][i].start()
-    for s in range(1, streams):
-        for copy in w_copies[s]:
+    copies = []
+    for i, part in enumerate(parts):
+        copies.append([pltpu.make_async_copy(tok_hbm.at[:, part], tok_ref.at[:, part], tok_sems.at[i])])
+        for s in range(streams):
+            copies[i].append(pltpu.make_async_copy(w_hbm.at[s, part], w_ref.at[s, part], w_sems.at[s, i]))
+    for piece in copies:
+        for copy in piece:
             copy.start()
+    for i, part in enumerate(parts):
+        for copy in copies[i]:
+            copy.wait()
+        for s in range(streams):
+            term = jnp.dot(tok_ref[:, part], w_ref[s, part, :], preferred_element_type=F32)
+            acc_ref[s] = term if i == 0 else acc_ref[s] + term
+    rows = acc_ref.shape[1] // 2
     for s in range(streams):
-        for i, part in enumerate(parts):
-            if s == 0:
-                tok_copies[i].wait()
-            w_copies[s][i].wait()
-            term = jnp.dot(tok_ref[:, part], w_ref[s, part, :], preferred_element_type=F32)
-            acc_ref[...] = term if i == 0 else acc_ref[...] + term
-        rows = acc_ref.shape[0] // 2
-        for pair in range(acc_ref.shape[1] // 128):
-            early = acc_ref[:rows, 128 * pair : 128 * (pair + 1)]
-            late = acc_ref[rows:, 128 * pair : 128 * (pair + 1)]
+        for pair in range(acc_ref.shape[2] // 128):
+            early = acc_ref[s, :rows, 128 * pair : 128 * (pair + 1)]
+            late = acc_ref[s, rows:, 128 * pair : 128 * (pair + 1)]
             left = lanes_of(early.shape) < 64
             out_ref[2 * pair, s] = jnp.where(left, early, swap(late))
             out_ref[2 * pair + 1, s] = jnp.where(left, swap(early), late)
@@ -89,7 +84,7 @@
         scratch_shapes=[
             pltpu.VMEM(tokens.shape, tokens.dtype),
             pltpu.VMEM(weight.shape, weight.dtype),
-            pltpu.VMEM((rows, width), F32),
+            pltpu.VMEM((streams, rows, width), F32),
             pltpu.SemaphoreType.DMA((pieces,)),
             pltpu.SemaphoreType.DMA((streams, pieces)),
         ],

time: 59.1 us -> 58.1 us (0.983)
  Pallas kernels: 7.58 us -> 6.56 us
    pallas_call x1, Pallas kernels: 4.48 us -> 3.46 us  [project(): pl.pallas_call(project_kernel, in_specs=[HBM, HBM], out_shape=pltpu.VMEM(...]
where the time goes in v4:
time: 58.1 us; the launch traced here: 57.8 us
  blocking collectives  51.2 us (88%)
  Pallas kernels  6.56 us (11%)
    all_to_all x1, blocking collectives, per_device(): got = lax.all_to_all(send, 'near', 0, 0, tiled=True)  21 us
    all_to_all x1, blocking collectives, per_device(): got = lax.all_to_all(send, 'far', 0, 0, tiled=True)  17.3 us
    all_to_all x1, blocking collectives, per_device(): parts = lax.all_to_all(partials, 'chan', 0, 0, tiled=True)  13 us
    pallas_call x1, Pallas kernels, project(): pl.pallas_call(project_kernel, in_specs=[HBM, HBM], out_shape=pltpu.VMEM(...  3.46 us
    pallas_call x1, Pallas kernels, finish(): pl.pallas_call(functools.partial(finish_kernel, shard_rows), out_shape=ja...  1.66 us

profile of v4, /device:TPU:1, one launch (start us, length us, event | category | flops | bytes accessed | tf_op | source)
XLA Modules:
  0.0 57.8 jit_solution(7192991024412649487)
XLA Ops:
  0.0 0.0 copy-start
  0.0 0.0 copy-start.1
  0.0 0.0 copy-start.2
  0.0 3.5 %project.1 = f32[4,3,128,128]{3,2,1,0:T(8,128)S(1)} custom-call(bf16[256,2048]{1,0:T(8,128)(2,1)} %tok_hbm.1, bf16[3,2048,256]{2,1,0:T(8,128)(2,1)} %bitcast.10), custom_call_target="tpu_custom_call" | custom-call | tf_op jit(solution)/shard_map/project/pallas_call | solution.py:80
  3.5 13.0 %all_to_all.15.part_ref = f32[4,3,128,128]{3,2,1,0:T(8,128)S(1)} all-to-all(f32[4,3,128,128]{3,2,1,0:T(8,128)S(1)} %project.1), channel_id=1, replica_groups=mesh['far'=8,'near'=16,'chan'=4] {'chan'}, dimensions={0} | all-to-all | bytes 1572864 | tf_op jit(solution)/shard_map/all_to_all | solution.py:302
  16.5 0.0 copy-done
  16.5 0.0 copy-done.1
  16.5 0.0 copy-done.2
  16.5 0.6 %local.1 = (f32[16,16,128]{2,1,0:T(8,128)S(1)}, f32[408,128]{1,0:T(8,128)S(1)}) custom-call(f32[4,3,128,128]{3,2,1,0:T(8,128)S(1)} %all_to_all.15.part_ref, f32[3,3,64]{2,1,0:T(4,128)S(1)} %copy-done.2, f32[16,64]{1,0:T(8,128)S(1)} %bitcast.9, f32[16,64]{1,0:T(8,128)S(1)} %bitcast.7), custom_call_target="tpu_custom_call" | custom-call | tf_op jit(solution)/shard_map/local/pallas_call | solution.py:166
  17.1 21.0 %all_to_all.16.got_ref = f32[16,16,128]{2,1,0:T(8,128)S(1)} all-to-all(f32[16,16,128]{2,1,0:T(8,128)S(1)} %get-tuple-element.9), channel_id=1, replica_groups=mesh['far'=8,'near'=16,'chan'=4] {'near'}, dimensions={0} | all-to-all | bytes 262144 | tf_op jit(solution)/shard_map/all_to_all | solution.py:304
  38.1 0.8 %near_sums.1 = (f32[8,16,128]{2,1,0:T(8,128)S(1)}, f32[16,128]{1,0:T(8,128)S(1)}) custom-call(f32[16,16,128]{2,1,0:T(8,128)S(1)} %all_to_all.16.got_ref, f32[16,64]{1,0:T(8,128)} %bitcast.5), custom_call_target="tpu_custom_call" | custom-call | tf_op jit(solution)/shard_map/near_sums/pallas_call | solution.py:212
  38.9 17.3 %all_to_all.17.got_ref = f32[8,16,128]{2,1,0:T(8,128)S(1)} all-to-all(f32[8,16,128]{2,1,0:T(8,128)S(1)} %get-tuple-element.10), channel_id=1, replica_groups=mesh['far'=8,'near'=16,'chan'=4] {'far'}, dimensions={0} | all-to-all | bytes 131072 | tf_op jit(solution)/shard_map/all_to_all | solution.py:306
  56.2 1.7 %finish.1 = bf16[64,256]{1,0:T(8,128)(2,1)} custom-call(f32[8,16,128]{2,1,0:T(8,128)S(1)} %all_to_all.17.got_ref, f32[16,128]{1,0:T(8,128)S(1)} %get-tuple-element.11.near_ref, f32[408,128]{1,0:T(8,128)S(1)} %get-tuple-element.12.keep_ref, f32[16,64]{1,0:T(8,128)} %bitcast.8, f32[16,64]{1,0:T(8,128)} %bitcast.6, f32[1,64]{1,0:T(1,128)} %bitcast.11), custom_call_target="tpu_custom_call" | custom-call | tf_op jit(solution)/shard_map/finish/pallas_call | solution.py:291
Async XLA Ops:
  0.0 16.5 %copy-start = (f32[64,16]{0,1:T(8,128)S(1)}, f32[64,16]{0,1:T(8,128)}, u32[]{:S(2)}) copy-start(f32[64,16]{0,1:T(8,128)} %param.10) | copy-start | bytes 12292
  0.0 16.5 %copy-start.1 = (f32[64,16]{0,1:T(8,128)S(1)}, f32[64,16]{0,1:T(8,128)}, u32[]{:S(2)}) copy-start(f32[64,16]{0,1:T(8,128)} %param.9) | copy-start | bytes 12292
  0.0 16.5 %copy-start.2 = (f32[3,3,64]{2,1,0:T(4,128)S(1)}, f32[3,3,64]{2,1,0:T(4,128)}, u32[]{:S(2)}) copy-start(f32[3,3,64]{2,1,0:T(4,128)} %short_ref.1) | copy-start | bytes 6916

commit v5 on v4

--- a/solution.py
+++ b/solution.py
@@ -43,16 +43,16 @@
     return jnp.concatenate([poles[:half], poles[half:]], axis=1)
 
 
-def project_kernel(tok_hbm, w_hbm, out_ref, tok_ref, w_ref, acc_ref, tok_sems, w_sems):
+def project_kernel(tok_hbm, w_hbm, out_ref, tok_ref, w_ref, acc_ref, sems):
     streams, depth, _ = w_ref.shape
-    pieces = tok_sems.shape[0]
+    pieces = sems.shape[0]
     deep = depth // pieces
     parts = [pl.ds(i * deep, deep) for i in range(pieces)]
     copies = []
     for i, part in enumerate(parts):
-        copies.append([pltpu.make_async_copy(tok_hbm.at[:, part], tok_ref.at[:, part], tok_sems.at[i])])
+        copies.append([pltpu.make_async_copy(tok_hbm.at[:, part], tok_ref.at[:, part], sems.at[i, streams])])
         for s in range(streams):
-            copies[i].append(pltpu.make_async_copy(w_hbm.at[s, part], w_ref.at[s, part], w_sems.at[s, i]))
+            copies[i].append(pltpu.make_async_copy(w_hbm.at[s, part], w_ref.at[s, part], sems.at[i, s]))
     for piece in copies:
         for copy in piece:
             copy.start()
@@ -85,8 +85,7 @@
             pltpu.VMEM(tokens.shape, tokens.dtype),
             pltpu.VMEM(weight.shape, weight.dtype),
             pltpu.VMEM((streams, rows, width), F32),
-            pltpu.SemaphoreType.DMA((pieces,)),
-            pltpu.SemaphoreType.DMA((streams, pieces)),
+            pltpu.SemaphoreType.DMA((pieces, streams + 1)),
         ],
         compiler_params=ROOMY,
         name="project",
@@ -171,7 +170,7 @@
         ),
         compiler_params=ROOMY,
         name="local",
-    )(in_vmem(parts), short_weight, residue, rates)
+    )(in_vmem(parts), in_vmem(short_weight), in_vmem(residue), in_vmem(rates))
 
 
 def gate_of(tile, before):
@@ -212,8 +211,9 @@
     return pl.pallas_call(
         functools.partial(near_kernel, shard_rows),
         out_shape=(pltpu.VMEM((far_count, 16, width), F32), pltpu.VMEM((16, width), F32)),
+        compiler_params=ROOMY,
         name="near_sums",
-    )(in_vmem(got), rates)
+    )(in_vmem(got), in_vmem(rates))
 
 
 def finish_kernel(shard_rows, got_ref, near_ref, keep_ref, residue_ref, rates_ref, skip_ref, out_ref):
@@ -291,8 +291,9 @@
     return pl.pallas_call(
         functools.partial(finish_kernel, shard_rows),
         out_shape=jax.ShapeDtypeStruct((width // 2, shard_rows), jnp.bfloat16),
+        compiler_params=ROOMY,
         name="finish",
-    )(in_vmem(got), in_vmem(near), in_vmem(keep), residue, rates, skip)
+    )(in_vmem(got), in_vmem(near), in_vmem(keep), in_vmem(residue), in_vmem(rates), in_vmem(skip))
 
 
 def per_device(tokens, in_weight, short_weight, residue, rates, skip):

time: 58.1 us -> 56.2 us (0.967)
  Pallas kernels: 6.56 us -> 4.76 us
    pallas_call x1, Pallas kernels: 1.66 us -> 0.94 us  [finish(): pl.pallas_call(functools.partial(finish_kernel, shard_rows), out_shape=ja...]
    pallas_call x1, Pallas kernels: 0.81 us -> 0.11 us  [near_sums(): pl.pallas_call(functools.partial(near_kernel, shard_rows), out_shape=(plt...]
where the time goes in v5:
time: 56.2 us; the launch traced here: 56 us
  blocking collectives  51.2 us (91%)
  Pallas kernels  4.76 us (8%)
    all_to_all x1, blocking collectives, per_device(): got = lax.all_to_all(send, 'near', 0, 0, tiled=True)  21 us
    all_to_all x1, blocking collectives, per_device(): got = lax.all_to_all(send, 'far', 0, 0, tiled=True)  17.3 us
    all_to_all x1, blocking collectives, per_device(): parts = lax.all_to_all(partials, 'chan', 0, 0, tiled=True)  13 us
    pallas_call x1, Pallas kernels, project(): pl.pallas_call(project_kernel, in_specs=[HBM, HBM], out_shape=pltpu.VMEM(...  3.07 us

profile of v5, /device:TPU:1, one launch (start us, length us, event | category | flops | bytes accessed | tf_op | source)
XLA Modules:
  0.0 56.0 jit_solution(13634863293270757059)
XLA Ops:
  0.0 0.0 copy-start
  0.0 0.0 copy-start.1
  0.0 0.0 copy-start.2
  0.0 0.0 copy-start.3
  0.0 3.1 %project.1 = f32[4,3,128,128]{3,2,1,0:T(8,128)S(1)} custom-call(bf16[256,2048]{1,0:T(8,128)(2,1)} %tok_hbm.1, bf16[3,2048,256]{2,1,0:T(8,128)(2,1)} %bitcast.11), custom_call_target="tpu_custom_call" | custom-call | tf_op jit(solution)/shard_map/project/pallas_call | solution.py:80
  3.1 13.0 %all_to_all.15.part_ref = f32[4,3,128,128]{3,2,1,0:T(8,128)S(1)} all-to-all(f32[4,3,128,128]{3,2,1,0:T(8,128)S(1)} %project.1), channel_id=1, replica_groups=mesh['far'=8,'near'=16,'chan'=4] {'chan'}, dimensions={0} | all-to-all | bytes 1572864 | tf_op jit(solution)/shard_map/all_to_all | solution.py:303
  16.1 0.0 copy-done
  16.1 0.0 copy-done.1
  16.1 0.0 copy-done.2
  16.1 0.6 %local.1 = (f32[16,16,128]{2,1,0:T(8,128)S(1)}, f32[408,128]{1,0:T(8,128)S(1)}) custom-call(f32[4,3,128,128]{3,2,1,0:T(8,128)S(1)} %all_to_all.15.part_ref, f32[3,3,64]{2,1,0:T(4,128)S(1)} %copy-done.2, f32[16,64]{1,0:T(8,128)S(1)} %bitcast.8, f32[16,64]{1,0:T(8,128)S(1)} %bitcast.5), custom_call_target="tpu_custom_call" | custom-call | tf_op jit(solution)/shard_map/local/pallas_call | solution.py:165
  16.7 21.0 %all_to_all.16.got_ref = f32[16,16,128]{2,1,0:T(8,128)S(1)} all-to-all(f32[16,16,128]{2,1,0:T(8,128)S(1)} %get-tuple-element.9), channel_id=1, replica_groups=mesh['far'=8,'near'=16,'chan'=4] {'near'}, dimensions={0} | all-to-all | bytes 262144 | tf_op jit(solution)/shard_map/all_to_all | solution.py:305
  37.7 0.1 near_sums.1
  37.8 17.3 %all_to_all.17.got_ref = f32[8,16,128]{2,1,0:T(8,128)S(1)} all-to-all(f32[8,16,128]{2,1,0:T(8,128)S(1)} %get-tuple-element.10), channel_id=1, replica_groups=mesh['far'=8,'near'=16,'chan'=4] {'far'}, dimensions={0} | all-to-all | bytes 131072 | tf_op jit(solution)/shard_map/all_to_all | solution.py:307
  55.1 0.0 copy-done.3
  55.1 0.9 %finish.1 = bf16[64,256]{1,0:T(8,128)(2,1)} custom-call(f32[8,16,128]{2,1,0:T(8,128)S(1)} %all_to_all.17.got_ref, f32[16,128]{1,0:T(8,128)S(1)} %get-tuple-element.11.near_ref, f32[408,128]{1,0:T(8,128)S(1)} %get-tuple-element.12.keep_ref, f32[16,64]{1,0:T(8,128)S(1)} %bitcast.9, f32[16,64]{1,0:T(8,128)S(1)} %bitcast.7, f32[1,64]{1,0:T(1,128)S(1)} %bitcast.10), custom_call_target="tpu_custom_call" | custom-call | tf_op jit(solution)/shard_map/finish/pallas_call | solution.py:291
Async XLA Ops:
  0.0 16.1 %copy-start = (f32[64,16]{0,1:T(8,128)S(1)}, f32[64,16]{0,1:T(8,128)}, u32[]{:S(2)}) copy-start(f32[64,16]{0,1:T(8,128)} %param.10) | copy-start | bytes 12292
  0.0 16.1 %copy-start.1 = (f32[64,16]{0,1:T(8,128)S(1)}, f32[64,16]{0,1:T(8,128)}, u32[]{:S(2)}) copy-start(f32[64,16]{0,1:T(8,128)} %param.9) | copy-start | bytes 12292
  0.0 16.1 %copy-start.2 = (f32[3,3,64]{2,1,0:T(4,128)S(1)}, f32[3,3,64]{2,1,0:T(4,128)}, u32[]{:S(2)}) copy-start(f32[3,3,64]{2,1,0:T(4,128)} %short_ref.1) | copy-start | bytes 6916
  0.0 55.1 %copy-start.3 = (f32[64]{0:T(128)S(1)}, f32[64]{0:T(128)}, u32[]{:S(2)}) copy-start(f32[64]{0:T(128)} %param.11) | copy-start | bytes 772

commit v6 on v5

--- a/solution.py
+++ b/solution.py
@@ -92,7 +92,7 @@
     )(in_hbm(tokens), in_hbm(weight))
 
 
-def local_kernel(part_ref, short_ref, residue_ref, rates_ref, send_ref, keep_ref):
+def local_kernel(part_ref, short_ref, residue_ref, rates_ref, skip_ref, send_ref, keep_ref):
     count = part_ref.shape[0]
     rows, width = part_ref.shape[2:]
     right = lanes_of((1, width)) >= width // 2
@@ -126,6 +126,10 @@
     rates = twice(rates_ref[...])
     weight = twice(residue_ref[...]) * jnp.sqrt(2.0 * rates)
     poles = rates.shape[0]
+    at = 3 * rows + 8 + poles
+    keep_ref[at : at + poles, :] = rates
+    keep_ref[at + poles : at + 2 * poles, :] = weight
+    keep_ref[at + 2 * poles :, :] = jnp.broadcast_to(twice(skip_ref[...]), (8, width))
     inner = rows_of((STEP, width))
     step_pos = inner.astype(F32)
     impulse = [jnp.sum(weight * jnp.exp(-rates * float(u)), axis=0, keepdims=True) for u in range(STEP)]
@@ -151,7 +155,7 @@
             state[r] = gain
         keep_ref[2 * rows + k * STEP : 2 * rows + (k + 1) * STEP, :] = yk
     half = jnp.concatenate(state, axis=0)
-    keep_ref[3 * rows + 8 :, :] = half
+    keep_ref[3 * rows + 8 : at, :] = half
     total = half + jnp.exp(-float(rows) * rates) * swap(half)
     h = poles // 2
     packed = jnp.where(right, total[h:], swap(total[:h]))
@@ -160,17 +164,17 @@
         send_ref[i, 8:16, :] = own
 
 
-def local(parts, short_weight, residue, rates):
+def local(parts, short_weight, residue, rates, skip):
     _, _, rows, width = parts.shape
     return pl.pallas_call(
         local_kernel,
         out_shape=(
             pltpu.VMEM((NEAR, 16, width), F32),
-            pltpu.VMEM((3 * rows + 8 + rates.shape[0], width), F32),
+            pltpu.VMEM((3 * rows + 16 + 3 * rates.shape[0], width), F32),
         ),
         compiler_params=ROOMY,
         name="local",
-    )(in_vmem(parts), in_vmem(short_weight), in_vmem(residue), in_vmem(rates))
+    )(in_vmem(parts), in_vmem(short_weight), in_vmem(residue), in_vmem(rates), in_vmem(skip))
 
 
 def gate_of(tile, before):
@@ -198,31 +202,81 @@
         prefix = jnp.where(near > i, grown, prefix)
     keep_ref[0:8, :] = prefix
     keep_ref[8:16, :] = before
+    keep_ref[16:24, :] = rates
     head = got_ref[0, 8:16, :]
     tail = got_ref[NEAR - 1, 8:16, :]
     ends = jnp.where(rows_of(head.shape) < 2, head, tail)
-    for i in range(send_ref.shape[0]):
-        send_ref[i, 0:8, :] = total
-        send_ref[i, 8:16, :] = ends
-
-
-def near_sums(got, rates, shard_rows, far_count):
+    send_ref[0:8, :] = total
+    send_ref[8:16, :] = ends
+
+
+def near_sums(got, rates, shard_rows):
     width = got.shape[2]
     return pl.pallas_call(
         functools.partial(near_kernel, shard_rows),
-        out_shape=(pltpu.VMEM((far_count, 16, width), F32), pltpu.VMEM((16, width), F32)),
+        out_shape=(pltpu.VMEM((16, width), F32), pltpu.VMEM((24, width), F32)),
         compiler_params=ROOMY,
         name="near_sums",
     )(in_vmem(got), in_vmem(rates))
 
 
-def finish_kernel(shard_rows, got_ref, near_ref, keep_ref, residue_ref, rates_ref, skip_ref, out_ref):
-    near, far = lax.axis_index("near"), lax.axis_index("far")
+def with_row(shard_rows, row, got, rates):
+    gate = gate_of(row[8:16], got[8:16])
+    start = jnp.exp(-(shard_rows - 1.0) * rates) * gate[0:1] + jnp.exp(-(shard_rows - 2.0) * rates) * gate[1:2]
+    state = row[0:8] + jnp.exp(-float((NEAR - 1) * shard_rows) * rates) * start
+    state = state + jnp.exp(-float(NEAR * shard_rows) * rates) * got[0:8]
+    return jnp.concatenate([state, row[8:16]], axis=0)
+
+
+def first_kernel(shard_rows, row_ref, near_ref, total_ref):
+    total_ref[...] = with_row(shard_rows, row_ref[...], jnp.zeros(row_ref.shape, F32), near_ref[16:24, :])
+
+
+def first_sum(shard_rows, row, near):
+    return pl.pallas_call(
+        functools.partial(first_kernel, shard_rows),
+        out_shape=pltpu.VMEM(row.shape, F32),
+        compiler_params=ROOMY,
+        name="first_sum",
+    )(in_vmem(row), in_vmem(near))
+
+
+def hop_kernel(shard_rows, sums, sources, *refs):
+    rows_before, (row_ref, near_ref, keep_ref), refs = refs[:sources], refs[sources : sources + 3], refs[sources + 3 :]
+    sum_refs, (before_ref, row_out, near_out, keep_out) = refs[:sums], refs[sums:]
+    rates = near_ref[16:24, :]
+    before = rows_before[0][...]
+    if sources > 1:
+        before = with_row(shard_rows, rows_before[1][...], before, rates)
+    before_ref[...] = before
+    if sums:
+        total = with_row(shard_rows, row_ref[...], before, rates)
+    for ref in sum_refs:
+        ref[...] = total
+    row_out[...] = row_ref[...]
+    near_out[...] = near_ref[...]
+    keep_out[...] = keep_ref[...]
+
+
+def hop(shard_rows, sums, sources, row, near, keep):
+    operands = [in_vmem(a) for a in (*sources, row, near, keep)]
+    outs = (row,) * (sums + 2) + (near, keep)
+    return pl.pallas_call(
+        functools.partial(hop_kernel, shard_rows, sums, len(sources)),
+        out_shape=tuple(pltpu.VMEM(a.shape, F32) for a in outs),
+        compiler_params=ROOMY,
+        name="hop",
+    )(*operands)
+
+
+def finish_kernel(shard_rows, row_ref, got_ref, near_ref, keep_ref, out_ref):
+    near = lax.axis_index("near")
     rows, width = out_ref.shape[1] // 2, keep_ref.shape[1]
-    rates = twice(rates_ref[...])
-    weight = twice(residue_ref[...]) * jnp.sqrt(2.0 * rates)
-    poles = rates.shape[0]
-    skip = twice(skip_ref[...])
+    poles = 2 * near_ref[16:24, :].shape[0]
+    at = 3 * rows + 8 + poles
+    rates = keep_ref[at : at + poles, :]
+    weight = keep_ref[at + poles : at + 2 * poles, :]
+    skip = keep_ref[at + 2 * poles : at + 2 * poles + 1, :]
     step_pos = rows_of((STEP, width)).astype(F32)
     decay = jnp.exp(-float(STEP) * rates)
     half_decay = jnp.exp(-float(rows) * rates)
@@ -232,28 +286,18 @@
         outof.append(weight[r : r + 1] * jnp.exp(-rates[r : r + 1] * (step_pos + 1.0)))
         fade.append(jnp.broadcast_to(decay[r : r + 1], (STEP, width)))
 
-    rates = folded(rates_ref[...])
+    rates = near_ref[16:24, :]
     first = jnp.exp(-(shard_rows - 1.0) * rates)
     second = jnp.exp(-(shard_rows - 2.0) * rates)
-    last = jnp.exp(-float((NEAR - 1) * shard_rows) * rates)
-    row_fade = jnp.exp(-float(NEAR * shard_rows) * rates)
     place = near.astype(F32) * float(shard_rows)
     place_fade = jnp.exp(-place * rates)
     beyond_fade = jnp.where(near > 0, jnp.exp(-jnp.maximum(place - shard_rows, 0.0) * rates), 0.0)
     ahead_one, ahead_two = jnp.exp(rates), jnp.exp(2.0 * rates)
-    before = near_ref[8:16, :]
-    carry = jnp.zeros_like(rates)
-    opening = jnp.zeros_like(rates)
-    edge = None
-    for z in range(got_ref.shape[0]):
-        gate = gate_of(got_ref[z, 8:16, :], edge)
-        start = first * gate[0:1] + second * gate[1:2]
-        opening = jnp.where(far == z, start, opening)
-        if edge is not None:
-            before = jnp.where(jnp.logical_and(near == 0, far == z), edge, before)
-        grown = carry * row_fade + (got_ref[z, 0:8, :] + last * start)
-        carry = jnp.where(far > z, grown, carry)
-        edge = got_ref[z, 8:16, :]
+    edge = got_ref[8:16, :]
+    before = jnp.where(near == 0, edge, near_ref[8:16, :])
+    gate = gate_of(row_ref[8:16, :], edge)
+    opening = first * gate[0:1] + second * gate[1:2]
+    carry = got_ref[0:8, :]
     state = near_ref[0:8, :] + place_fade * carry + beyond_fade * opening
     gate = gate_of(keep_ref[3 * rows : 3 * rows + 8, :], before)
     state = state + ahead_one * gate[0:1] + ahead_two * gate[1:2]
@@ -261,7 +305,7 @@
     left = lanes_of((1, width)) < width // 2
     other = swap(state)
     whole = jnp.concatenate([jnp.where(left, state, other), jnp.where(left, other, state)], axis=0)
-    whole = jnp.where(left, whole, swap(keep_ref[3 * rows + 8 :, :]) + half_decay * whole)
+    whole = jnp.where(left, whole, swap(keep_ref[3 * rows + 8 : 3 * rows + 8 + poles, :]) + half_decay * whole)
     states = [jnp.broadcast_to(whole[r : r + 1], (STEP, width)) * outof[r] for r in range(poles)]
     steps = []
     for k in range(rows // STEP):
@@ -286,26 +330,81 @@
     out_ref[:, rows:] = mixed[width // 2 :].astype(out_ref.dtype)
 
 
-def finish(shard_rows, got, near, keep, residue, rates, skip):
+def finish(shard_rows, row, got, near, keep):
     width = keep.shape[1]
     return pl.pallas_call(
         functools.partial(finish_kernel, shard_rows),
         out_shape=jax.ShapeDtypeStruct((width // 2, shard_rows), jnp.bfloat16),
         compiler_params=ROOMY,
         name="finish",
-    )(in_vmem(got), in_vmem(near), in_vmem(keep), in_vmem(residue), in_vmem(rates), in_vmem(skip))
+    )(in_vmem(row), in_vmem(got), in_vmem(near), in_vmem(keep))
+
+
+def moved_kernel(source_ref, target_ref):
+    target_ref[...] = source_ref[...]
+
+
+def moved(array):
+    return pl.pallas_call(
+        moved_kernel, out_shape=pltpu.VMEM(array.shape, F32), compiler_params=ROOMY, name="moved"
+    )(in_vmem(array))
+
+
+def nothing(*shapes):
+    return pl.pallas_call(
+        lambda *refs: None,
+        out_shape=tuple(pltpu.VMEM(shape, F32) for shape in shapes),
+        name="nothing",
+    )()
 
 
 def per_device(tokens, in_weight, short_weight, residue, rates, skip):
     shard_rows = tokens.shape[0]
-    residue, rates = residue.T, rates.T
-    partials = project(tokens, in_weight.transpose(1, 0, 2))
-    parts = lax.all_to_all(partials, "chan", 0, 0, tiled=True)
-    send, keep = local(parts, short_weight, residue, rates)
-    got = lax.all_to_all(send, "near", 0, 0, tiled=True)
-    send, near = near_sums(got, rates, shard_rows, lax.axis_size("far"))
-    got = lax.all_to_all(send, "far", 0, 0, tiled=True)
-    return finish(shard_rows, got, near, keep, residue, rates, skip[None, :]).T
+    residue, rates, skip = residue.T, rates.T, skip[None, :]
+    weight = in_weight.transpose(1, 0, 2)
+    far, far_count = lax.axis_index("far"), lax.axis_size("far")
+
+    def row_of_shards():
+        parts = lax.all_to_all(project(tokens, weight), "chan", 0, 0, tiled=True)
+        send, keep = local(parts, short_weight, residue, rates, skip)
+        row, near = near_sums(lax.all_to_all(send, "near", 0, 0, tiled=True), rates, shard_rows)
+        return row, near, keep
+
+    shapes = [a.shape for a in jax.eval_shape(row_of_shards)]
+
+    def work_of(mine):
+        return lax.cond(mine, row_of_shards, lambda: nothing(*shapes))
+
+    row, near, keep = even = work_of(far % 2 == 0)
+    none = jnp.zeros(shapes[0], F32)
+
+    def hand_on(after, total, k):
+        here = jnp.logical_or(far == k, far == k + 1)
+        return lax.cond(here, lambda: moved(lax.ppermute(total, "far", [(k, k + 1)])), lambda: moved(after))
+
+    total = first_sum(shard_rows, row, near)
+    results = [(row, none, near, keep)]
+    after = none
+    for k in range(1, far_count, 2):
+        sums = 2 if k + 1 < far_count else 0
+
+        def odd_row(k=k, total=total, sums=sums):
+            sources = [lax.ppermute(total, "far", [(max(k - 2, 0), k)])]
+            if k > 1:
+                sources.append(lax.ppermute(even[0], "far", [(k - 1, k)]))
+            return hop(shard_rows, sums, sources, *work_of(far == k))
+
+        here = jnp.logical_and(far <= k, far >= k - 2)
+        out = lax.cond(here, odd_row, lambda sums=sums: nothing(*shapes[:1] * (sums + 1), *shapes))
+        before, *rest = out[sums:]
+        results.append((rest[0], before, *rest[1:]))
+        if k > 1:
+            again, *out = lax.optimization_barrier((again, *out))
+            after = hand_on(after, again, k - 2)
+        total, again = out[:2]
+    results[0] = (row, after, near, keep)
+    branches = [lambda r=r: finish(shard_rows, *r) for r in results]
+    return lax.switch(jnp.where(far % 2 == 0, 0, (far + 1) // 2), branches).T
 
 
 def solution(mesh):

time: 56.2 us -> 50.5 us (0.90)
  the two profiles are of different devices: /device:TPU:1 before, /device:TPU:384 now
where the time goes in v6:
time: 50.5 us; the launch traced here: 50.3 us
  blocking collectives  32.1 us (64%)
  waiting for transfers between devices  9.69 us (19%)
  Pallas kernels  4.3 us (9%)
  starting transfers between devices  3.24 us (6%)
  local copies, waits for them, and re-layouts  0.63 us (1%)
    all_to_all x1, blocking collectives, row_of_shards(): parts = lax.all_to_all(project(tokens, weight), 'chan', 0, 0, tiled=True)  16.4 us
    all_to_all x1, blocking collectives, row_of_shards(): lax.all_to_all(send, 'near', 0, 0, tiled=True)  15.7 us
    ppermute x1, waiting for transfers between devices, hand_on(): lax.ppermute(total, 'far', [(k, k + 1)])  8.38 us
    pallas_call x1, Pallas kernels, project(): pl.pallas_call(project_kernel, in_specs=[HBM, HBM], out_shape=pltpu.VMEM(...  3.07 us
    ppermute x1, waiting for transfers between devices, odd_row(): sources.append(lax.ppermute(even[0], 'far', [(k - 1, k)]))  1.3 us
    ppermute x1, starting transfers between devices, hand_on(): lax.ppermute(total, 'far', [(k, k + 1)])  1.29 us
    ppermute x1, starting transfers between devices, odd_row(): sources.append(lax.ppermute(even[0], 'far', [(k - 1, k)]))  1.29 us
  transfers between devices with their start and end apart: 3, of which 2 were waited for; matrix products, arithmetic and copies ran while one was open for 0% of the time, Pallas kernels for 0%

profile of v6, /device:TPU:384, one launch (start us, length us, event | category | flops | bytes accessed | tf_op | source)
XLA Modules:
  0.0 50.3 jit_solution(12432592666976496209)
XLA Ops:
  0.0 36.0 %conditional.13 = ((f32[16,128]{1,0:T(8,128)S(1)}, f32[24,128]{1,0:T(8,128)S(1)}, f32[448,128]{1,0:T(8,128)S(1)})) conditional(s32[]{:T(128)} %convert_element_type.36, () %tuple.100, (bf16[256,2048]{1,0:T(8,128)(2,1)}, bf16[3,2048,256]{2,1,0:T(8,128)(2,1)}, f32[3,3,64]{2,1,0:T(4,128)}, f32[16,64]{1,0:T(8,128)}, f32[16,64]{1,0:T(8,128)}, ...), branch_computations={%region_0.1_spmd, %region_1.2_spmd} | conditional | bytes 1878160 | solution.py:376
  0.0 0.0 copy-start.15
  0.0 3.1 %project.5 = f32[4,3,128,128]{3,2,1,0:T(8,128)S(1)} custom-call(bf16[256,2048]{1,0:T(8,128)(2,1)} %get-tuple-element.194.tok_hbm, bf16[3,2048,256]{2,1,0:T(8,128)(2,1)} %get-tuple-element.196.w_hbm), custom_call_target="tpu_custom_call" | custom-call | tf_op jit(solution)/shard_map/cond/branch_1_fun/project/pallas_call | solution.py:80
  3.1 16.4 %all_to_all.40.part_ref = f32[4,3,128,128]{3,2,1,0:T(8,128)S(1)} all-to-all(f32[4,3,128,128]{3,2,1,0:T(8,128)S(1)} %project.5), channel_id=1, replica_groups=mesh['far'=8,'near'=16,'chan'=4] {'chan'}, dimensions={0} | all-to-all | bytes 1572864 | tf_op jit(solution)/shard_map/cond/branch_1_fun/all_to_all | solution.py:368
  19.5 0.0 copy-done
  19.5 0.0 copy-done.5
  19.5 0.0 copy-done.10
  19.5 0.6 %local.5 = (f32[16,16,128]{2,1,0:T(8,128)S(1)}, f32[448,128]{1,0:T(8,128)S(1)}) custom-call(f32[4,3,128,128]{3,2,1,0:T(8,128)S(1)} %all_to_all.40.part_ref, f32[3,3,64]{2,1,0:T(4,128)S(1)} %copy-done.10, f32[16,64]{1,0:T(8,128)S(1)} %copy-done.5, f32[16,64]{1,0:T(8,128)S(1)} %copy-done, f32[1,64]{1,0:T(1,128)S(1)} %copy-done.15), custom_call_target="tpu_custom_call" | custom-call | tf_op jit(solution)/shard_map/cond/branch_1_fun/local/pallas_call | solution.py:169
  20.1 15.7 %all_to_all.41.got_ref = f32[16,16,128]{2,1,0:T(8,128)S(1)} all-to-all(f32[16,16,128]{2,1,0:T(8,128)S(1)} %get-tuple-element.201), channel_id=1, replica_groups=mesh['far'=8,'near'=16,'chan'=4] {'near'}, dimensions={0} | all-to-all | bytes 262144 | tf_op jit(solution)/shard_map/cond/branch_1_fun/all_to_all | solution.py:370
  35.9 0.1 near_sums.5
  36.0 0.1 first_sum.1
  36.1 3.4 %conditional.19 = ((f32[16,128]{1,0:T(8,128)S(1)}, f32[16,128]{1,0:T(8,128)S(1)}, f32[24,128]{1,0:T(8,128)S(1)}, f32[448,128]{1,0:T(8,128)S(1)})) conditional(s32[]{:T(128)} %convert_element_type.43, () %tuple.111, (f32[16,128]{1,0:T(8,128)S(1)}, f32[16,128]{1,0:T(8,128)S(1)}, s32[]{:T(128)}, bf16[256,2048]{1,0:T(8,128)(2,1)}, ...), branch_computations={%region_18.19_spmd, %region_19.22_spmd} | conditional | flops 2 | bytes 1943846 | solution.py:398
  36.2 0.7 %collective-permute-start.7 = (f32[16,128]{1,0:T(8,128)S(1)}, f32[16,128]{1,0:T(8,128)S(1)}, u32[]{:S(2)}, u32[]{:S(2)}) collective-permute-start(f32[16,128]{1,0:T(8,128)S(1)} %get-tuple-element.280), channel_id=1, source_target_pairs={{320,448},{321,449},{322,450},{323,451},{324,452},{325,453},{326,4... | collective-permute-start | bytes 24584 | tf_op jit(solution)/shard_map/cond/branch_1_fun/ppermute | solution.py:392
  36.8 1.3 %collective-permute-start.8 = (f32[16,128]{1,0:T(8,128)S(1)}, f32[16,128]{1,0:T(8,128)S(1)}, u32[]{:S(2)}, u32[]{:S(2)}) collective-permute-start(f32[16,128]{1,0:T(8,128)S(1)} %get-tuple-element.281), channel_id=1, source_target_pairs={{384,448},{385,449},{386,450},{387,451},{388,452},{389,453},{390,4... | collective-permute-start | bytes 24584 | tf_op jit(solution)/shard_map/cond/branch_1_fun/ppermute | solution.py:394
  38.2 0.0 collective-permute-done.7.refs_0_
  38.2 1.3 %collective-permute-done.8.refs_1_ = f32[16,128]{1,0:T(8,128)S(1)} collective-permute-done((f32[16,128]{1,0:T(8,128)S(1)}, f32[16,128]{1,0:T(8,128)S(1)}, u32[]{:S(2)}, u32[]{:S(2)}) %collective-permute-start.8) | collective-permute-done | bytes 8224 | tf_op jit(solution)/shard_map/cond/branch_1_fun/ppermute | solution.py:394
  39.5 0.1 hop.7
  39.6 9.7 %conditional.20 = (f32[16,128]{1,0:T(8,128)S(1)}) conditional(s32[]{:T(128)} %convert_element_type.37, f32[16,128]{1,0:T(8,128)S(1)} %get-tuple-element.459, f32[16,128]{1,0:T(8,128)S(1)} %get-tuple-element.370), branch_computations={%region_22.23_spmd, %region_23.24_spmd} | conditional | bytes 32816 | solution.py:383
  39.6 1.3 %collective-permute-start.9 = (f32[16,128]{1,0:T(8,128)S(1)}, f32[16,128]{1,0:T(8,128)S(1)}, u32[]{:S(2)}, u32[]{:S(2)}) collective-permute-start(f32[16,128]{1,0:T(8,128)S(1)} %param.23), channel_id=1, source_target_pairs={{320,384},{321,385},{322,386},{323,387},{324,388},{325,389},{326,3... | collective-permute-start | bytes 24584 | tf_op jit(solution)/shard_map/cond/branch_1_fun/ppermute | solution.py:383
  40.9 8.4 %collective-permute-done.9.source_ref = f32[16,128]{1,0:T(8,128)S(1)} collective-permute-done((f32[16,128]{1,0:T(8,128)S(1)}, f32[16,128]{1,0:T(8,128)S(1)}, u32[]{:S(2)}, u32[]{:S(2)}) %collective-permute-start.9) | collective-permute-done | bytes 8224 | tf_op jit(solution)/shard_map/cond/branch_1_fun/ppermute | solution.py:383
  49.3 0.3 conditional.21
  49.3 0.3 finish.5
  49.6 0.0 copy-start.20
  49.7 0.6 %copy-done.20 = bf16[64,256]{1,0:T(8,128)(2,1)} copy-done((bf16[64,256]{1,0:T(8,128)(2,1)}, bf16[64,256]{1,0:T(8,128)(2,1)S(1)}, u32[]{:S(2)}) %copy-start.20) | copy-done | bytes 32792
  (18 shorter events, 0.1 us)
Async XLA Ops:
  0.0 19.5 %copy-start = (f32[16,64]{1,0:T(8,128)S(1)}, f32[16,64]{1,0:T(8,128)}, u32[]{:S(2)}) copy-start(f32[16,64]{1,0:T(8,128)} %get-tuple-element.199.rates_ref) | copy-start | bytes 12292 | tf_op jit(solution)/shard_map/cond
  0.0 19.5 %copy-start.5 = (f32[16,64]{1,0:T(8,128)S(1)}, f32[16,64]{1,0:T(8,128)}, u32[]{:S(2)}) copy-start(f32[16,64]{1,0:T(8,128)} %get-tuple-element.198.residue_ref) | copy-start | bytes 12292 | tf_op jit(solution)/shard_map/cond
  0.0 19.5 %copy-start.10 = (f32[3,3,64]{2,1,0:T(4,128)S(1)}, f32[3,3,64]{2,1,0:T(4,128)}, u32[]{:S(2)}) copy-start(f32[3,3,64]{2,1,0:T(4,128)} %get-tuple-element.197.short_ref) | copy-start | bytes 6916 | tf_op jit(solution)/shard_map/cond
  0.0 19.5 %copy-start.15 = (f32[1,64]{1,0:T(1,128)S(1)}, f32[1,64]{1,0:T(1,128)}, u32[]{:S(2)}) copy-start(f32[1,64]{1,0:T(1,128)} %get-tuple-element.200.skip_ref) | copy-start | bytes 772 | tf_op jit(solution)/shard_map/cond
  36.2 2.0 %collective-permute-start.7 = (f32[16,128]{1,0:T(8,128)S(1)}, f32[16,128]{1,0:T(8,128)S(1)}, u32[]{:S(2)}, u32[]{:S(2)}) collective-permute-start(f32[16,128]{1,0:T(8,128)S(1)} %get-tuple-element.280), channel_id=1, source_target_pairs={{320,448},{321,449},{322,450},{323,451},{324,452},{325,453},{326,4... | collective-permute-start | bytes 24584 | tf_op jit(solution)/shard_map/cond/branch_1_fun/ppermute | solution.py:392
  36.8 2.6 %collective-permute-start.8 = (f32[16,128]{1,0:T(8,128)S(1)}, f32[16,128]{1,0:T(8,128)S(1)}, u32[]{:S(2)}, u32[]{:S(2)}) collective-permute-start(f32[16,128]{1,0:T(8,128)S(1)} %get-tuple-element.281), channel_id=1, source_target_pairs={{384,448},{385,449},{386,450},{387,451},{388,452},{389,453},{390,4... | collective-permute-start | bytes 24584 | tf_op jit(solution)/shard_map/cond/branch_1_fun/ppermute | solution.py:394
  39.6 9.7 %collective-permute-start.9 = (f32[16,128]{1,0:T(8,128)S(1)}, f32[16,128]{1,0:T(8,128)S(1)}, u32[]{:S(2)}, u32[]{:S(2)}) collective-permute-start(f32[16,128]{1,0:T(8,128)S(1)} %param.23), channel_id=1, source_target_pairs={{320,384},{321,385},{322,386},{323,387},{324,388},{325,389},{326,3... | collective-permute-start | bytes 24584 | tf_op jit(solution)/shard_map/cond/branch_1_fun/ppermute | solution.py:383
  49.6 0.6 %copy-start.20 = (bf16[64,256]{1,0:T(8,128)(2,1)}, bf16[64,256]{1,0:T(8,128)(2,1)S(1)}, u32[]{:S(2)}) copy-start(bf16[64,256]{1,0:T(8,128)(2,1)S(1)} %get-tuple-element.462) | copy-start | bytes 98308

commit v7 on v6

--- a/solution.py
+++ b/solution.py
@@ -375,36 +375,36 @@
     def work_of(mine):
         return lax.cond(mine, row_of_shards, lambda: nothing(*shapes))
 
-    row, near, keep = even = work_of(far % 2 == 0)
     none = jnp.zeros(shapes[0], F32)
+    chained = jnp.logical_and(far > 0, far % 2 == 0)
+    row, near, keep = work_of(jnp.logical_not(chained))
+    total = first_sum(shard_rows, row, near)
+    again = total
+    after = none
+    results = [None]
 
     def hand_on(after, total, k):
         here = jnp.logical_or(far == k, far == k + 1)
         return lax.cond(here, lambda: moved(lax.ppermute(total, "far", [(k, k + 1)])), lambda: moved(after))
 
-    total = first_sum(shard_rows, row, near)
-    results = [(row, none, near, keep)]
-    after = none
-    for k in range(1, far_count, 2):
-        sums = 2 if k + 1 < far_count else 0
-
-        def odd_row(k=k, total=total, sums=sums):
-            sources = [lax.ppermute(total, "far", [(max(k - 2, 0), k)])]
-            if k > 1:
-                sources.append(lax.ppermute(even[0], "far", [(k - 1, k)]))
+    for k in range(2, far_count, 2):
+
+        sums = 2 if k + 2 < far_count else 1
+
+        def even_row(k=k, total=total, sums=sums):
+            sources = [lax.ppermute(total, "far", [(k - 2, k)]), lax.ppermute(row, "far", [(k - 1, k)])]
             return hop(shard_rows, sums, sources, *work_of(far == k))
 
         here = jnp.logical_and(far <= k, far >= k - 2)
-        out = lax.cond(here, odd_row, lambda sums=sums: nothing(*shapes[:1] * (sums + 1), *shapes))
-        before, *rest = out[sums:]
-        results.append((rest[0], before, *rest[1:]))
-        if k > 1:
-            again, *out = lax.optimization_barrier((again, *out))
-            after = hand_on(after, again, k - 2)
-        total, again = out[:2]
-    results[0] = (row, after, near, keep)
+        out = lax.cond(here, even_row, lambda sums=sums: nothing(*shapes[:1] * (sums + 1), *shapes))
+        results.append((out[sums + 1], out[sums], *out[sums + 2 :]))
+        again, *out = lax.optimization_barrier((again, *out))
+        after = hand_on(after, again, k - 2)
+        total, again = out[0], out[sums - 1]
+    after = hand_on(after, again, far_count - 2)
+    results[0] = (row, jnp.where(far == 0, none, after), near, keep)
     branches = [lambda r=r: finish(shard_rows, *r) for r in results]
-    return lax.switch(jnp.where(far % 2 == 0, 0, (far + 1) // 2), branches).T
+    return lax.switch(jnp.where(chained, far // 2, 0), branches).T
 
 
 def solution(mesh):

time: 50.5 us -> 49.4 us (0.978)
  the two profiles are of different devices: /device:TPU:384 before, /device:TPU:448 now
where the time goes in v7:
time: 49.4 us; the launch traced here: 49.2 us
  blocking collectives  32.1 us (65%)
  waiting for transfers between devices  10.6 us (21%)
  Pallas kernels  4.22 us (9%)
  starting transfers between devices  1.29 us (3%)
  local copies, waits for them, and re-layouts  0.63 us (1%)
    all_to_all x1, blocking collectives, row_of_shards(): parts = lax.all_to_all(project(tokens, weight), 'chan', 0, 0, tiled=True)  16.4 us
    all_to_all x1, blocking collectives, row_of_shards(): lax.all_to_all(send, 'near', 0, 0, tiled=True)  15.7 us
    ppermute x1, waiting for transfers between devices, hand_on(): lax.ppermute(total, 'far', [(k, k + 1)])  10.6 us
    pallas_call x1, Pallas kernels, project(): pl.pallas_call(project_kernel, in_specs=[HBM, HBM], out_shape=pltpu.VMEM(...  3.06 us
    ppermute x1, starting transfers between devices, hand_on(): lax.ppermute(total, 'far', [(k, k + 1)])  1.29 us
  transfers between devices with their start and end apart: 1, of which 1 were waited for; matrix products, arithmetic and copies ran while one was open for 0% of the time, Pallas kernels for 0%

profile of v7, /device:TPU:448, one launch (start us, length us, event | category | flops | bytes accessed | tf_op | source)
XLA Modules:
  0.0 49.2 jit_solution(10167905759303148491)
XLA Ops:
  0.0 36.0 %conditional.12 = ((f32[16,128]{1,0:T(8,128)S(1)}, f32[24,128]{1,0:T(8,128)S(1)}, f32[448,128]{1,0:T(8,128)S(1)})) conditional(s32[]{:T(128)} %convert_element_type.37, () %tuple.94, (bf16[256,2048]{1,0:T(8,128)(2,1)}, bf16[3,2048,256]{2,1,0:T(8,128)(2,1)}, f32[3,3,64]{2,1,0:T(4,128)}, f32[16,64]{1,0:T(8,128)}, f32[16,64]{1,0:T(8,128)}, ...), branch_computations={%region_0.1_spmd, %region_1.2_spmd} | conditional | bytes 1878160 | solution.py:376
  0.0 0.0 copy-start
  0.0 0.0 copy-start.4
  0.0 0.0 copy-start.8
  0.0 0.0 copy-start.12
  0.0 3.1 %project.4 = f32[4,3,128,128]{3,2,1,0:T(8,128)S(1)} custom-call(bf16[256,2048]{1,0:T(8,128)(2,1)} %get-tuple-element.176.tok_hbm, bf16[3,2048,256]{2,1,0:T(8,128)(2,1)} %get-tuple-element.177.w_hbm), custom_call_target="tpu_custom_call" | custom-call | tf_op jit(solution)/shard_map/cond/branch_1_fun/project/pallas_call | solution.py:80
  3.1 16.4 %all_to_all.32.part_ref = f32[4,3,128,128]{3,2,1,0:T(8,128)S(1)} all-to-all(f32[4,3,128,128]{3,2,1,0:T(8,128)S(1)} %project.4), channel_id=1, replica_groups=mesh['far'=8,'near'=16,'chan'=4] {'chan'}, dimensions={0} | all-to-all | bytes 1572864 | tf_op jit(solution)/shard_map/cond/branch_1_fun/all_to_all | solution.py:368
  19.5 0.0 copy-done
  19.5 0.0 copy-done.4
  19.5 0.0 copy-done.8
  19.5 0.0 copy-done.12
  19.5 0.6 %local.4 = (f32[16,16,128]{2,1,0:T(8,128)S(1)}, f32[448,128]{1,0:T(8,128)S(1)}) custom-call(f32[4,3,128,128]{3,2,1,0:T(8,128)S(1)} %all_to_all.32.part_ref, f32[3,3,64]{2,1,0:T(4,128)S(1)} %copy-done.8, f32[16,64]{1,0:T(8,128)S(1)} %copy-done.4, f32[16,64]{1,0:T(8,128)S(1)} %copy-done, f32[1,64]{1,0:T(1,128)S(1)} %copy-done.12), custom_call_target="tpu_custom_call" | custom-call | tf_op jit(solution)/shard_map/cond/branch_1_fun/local/pallas_call | solution.py:169
  20.1 15.7 %all_to_all.33.got_ref = f32[16,16,128]{2,1,0:T(8,128)S(1)} all-to-all(f32[16,16,128]{2,1,0:T(8,128)S(1)} %get-tuple-element.182), channel_id=1, replica_groups=mesh['far'=8,'near'=16,'chan'=4] {'near'}, dimensions={0} | all-to-all | bytes 262144 | tf_op jit(solution)/shard_map/cond/branch_1_fun/all_to_all | solution.py:370
  35.9 0.1 near_sums.4
  36.0 0.1 first_sum.1
  36.3 11.9 %conditional.19 = (f32[16,128]{1,0:T(8,128)S(1)}) conditional(s32[]{:T(128)} %convert_element_type.33, f32[16,128]{1,0:T(8,128)S(1)} %get-tuple-element.392, f32[16,128]{1,0:T(8,128)S(1)} %get-tuple-element.323), branch_computations={%region_20.21_spmd, %region_21.22_spmd} | conditional | bytes 32816 | solution.py:388
  36.3 1.3 %collective-permute-start.9 = (f32[16,128]{1,0:T(8,128)S(1)}, f32[16,128]{1,0:T(8,128)S(1)}, u32[]{:S(2)}, u32[]{:S(2)}) collective-permute-start(f32[16,128]{1,0:T(8,128)S(1)} %param.21), channel_id=1, source_target_pairs={{384,448},{385,449},{386,450},{387,451},{388,452},{389,453},{390,4... | collective-permute-start | bytes 24584 | tf_op jit(solution)/shard_map/cond/branch_1_fun/ppermute | solution.py:388
  37.6 10.6 %collective-permute-done.9.source_ref = f32[16,128]{1,0:T(8,128)S(1)} collective-permute-done((f32[16,128]{1,0:T(8,128)S(1)}, f32[16,128]{1,0:T(8,128)S(1)}, u32[]{:S(2)}, u32[]{:S(2)}) %collective-permute-start.9) | collective-permute-done | bytes 8224 | tf_op jit(solution)/shard_map/cond/branch_1_fun/ppermute | solution.py:388
  48.2 0.3 conditional.20
  48.2 0.3 finish.5
  48.5 0.0 copy-start.16
  48.6 0.6 %copy-done.16 = bf16[64,256]{1,0:T(8,128)(2,1)} copy-done((bf16[64,256]{1,0:T(8,128)(2,1)}, bf16[64,256]{1,0:T(8,128)(2,1)S(1)}, u32[]{:S(2)}) %copy-start.16) | copy-done | bytes 32792
  (15 shorter events, 0.1 us)
Async XLA Ops:
  0.0 19.5 %copy-start = (f32[16,64]{1,0:T(8,128)S(1)}, f32[16,64]{1,0:T(8,128)}, u32[]{:S(2)}) copy-start(f32[16,64]{1,0:T(8,128)} %get-tuple-element.180.rates_ref) | copy-start | bytes 12292 | tf_op jit(solution)/shard_map/cond
  0.0 19.5 %copy-start.4 = (f32[16,64]{1,0:T(8,128)S(1)}, f32[16,64]{1,0:T(8,128)}, u32[]{:S(2)}) copy-start(f32[16,64]{1,0:T(8,128)} %get-tuple-element.179.residue_ref) | copy-start | bytes 12292 | tf_op jit(solution)/shard_map/cond
  0.0 19.5 %copy-start.8 = (f32[3,3,64]{2,1,0:T(4,128)S(1)}, f32[3,3,64]{2,1,0:T(4,128)}, u32[]{:S(2)}) copy-start(f32[3,3,64]{2,1,0:T(4,128)} %get-tuple-element.178.short_ref) | copy-start | bytes 6916 | tf_op jit(solution)/shard_map/cond
  0.0 19.5 %copy-start.12 = (f32[1,64]{1,0:T(1,128)S(1)}, f32[1,64]{1,0:T(1,128)}, u32[]{:S(2)}) copy-start(f32[1,64]{1,0:T(1,128)} %get-tuple-element.181.skip_ref) | copy-start | bytes 772 | tf_op jit(solution)/shard_map/cond
  36.3 11.9 %collective-permute-start.9 = (f32[16,128]{1,0:T(8,128)S(1)}, f32[16,128]{1,0:T(8,128)S(1)}, u32[]{:S(2)}, u32[]{:S(2)}) collective-permute-start(f32[16,128]{1,0:T(8,128)S(1)} %param.21), channel_id=1, source_target_pairs={{384,448},{385,449},{386,450},{387,451},{388,452},{389,453},{390,4... | collective-permute-start | bytes 24584 | tf_op jit(solution)/shard_map/cond/branch_1_fun/ppermute | solution.py:388
  48.5 0.6 %copy-start.16 = (bf16[64,256]{1,0:T(8,128)(2,1)}, bf16[64,256]{1,0:T(8,128)(2,1)S(1)}, u32[]{:S(2)}) copy-start(bf16[64,256]{1,0:T(8,128)(2,1)S(1)} %get-tuple-element.394) | copy-start | bytes 98308

commit v8 on v7

--- a/solution.py
+++ b/solution.py
@@ -121,15 +121,43 @@
         jnp.where(right, edges[0][1], swap(edges[0][0])),
     ]
     own = jnp.concatenate(tile + [jnp.zeros((3, width), F32)], axis=0)
-    keep_ref[3 * rows : 3 * rows + 8, :] = own
+    keep_ref[2 * rows : 2 * rows + 8, :] = own
 
     rates = twice(rates_ref[...])
     weight = twice(residue_ref[...]) * jnp.sqrt(2.0 * rates)
     poles = rates.shape[0]
-    at = 3 * rows + 8 + poles
+    at = 2 * rows + 8 + poles
     keep_ref[at : at + poles, :] = rates
     keep_ref[at + poles : at + 2 * poles, :] = weight
     keep_ref[at + 2 * poles :, :] = jnp.broadcast_to(twice(skip_ref[...]), (8, width))
+    step_pos = rows_of((STEP, width)).astype(F32)
+    decay = jnp.exp(-float(STEP) * rates)
+    half = []
+    for r in range(poles):
+        sums = x[:STEP]
+        for k in range(1, rows // STEP):
+            sums = sums * decay[r : r + 1] + x[k * STEP : (k + 1) * STEP]
+        into = jnp.exp(-rates[r : r + 1] * (STEP - 1.0 - step_pos))
+        half.append(jnp.sum(into * sums, axis=0, keepdims=True))
+    half = jnp.concatenate(half, axis=0)
+    keep_ref[2 * rows + 8 : at, :] = half
+    total = half + jnp.exp(-float(rows) * rates) * swap(half)
+    h = poles // 2
+    packed = jnp.where(right, total[h:], swap(total[:h]))
+    for i in range(send_ref.shape[0]):
+        send_ref[i, 0:8, :] = packed
+        send_ref[i, 8:16, :] = own
+
+
+def within_kernel(keep_ref, *outs):
+    *kept_refs, y_ref = outs
+    for ref in kept_refs:
+        ref[...] = keep_ref[...]
+    rows, width = y_ref.shape
+    poles = (keep_ref.shape[0] - 2 * rows - 16) // 3
+    at = 2 * rows + 8 + poles
+    rates = keep_ref[at : at + poles, :]
+    weight = keep_ref[at + poles : at + 2 * poles, :]
     inner = rows_of((STEP, width))
     step_pos = inner.astype(F32)
     impulse = [jnp.sum(weight * jnp.exp(-rates * float(u)), axis=0, keepdims=True) for u in range(STEP)]
@@ -143,7 +171,7 @@
         fade.append(decay[r : r + 1])
     state = [None] * poles
     for k in range(rows // STEP):
-        xk = x[k * STEP : (k + 1) * STEP]
+        xk = keep_ref[rows + k * STEP : rows + (k + 1) * STEP, :]
         yk = near[0] * xk
         for u in range(1, STEP):
             yk = yk + near[u] * pltpu.roll(xk, u, 0)
@@ -153,15 +181,12 @@
                 yk = yk + outof[r] * state[r]
                 gain = gain + fade[r] * state[r]
             state[r] = gain
-        keep_ref[2 * rows + k * STEP : 2 * rows + (k + 1) * STEP, :] = yk
-    half = jnp.concatenate(state, axis=0)
-    keep_ref[3 * rows + 8 : at, :] = half
-    total = half + jnp.exp(-float(rows) * rates) * swap(half)
-    h = poles // 2
-    packed = jnp.where(right, total[h:], swap(total[:h]))
-    for i in range(send_ref.shape[0]):
-        send_ref[i, 0:8, :] = packed
-        send_ref[i, 8:16, :] = own
+        y_ref[k * STEP : (k + 1) * STEP, :] = yk
+
+
+def within(keep, rows, both):
+    outs = (pltpu.VMEM(keep.shape, F32),) * both + (pltpu.VMEM((rows, keep.shape[1]), F32),)
+    return pl.pallas_call(within_kernel, out_shape=outs, compiler_params=ROOMY, name="within")(in_vmem(keep))
 
 
 def local(parts, short_weight, residue, rates, skip):
@@ -170,7 +195,7 @@
         local_kernel,
         out_shape=(
             pltpu.VMEM((NEAR, 16, width), F32),
-            pltpu.VMEM((3 * rows + 16 + 3 * rates.shape[0], width), F32),
+            pltpu.VMEM((2 * rows + 16 + 3 * rates.shape[0], width), F32),
         ),
         compiler_params=ROOMY,
         name="local",
@@ -242,8 +267,10 @@
 
 
 def hop_kernel(shard_rows, sums, sources, *refs):
-    rows_before, (row_ref, near_ref, keep_ref), refs = refs[:sources], refs[sources : sources + 3], refs[sources + 3 :]
-    sum_refs, (before_ref, row_out, near_out, keep_out) = refs[:sums], refs[sums:]
+    kept = (len(refs) - sources - sums - 1) // 2
+    rows_before, work_refs, refs = refs[:sources], refs[sources : sources + kept], refs[sources + kept :]
+    sum_refs, before_ref, work_outs = refs[:sums], refs[sums], refs[sums + 1 :]
+    row_ref, near_ref = work_refs[:2]
     rates = near_ref[16:24, :]
     before = rows_before[0][...]
     if sources > 1:
@@ -253,14 +280,13 @@
         total = with_row(shard_rows, row_ref[...], before, rates)
     for ref in sum_refs:
         ref[...] = total
-    row_out[...] = row_ref[...]
-    near_out[...] = near_ref[...]
-    keep_out[...] = keep_ref[...]
-
-
-def hop(shard_rows, sums, sources, row, near, keep):
-    operands = [in_vmem(a) for a in (*sources, row, near, keep)]
-    outs = (row,) * (sums + 2) + (near, keep)
+    for ref, out in zip(work_refs, work_outs):
+        out[...] = ref[...]
+
+
+def hop(shard_rows, sums, sources, row, *rest):
+    operands = [in_vmem(a) for a in (*sources, row, *rest)]
+    outs = (row,) * (sums + 2) + rest
     return pl.pallas_call(
         functools.partial(hop_kernel, shard_rows, sums, len(sources)),
         out_shape=tuple(pltpu.VMEM(a.shape, F32) for a in outs),
@@ -269,11 +295,11 @@
     )(*operands)
 
 
-def finish_kernel(shard_rows, row_ref, got_ref, near_ref, keep_ref, out_ref):
+def finish_kernel(shard_rows, row_ref, got_ref, near_ref, keep_ref, y_ref, out_ref):
     near = lax.axis_index("near")
     rows, width = out_ref.shape[1] // 2, keep_ref.shape[1]
     poles = 2 * near_ref[16:24, :].shape[0]
-    at = 3 * rows + 8 + poles
+    at = 2 * rows + 8 + poles
     rates = keep_ref[at : at + poles, :]
     weight = keep_ref[at + poles : at + 2 * poles, :]
     skip = keep_ref[at + 2 * poles : at + 2 * poles + 1, :]
@@ -299,20 +325,20 @@
     opening = first * gate[0:1] + second * gate[1:2]
     carry = got_ref[0:8, :]
     state = near_ref[0:8, :] + place_fade * carry + beyond_fade * opening
-    gate = gate_of(keep_ref[3 * rows : 3 * rows + 8, :], before)
+    gate = gate_of(keep_ref[2 * rows : 2 * rows + 8, :], before)
     state = state + ahead_one * gate[0:1] + ahead_two * gate[1:2]
 
     left = lanes_of((1, width)) < width // 2
     other = swap(state)
     whole = jnp.concatenate([jnp.where(left, state, other), jnp.where(left, other, state)], axis=0)
-    whole = jnp.where(left, whole, swap(keep_ref[3 * rows + 8 : 3 * rows + 8 + poles, :]) + half_decay * whole)
+    whole = jnp.where(left, whole, swap(keep_ref[2 * rows + 8 : 2 * rows + 8 + poles, :]) + half_decay * whole)
     states = [jnp.broadcast_to(whole[r : r + 1], (STEP, width)) * outof[r] for r in range(poles)]
     steps = []
     for k in range(rows // STEP):
         at = k * STEP
         qk = keep_ref[at : at + STEP, :]
         xk = keep_ref[rows + at : rows + at + STEP, :]
-        yk = keep_ref[2 * rows + at : 2 * rows + at + STEP, :]
+        yk = y_ref[at : at + STEP, :]
         if k == 0:
             inner = rows_of((STEP, width))
             top = jnp.logical_and(left, inner == 0)
@@ -330,14 +356,16 @@
     out_ref[:, rows:] = mixed[width // 2 :].astype(out_ref.dtype)
 
 
-def finish(shard_rows, row, got, near, keep):
+def finish(shard_rows, row, got, near, keep, y=None):
     width = keep.shape[1]
+    if y is None:
+        (y,) = within(keep, shard_rows // 2, False)
     return pl.pallas_call(
         functools.partial(finish_kernel, shard_rows),
         out_shape=jax.ShapeDtypeStruct((width // 2, shard_rows), jnp.bfloat16),
         compiler_params=ROOMY,
         name="finish",
-    )(in_vmem(row), in_vmem(got), in_vmem(near), in_vmem(keep))
+    )(in_vmem(row), in_vmem(got), in_vmem(near), in_vmem(keep), in_vmem(y))
 
 
 def moved_kernel(source_ref, target_ref):
@@ -356,6 +384,10 @@
         out_shape=tuple(pltpu.VMEM(shape, F32) for shape in shapes),
         name="nothing",
     )()
+
+
+def crossed(source, target):
+    return [(source * NEAR + i, target * NEAR + (i ^ 1)) for i in range(NEAR)]
 
 
 def per_device(tokens, in_weight, short_weight, residue, rates, skip):
@@ -364,20 +396,23 @@
     weight = in_weight.transpose(1, 0, 2)
     far, far_count = lax.axis_index("far"), lax.axis_size("far")
 
-    def row_of_shards():
+    def row_of_shards(full):
         parts = lax.all_to_all(project(tokens, weight), "chan", 0, 0, tiled=True)
         send, keep = local(parts, short_weight, residue, rates, skip)
         row, near = near_sums(lax.all_to_all(send, "near", 0, 0, tiled=True), rates, shard_rows)
-        return row, near, keep
-
-    shapes = [a.shape for a in jax.eval_shape(row_of_shards)]
-
-    def work_of(mine):
-        return lax.cond(mine, row_of_shards, lambda: nothing(*shapes))
+        if not full:
+            return row, near, keep
+        row, keep = lax.optimization_barrier((row, keep))
+        return row, near, *within(keep, shard_rows // 2, True)
+
+    shapes = [a.shape for a in jax.eval_shape(lambda: row_of_shards(True))]
+
+    def work_of(mine, full=True):
+        return lax.cond(mine, lambda: row_of_shards(full), lambda: nothing(*shapes[: 3 + full]))
 
     none = jnp.zeros(shapes[0], F32)
     chained = jnp.logical_and(far > 0, far % 2 == 0)
-    row, near, keep = work_of(jnp.logical_not(chained))
+    row, near, keep = work_of(jnp.logical_not(chained), False)
     total = first_sum(shard_rows, row, near)
     again = total
     after = none
@@ -390,19 +425,28 @@
     for k in range(2, far_count, 2):
 
         sums = 2 if k + 2 < far_count else 1
-
-        def even_row(k=k, total=total, sums=sums):
-            sources = [lax.ppermute(total, "far", [(k - 2, k)]), lax.ppermute(row, "far", [(k - 1, k)])]
-            return hop(shard_rows, sums, sources, *work_of(far == k))
+        full = k > 2
+
+        def even_row(k=k, total=total, sums=sums, full=full):
+            sources = [lax.ppermute(total, ("far", "near"), crossed(k - 2, k)), lax.ppermute(row, "far", [(k - 1, k)])]
+            return hop(shard_rows, sums, sources, *work_of(far == k, full))
 
         here = jnp.logical_and(far <= k, far >= k - 2)
-        out = lax.cond(here, even_row, lambda sums=sums: nothing(*shapes[:1] * (sums + 1), *shapes))
+        out = lax.cond(here, even_row, lambda sums=sums, full=full: nothing(*shapes[:1] * (sums + 1), *shapes[: 3 + full]))
         results.append((out[sums + 1], out[sums], *out[sums + 2 :]))
         again, *out = lax.optimization_barrier((again, *out))
+        if k == 2:
+            keep, again = lax.optimization_barrier((keep, again))
+            kept = lax.cond(
+                chained,
+                lambda: nothing(shapes[2], shapes[3]),
+                lambda: within(keep, shard_rows // 2, True),
+            )
+            again, *kept = lax.optimization_barrier((again, *kept))
         after = hand_on(after, again, k - 2)
         total, again = out[0], out[sums - 1]
     after = hand_on(after, again, far_count - 2)
-    results[0] = (row, jnp.where(far == 0, none, after), near, keep)
+    results[0] = (row, jnp.where(far == 0, none, after), near, *kept)
     branches = [lambda r=r: finish(shard_rows, *r) for r in results]
     return lax.switch(jnp.where(chained, far // 2, 0), branches).T
 

time: 49.4 us -> 48.2 us (0.976)
  waiting for transfers between devices: 10.6 us -> 9.26 us
    ppermute x1, waiting for transfers between devices: 10.6 us -> 9.26 us  [hand_on(): lax.ppermute(total, 'far', [(k, k + 1)])]
where the time goes in v8:
time: 48.2 us; the launch traced here: 48 us
  blocking collectives  32.1 us (67%)
  waiting for transfers between devices  9.26 us (19%)
  Pallas kernels  4.36 us (9%)
  starting transfers between devices  1.29 us (3%)
  local copies, waits for them, and re-layouts  0.63 us (1%)
    all_to_all x1, blocking collectives, row_of_shards(): parts = lax.all_to_all(project(tokens, weight), 'chan', 0, 0, tiled=True)  16.4 us
    all_to_all x1, blocking collectives, row_of_shards(): lax.all_to_all(send, 'near', 0, 0, tiled=True)  15.7 us
    ppermute x1, waiting for transfers between devices, hand_on(): lax.ppermute(total, 'far', [(k, k + 1)])  9.26 us
    pallas_call x1, Pallas kernels, project(): pl.pallas_call(project_kernel, in_specs=[HBM, HBM], out_shape=pltpu.VMEM(...  3.06 us
    ppermute x1, starting transfers between devices, hand_on(): lax.ppermute(total, 'far', [(k, k + 1)])  1.29 us
  transfers between devices with their start and end apart: 1, of which 1 were waited for; matrix products, arithmetic and copies ran while one was open for 0% of the time, Pallas kernels for 0%

profile of v8, /device:TPU:448, one launch (start us, length us, event | category | flops | bytes accessed | tf_op | source)
XLA Modules:
  0.0 48.0 jit_solution(12928704948176008751)
XLA Ops:
  0.0 35.7 %conditional.13 = ((f32[16,128]{1,0:T(8,128)S(1)}, f32[24,128]{1,0:T(8,128)S(1)}, f32[320,128]{1,0:T(8,128)S(1)})) conditional(s32[]{:T(128)} %convert_element_type.40, () %tuple.104, (bf16[256,2048]{1,0:T(8,128)(2,1)}, bf16[3,2048,256]{2,1,0:T(8,128)(2,1)}, f32[3,3,64]{2,1,0:T(4,128)}, f32[16,64]{1,0:T(8,128)}, f32[16,64]{1,0:T(8,128)}, ...), branch_computations={%region_0.1_spmd, %region_1.2_spmd} | conditional | bytes 1878160 | solution.py:411
  0.0 0.0 copy-start
  0.0 0.0 copy-start.4
  0.0 0.0 copy-start.8
  0.0 0.0 copy-start.12
  0.0 3.1 %project.4 = f32[4,3,128,128]{3,2,1,0:T(8,128)S(1)} custom-call(bf16[256,2048]{1,0:T(8,128)(2,1)} %get-tuple-element.184.tok_hbm, bf16[3,2048,256]{2,1,0:T(8,128)(2,1)} %get-tuple-element.185.w_hbm), custom_call_target="tpu_custom_call" | custom-call | tf_op jit(solution)/shard_map/cond/branch_1_fun/project/pallas_call | solution.py:80
  3.1 16.4 %all_to_all.32.part_ref = f32[4,3,128,128]{3,2,1,0:T(8,128)S(1)} all-to-all(f32[4,3,128,128]{3,2,1,0:T(8,128)S(1)} %project.4), channel_id=1, replica_groups=mesh['far'=8,'near'=16,'chan'=4] {'chan'}, dimensions={0} | all-to-all | bytes 1572864 | tf_op jit(solution)/shard_map/cond/branch_1_fun/all_to_all | solution.py:400
  19.5 0.0 copy-done
  19.5 0.0 copy-done.4
  19.5 0.0 copy-done.8
  19.5 0.0 copy-done.12
  19.5 0.3 local.4
  19.8 15.7 %all_to_all.33.got_ref = f32[16,16,128]{2,1,0:T(8,128)S(1)} all-to-all(f32[16,16,128]{2,1,0:T(8,128)S(1)} %get-tuple-element.190), channel_id=1, replica_groups=mesh['far'=8,'near'=16,'chan'=4] {'near'}, dimensions={0} | all-to-all | bytes 262144 | tf_op jit(solution)/shard_map/cond/branch_1_fun/all_to_all | solution.py:402
  35.5 0.1 near_sums.4
  35.7 0.1 first_sum.1
  35.8 0.5 %conditional.15 = ((f32[320,128]{1,0:T(8,128)S(1)}, f32[128,128]{1,0:T(8,128)S(1)})) conditional(s32[]{:T(128)} %convert_element_type.42, f32[320,128]{1,0:T(8,128)S(1)} %get-tuple-element.338, () %tuple.110), branch_computations={%region_6.7_spmd, %region_7.8_spmd} | conditional | bytes 8 | solution.py:440
  35.8 0.5 within.4
  36.4 10.6 %conditional.21 = (f32[16,128]{1,0:T(8,128)S(1)}) conditional(s32[]{:T(128)} %convert_element_type.36, f32[16,128]{1,0:T(8,128)S(1)} %get-tuple-element.444, f32[16,128]{1,0:T(8,128)S(1)} %get-tuple-element.361), branch_computations={%region_22.23_spmd, %region_23.24_spmd} | conditional | bytes 32816 | solution.py:423
  36.4 1.3 %collective-permute-start.9 = (f32[16,128]{1,0:T(8,128)S(1)}, f32[16,128]{1,0:T(8,128)S(1)}, u32[]{:S(2)}, u32[]{:S(2)}) collective-permute-start(f32[16,128]{1,0:T(8,128)S(1)} %param.23), channel_id=1, source_target_pairs={{384,448},{385,449},{386,450},{387,451},{388,452},{389,453},{390,4... | collective-permute-start | bytes 24584 | tf_op jit(solution)/shard_map/cond/branch_1_fun/ppermute | solution.py:423
  37.7 9.3 %collective-permute-done.9.source_ref = f32[16,128]{1,0:T(8,128)S(1)} collective-permute-done((f32[16,128]{1,0:T(8,128)S(1)}, f32[16,128]{1,0:T(8,128)S(1)}, u32[]{:S(2)}, u32[]{:S(2)}) %collective-permute-start.9) | collective-permute-done | bytes 8224 | tf_op jit(solution)/shard_map/cond/branch_1_fun/ppermute | solution.py:423
  47.0 0.3 conditional.22
  47.0 0.3 finish.5
  47.4 0.0 copy-start.16
  47.4 0.6 %copy-done.16 = bf16[64,256]{1,0:T(8,128)(2,1)} copy-done((bf16[64,256]{1,0:T(8,128)(2,1)}, bf16[64,256]{1,0:T(8,128)(2,1)S(1)}, u32[]{:S(2)}) %copy-start.16) | copy-done | bytes 32792
  (15 shorter events, 0.1 us)
Async XLA Ops:
  0.0 19.5 %copy-start = (f32[16,64]{1,0:T(8,128)S(1)}, f32[16,64]{1,0:T(8,128)}, u32[]{:S(2)}) copy-start(f32[16,64]{1,0:T(8,128)} %get-tuple-element.188.rates_ref) | copy-start | bytes 12292 | tf_op jit(solution)/shard_map/cond
  0.0 19.5 %copy-start.4 = (f32[16,64]{1,0:T(8,128)S(1)}, f32[16,64]{1,0:T(8,128)}, u32[]{:S(2)}) copy-start(f32[16,64]{1,0:T(8,128)} %get-tuple-element.187.residue_ref) | copy-start | bytes 12292 | tf_op jit(solution)/shard_map/cond
  0.0 19.5 %copy-start.8 = (f32[3,3,64]{2,1,0:T(4,128)S(1)}, f32[3,3,64]{2,1,0:T(4,128)}, u32[]{:S(2)}) copy-start(f32[3,3,64]{2,1,0:T(4,128)} %get-tuple-element.186.short_ref) | copy-start | bytes 6916 | tf_op jit(solution)/shard_map/cond
  0.0 19.5 %copy-start.12 = (f32[1,64]{1,0:T(1,128)S(1)}, f32[1,64]{1,0:T(1,128)}, u32[]{:S(2)}) copy-start(f32[1,64]{1,0:T(1,128)} %get-tuple-element.189.skip_ref) | copy-start | bytes 772 | tf_op jit(solution)/shard_map/cond
  36.4 10.6 %collective-permute-start.9 = (f32[16,128]{1,0:T(8,128)S(1)}, f32[16,128]{1,0:T(8,128)S(1)}, u32[]{:S(2)}, u32[]{:S(2)}) collective-permute-start(f32[16,128]{1,0:T(8,128)S(1)} %param.23), channel_id=1, source_target_pairs={{384,448},{385,449},{386,450},{387,451},{388,452},{389,453},{390,4... | collective-permute-start | bytes 24584 | tf_op jit(solution)/shard_map/cond/branch_1_fun/ppermute | solution.py:423
  47.4 0.6 %copy-start.16 = (bf16[64,256]{1,0:T(8,128)(2,1)}, bf16[64,256]{1,0:T(8,128)(2,1)S(1)}, u32[]{:S(2)}) copy-start(bf16[64,256]{1,0:T(8,128)(2,1)S(1)} %get-tuple-element.446) | copy-start | bytes 98308

commit v9 on v8

--- a/solution.py
+++ b/solution.py
@@ -368,16 +368,6 @@
     )(in_vmem(row), in_vmem(got), in_vmem(near), in_vmem(keep), in_vmem(y))
 
 
-def moved_kernel(source_ref, target_ref):
-    target_ref[...] = source_ref[...]
-
-
-def moved(array):
-    return pl.pallas_call(
-        moved_kernel, out_shape=pltpu.VMEM(array.shape, F32), compiler_params=ROOMY, name="moved"
-    )(in_vmem(array))
-
-
 def nothing(*shapes):
     return pl.pallas_call(
         lambda *refs: None,
@@ -411,44 +401,44 @@
         return lax.cond(mine, lambda: row_of_shards(full), lambda: nothing(*shapes[: 3 + full]))
 
     none = jnp.zeros(shapes[0], F32)
-    chained = jnp.logical_and(far > 0, far % 2 == 0)
-    row, near, keep = work_of(jnp.logical_not(chained), False)
+    even = far % 2 == 0
+    row, near, keep = work_of(even, False)
     total = first_sum(shard_rows, row, near)
-    again = total
     after = none
     results = [None]
-
-    def hand_on(after, total, k):
-        here = jnp.logical_or(far == k, far == k + 1)
-        return lax.cond(here, lambda: moved(lax.ppermute(total, "far", [(k, k + 1)])), lambda: moved(after))
-
-    for k in range(2, far_count, 2):
-
-        sums = 2 if k + 2 < far_count else 1
-        full = k > 2
-
-        def even_row(k=k, total=total, sums=sums, full=full):
-            sources = [lax.ppermute(total, ("far", "near"), crossed(k - 2, k)), lax.ppermute(row, "far", [(k - 1, k)])]
-            return hop(shard_rows, sums, sources, *work_of(far == k, full))
+    for k in range(1, far_count, 2):
+        sums = int(k + 1 < far_count)
+        full = k != 3
+
+        two = jnp.where(far == k - 1, row, total)
+
+        def odd_row(k=k, total=total, two=two, sums=sums, full=full):
+            block = jnp.where(far == max(k - 2, 0), total, none)
+            sources = [lax.ppermute(block, ("far", "near"), crossed(max(k - 2, 0), k))]
+            extra = []
+            if k > 1:
+                steps = crossed(k - 2, k - 1) + crossed(k - 1, k)
+                extra = [lax.ppermute(two, ("far", "near"), steps)]
+                sources += extra
+            return hop(shard_rows, sums, sources, *work_of(far == k, full), *extra)
 
         here = jnp.logical_and(far <= k, far >= k - 2)
-        out = lax.cond(here, even_row, lambda sums=sums, full=full: nothing(*shapes[:1] * (sums + 1), *shapes[: 3 + full]))
-        results.append((out[sums + 1], out[sums], *out[sums + 2 :]))
-        again, *out = lax.optimization_barrier((again, *out))
-        if k == 2:
-            keep, again = lax.optimization_barrier((keep, again))
+        outs = shapes[:1] * (sums + 1) + shapes[: 3 + full] + shapes[:1] * (k > 1)
+        out = lax.cond(here, odd_row, lambda outs=outs: nothing(*outs))
+        results.append((out[sums + 1], out[sums], *out[sums + 2 : sums + 4 + full]))
+        if k > 1:
+            after = jnp.where(far == k - 1, out[-1], after)
+        if k == 3:
+            keep, *out = lax.optimization_barrier((keep, *out))
             kept = lax.cond(
-                chained,
-                lambda: nothing(shapes[2], shapes[3]),
-                lambda: within(keep, shard_rows // 2, True),
+                even, lambda: within(keep, shard_rows // 2, True), lambda: nothing(shapes[2], shapes[3])
             )
-            again, *kept = lax.optimization_barrier((again, *kept))
-        after = hand_on(after, again, k - 2)
-        total, again = out[0], out[sums - 1]
-    after = hand_on(after, again, far_count - 2)
-    results[0] = (row, jnp.where(far == 0, none, after), near, *kept)
+            *out, kept0, kept1 = lax.optimization_barrier((*out, *kept))
+            kept = (kept0, kept1)
+        total = out[0]
+    results[0] = (row, after, near, *kept)
     branches = [lambda r=r: finish(shard_rows, *r) for r in results]
-    return lax.switch(jnp.where(chained, far // 2, 0), branches).T
+    return lax.switch(jnp.where(even, 0, (far + 1) // 2), branches).T
 
 
 def solution(mesh):

time: 48.2 us -> 48 us (level)
  the two profiles are of different devices: /device:TPU:448 before, /device:TPU:385 now
where the time goes in v9:
time: 48 us; the launch traced here: 47.8 us
  blocking collectives  33.1 us (69%)
  waiting for transfers between devices  6.82 us (14%)
  Pallas kernels  4.43 us (9%)
  starting transfers between devices  2.58 us (5%)
  local copies, waits for them, and re-layouts  0.63 us (1%)
    all_to_all x1, blocking collectives, row_of_shards(): lax.all_to_all(send, 'near', 0, 0, tiled=True)  17.9 us
    all_to_all x1, blocking collectives, row_of_shards(): parts = lax.all_to_all(project(tokens, weight), 'chan', 0, 0, tiled=True)  15.2 us
    ppermute x1, waiting for transfers between devices, odd_row(): extra = [lax.ppermute(two, ('far', 'near'), steps)]  6.82 us
    pallas_call x1, Pallas kernels, project(): pl.pallas_call(project_kernel, in_specs=[HBM, HBM], out_shape=pltpu.VMEM(...  3.06 us
    ppermute x1, starting transfers between devices, odd_row(): extra = [lax.ppermute(two, ('far', 'near'), steps)]  1.92 us
  transfers between devices with their start and end apart: 2, of which 1 were waited for; matrix products, arithmetic and copies ran while one was open for 0% of the time, Pallas kernels for 0%

profile of v9, /device:TPU:385, one launch (start us, length us, event | category | flops | bytes accessed | tf_op | source)
XLA Modules:
  0.0 47.8 jit_solution(11376212967301801410)
XLA Ops:
  0.0 36.6 %conditional.11 = ((f32[16,128]{1,0:T(8,128)S(1)}, f32[24,128]{1,0:T(8,128)S(1)}, f32[320,128]{1,0:T(8,128)S(1)})) conditional(s32[]{:T(128)} %convert_element_type.30, () %tuple.96, (bf16[256,2048]{1,0:T(8,128)(2,1)}, bf16[3,2048,256]{2,1,0:T(8,128)(2,1)}, f32[3,3,64]{2,1,0:T(4,128)}, f32[16,64]{1,0:T(8,128)}, f32[16,64]{1,0:T(8,128)}, ...), branch_computations={%region_0.1_spmd, %region_1.2_spmd} | conditional | bytes 1878160 | solution.py:401
  0.0 0.0 copy-start.15
  0.0 3.1 %project.5 = f32[4,3,128,128]{3,2,1,0:T(8,128)S(1)} custom-call(bf16[256,2048]{1,0:T(8,128)(2,1)} %get-tuple-element.239.tok_hbm, bf16[3,2048,256]{2,1,0:T(8,128)(2,1)} %get-tuple-element.240.w_hbm), custom_call_target="tpu_custom_call" | custom-call | tf_op jit(solution)/shard_map/cond/branch_1_fun/project/pallas_call | solution.py:80
  3.1 15.2 %all_to_all.40.part_ref = f32[4,3,128,128]{3,2,1,0:T(8,128)S(1)} all-to-all(f32[4,3,128,128]{3,2,1,0:T(8,128)S(1)} %project.5), channel_id=1, replica_groups=mesh['far'=8,'near'=16,'chan'=4] {'chan'}, dimensions={0} | all-to-all | bytes 1572864 | tf_op jit(solution)/shard_map/cond/branch_1_fun/all_to_all | solution.py:390
  18.3 0.0 copy-done
  18.3 0.0 copy-done.5
  18.3 0.0 copy-done.10
  18.3 0.0 copy-done.15
  18.3 0.3 local.5
  18.6 17.9 %all_to_all.41.got_ref = f32[16,16,128]{2,1,0:T(8,128)S(1)} all-to-all(f32[16,16,128]{2,1,0:T(8,128)S(1)} %get-tuple-element.245), channel_id=1, replica_groups=mesh['far'=8,'near'=16,'chan'=4] {'near'}, dimensions={0} | all-to-all | bytes 262144 | tf_op jit(solution)/shard_map/cond/branch_1_fun/all_to_all | solution.py:392
  36.5 0.1 near_sums.5
  36.7 0.1 first_sum.1
  36.7 0.5 %conditional.14 = ((f32[320,128]{1,0:T(8,128)S(1)}, f32[128,128]{1,0:T(8,128)S(1)})) conditional(s32[]{:T(128)} %convert_element_type.30, () %tuple.102, f32[320,128]{1,0:T(8,128)S(1)} %get-tuple-element.429), branch_computations={%region_10.11_spmd, %region_11.12_spmd} | conditional | bytes 8 | solution.py:433
  36.8 0.5 within.6
  37.3 9.6 %conditional.16 = ((f32[16,128]{1,0:T(8,128)S(1)}, f32[16,128]{1,0:T(8,128)S(1)}, f32[24,128]{1,0:T(8,128)S(1)}, f32[320,128]{1,0:T(8,128)S(1)}, f32[128,128]{1,0:T(8,128)S(1)}, /*index=5*/f32[16,128]{1,0:T(8,128)S(1)})) conditional(s32[]{:T(128)} %convert_element_type.32, () %tuple.105, (s32[]{:T(128)}, f32[16,128]{1,0:T(8,128)S(1)}, pred[]{:T(512)}, ...), branch_computations={%region_16.17_spmd, %region_17.20_spmd} | conditional | flops 4099 | bytes 1976633 | solution.py:427
  37.3 0.7 %collective-permute-start.5 = (f32[16,128]{1,0:T(8,128)S(1)}, f32[16,128]{1,0:T(8,128)S(1)}, u32[]{:S(2)}, u32[]{:S(2)}) collective-permute-start(f32[16,128]{1,0:T(8,128)S(1)} %get-tuple-element.458), channel_id=1, source_target_pairs={{320,452},{324,448},{328,460},{332,456},{336,468},{340,464},{344,4... | collective-permute-start | bytes 24584 | tf_op jit(solution)/shard_map/cond/branch_1_fun/ppermute | solution.py:417
  38.0 1.9 %collective-permute-start.6 = (f32[16,128]{1,0:T(8,128)S(1)}, f32[16,128]{1,0:T(8,128)S(1)}, u32[]{:S(2)}, u32[]{:S(2)}) collective-permute-start(f32[16,128]{1,0:T(8,128)S(1)} %get-tuple-element.457), channel_id=1, source_target_pairs={{320,388},{324,384},{328,396},{332,392},{336,404},{340,400},{344,4... | collective-permute-start | bytes 24584 | tf_op jit(solution)/shard_map/cond/branch_1_fun/ppermute | solution.py:421
  40.0 0.0 collective-permute-done.5.refs_0_
  40.0 6.8 %collective-permute-done.6.refs_1_.refs_6_ = f32[16,128]{1,0:T(8,128)S(1)} collective-permute-done((f32[16,128]{1,0:T(8,128)S(1)}, f32[16,128]{1,0:T(8,128)S(1)}, u32[]{:S(2)}, u32[]{:S(2)}) %collective-permute-start.6) | collective-permute-done | bytes 8224 | tf_op jit(solution)/shard_map/cond/branch_1_fun/ppermute | solution.py:421
  46.8 0.1 hop.7
  46.9 0.3 conditional.17
  46.9 0.3 finish.6
  47.2 0.0 copy-start.20
  47.2 0.6 %copy-done.20 = bf16[64,256]{1,0:T(8,128)(2,1)} copy-done((bf16[64,256]{1,0:T(8,128)(2,1)}, bf16[64,256]{1,0:T(8,128)(2,1)S(1)}, u32[]{:S(2)}) %copy-start.20) | copy-done | bytes 32792
  (13 shorter events, 0.1 us)
Async XLA Ops:
  0.0 18.3 %copy-start = (f32[16,64]{1,0:T(8,128)S(1)}, f32[16,64]{1,0:T(8,128)}, u32[]{:S(2)}) copy-start(f32[16,64]{1,0:T(8,128)} %get-tuple-element.243.rates_ref) | copy-start | bytes 12292 | tf_op jit(solution)/shard_map/cond
  0.0 18.3 %copy-start.5 = (f32[16,64]{1,0:T(8,128)S(1)}, f32[16,64]{1,0:T(8,128)}, u32[]{:S(2)}) copy-start(f32[16,64]{1,0:T(8,128)} %get-tuple-element.242.residue_ref) | copy-start | bytes 12292 | tf_op jit(solution)/shard_map/cond
  0.0 18.3 %copy-start.10 = (f32[3,3,64]{2,1,0:T(4,128)S(1)}, f32[3,3,64]{2,1,0:T(4,128)}, u32[]{:S(2)}) copy-start(f32[3,3,64]{2,1,0:T(4,128)} %get-tuple-element.241.short_ref) | copy-start | bytes 6916 | tf_op jit(solution)/shard_map/cond
  0.0 18.3 %copy-start.15 = (f32[1,64]{1,0:T(1,128)S(1)}, f32[1,64]{1,0:T(1,128)}, u32[]{:S(2)}) copy-start(f32[1,64]{1,0:T(1,128)} %get-tuple-element.244.skip_ref) | copy-start | bytes 772 | tf_op jit(solution)/shard_map/cond
  37.3 2.6 %collective-permute-start.5 = (f32[16,128]{1,0:T(8,128)S(1)}, f32[16,128]{1,0:T(8,128)S(1)}, u32[]{:S(2)}, u32[]{:S(2)}) collective-permute-start(f32[16,128]{1,0:T(8,128)S(1)} %get-tuple-element.458), channel_id=1, source_target_pairs={{320,452},{324,448},{328,460},{332,456},{336,468},{340,464},{344,4... | collective-permute-start | bytes 24584 | tf_op jit(solution)/shard_map/cond/branch_1_fun/ppermute | solution.py:417
  38.0 8.8 %collective-permute-start.6 = (f32[16,128]{1,0:T(8,128)S(1)}, f32[16,128]{1,0:T(8,128)S(1)}, u32[]{:S(2)}, u32[]{:S(2)}) collective-permute-start(f32[16,128]{1,0:T(8,128)S(1)} %get-tuple-element.457), channel_id=1, source_target_pairs={{320,388},{324,384},{328,396},{332,392},{336,404},{340,400},{344,4... | collective-permute-start | bytes 24584 | tf_op jit(solution)/shard_map/cond/branch_1_fun/ppermute | solution.py:421
  47.2 0.6 %copy-start.20 = (bf16[64,256]{1,0:T(8,128)(2,1)}, bf16[64,256]{1,0:T(8,128)(2,1)S(1)}, u32[]{:S(2)}) copy-start(bf16[64,256]{1,0:T(8,128)(2,1)S(1)} %get-tuple-element.559) | copy-start | bytes 98308

commit v10 on v9

--- a/solution.py
+++ b/solution.py
@@ -144,9 +144,11 @@
     total = half + jnp.exp(-float(rows) * rates) * swap(half)
     h = poles // 2
     packed = jnp.where(right, total[h:], swap(total[:h]))
-    for i in range(send_ref.shape[0]):
-        send_ref[i, 0:8, :] = packed
-        send_ref[i, 8:16, :] = own
+    block = jnp.concatenate([packed, own[0:6]], axis=0)
+    for j in range(send_ref.shape[1]):
+        piece = block[2 * j : 2 * j + 2]
+        for i in range(send_ref.shape[0]):
+            send_ref[i, j] = piece
 
 
 def within_kernel(keep_ref, *outs):
@@ -194,7 +196,7 @@
     return pl.pallas_call(
         local_kernel,
         out_shape=(
-            pltpu.VMEM((NEAR, 16, width), F32),
+            pltpu.VMEM((NEAR, 7, 2, width), F32),
             pltpu.VMEM((2 * rows + 16 + 3 * rates.shape[0], width), F32),
         ),
         compiler_params=ROOMY,
@@ -215,28 +217,36 @@
     fade = jnp.exp(-float(shard_rows) * rates)
     first = jnp.exp(-(shard_rows - 1.0) * rates)
     second = jnp.exp(-(shard_rows - 2.0) * rates)
-    total = got_ref[0, 0:8, :]
+    blank = jnp.zeros((2, got_ref.shape[3]), F32)
+
+    def state_of(i):
+        return jnp.concatenate([got_ref[i, j] for j in range(4)], axis=0)
+
+    def tile_of(i):
+        return jnp.concatenate([got_ref[i, j] for j in range(4, 7)] + [blank], axis=0)
+
+    total = state_of(0)
+    head = edge = tile_of(0)
     prefix = jnp.where(near > 0, total, 0.0)
     before = jnp.zeros_like(total)
     for i in range(1, NEAR):
-        edge = got_ref[i - 1, 8:16, :]
-        gate = gate_of(got_ref[i, 8:16, :], edge)
-        grown = total * fade + (got_ref[i, 0:8, :] + first * gate[0:1] + second * gate[1:2])
+        tile = tile_of(i)
+        gate = gate_of(tile, edge)
+        grown = total * fade + (state_of(i) + first * gate[0:1] + second * gate[1:2])
         before = jnp.where(near == i, edge, before)
         total = grown
         prefix = jnp.where(near > i, grown, prefix)
+        edge = tile
     keep_ref[0:8, :] = prefix
     keep_ref[8:16, :] = before
     keep_ref[16:24, :] = rates
-    head = got_ref[0, 8:16, :]
-    tail = got_ref[NEAR - 1, 8:16, :]
-    ends = jnp.where(rows_of(head.shape) < 2, head, tail)
+    ends = jnp.where(rows_of(head.shape) < 2, head, edge)
     send_ref[0:8, :] = total
     send_ref[8:16, :] = ends
 
 
 def near_sums(got, rates, shard_rows):
-    width = got.shape[2]
+    width = got.shape[-1]
     return pl.pallas_call(
         functools.partial(near_kernel, shard_rows),
         out_shape=(pltpu.VMEM((16, width), F32), pltpu.VMEM((24, width), F32)),

time: 48 us -> 47.7 us (level)
  no operation moved by 1% of the time
where the time goes in v10:
time: 47.7 us; the launch traced here: 47.5 us
  blocking collectives  32.8 us (69%)
  waiting for transfers between devices  6.84 us (14%)
  Pallas kernels  4.44 us (9%)
  starting transfers between devices  2.58 us (5%)
  local copies, waits for them, and re-layouts  0.63 us (1%)
    all_to_all x1, blocking collectives, row_of_shards(): lax.all_to_all(send, 'near', 0, 0, tiled=True)  17.6 us
    all_to_all x1, blocking collectives, row_of_shards(): parts = lax.all_to_all(project(tokens, weight), 'chan', 0, 0, tiled=True)  15.2 us
    ppermute x1, waiting for transfers between devices, odd_row(): extra = [lax.ppermute(two, ('far', 'near'), steps)]  6.84 us
    pallas_call x1, Pallas kernels, project(): pl.pallas_call(project_kernel, in_specs=[HBM, HBM], out_shape=pltpu.VMEM(...  3.06 us
    ppermute x1, starting transfers between devices, odd_row(): extra = [lax.ppermute(two, ('far', 'near'), steps)]  1.92 us
  transfers between devices with their start and end apart: 2, of which 1 were waited for; matrix products, arithmetic and copies ran while one was open for 0% of the time, Pallas kernels for 0%

profile of v10, /device:TPU:385, one launch (start us, length us, event | category | flops | bytes accessed | tf_op | source)
XLA Modules:
  0.0 47.5 jit_solution(10758476790960062014)
XLA Ops:
  0.0 36.3 %conditional.11 = ((f32[16,128]{1,0:T(8,128)S(1)}, f32[24,128]{1,0:T(8,128)S(1)}, f32[320,128]{1,0:T(8,128)S(1)})) conditional(s32[]{:T(128)} %convert_element_type.30, () %tuple.96, (bf16[256,2048]{1,0:T(8,128)(2,1)}, bf16[3,2048,256]{2,1,0:T(8,128)(2,1)}, f32[3,3,64]{2,1,0:T(4,128)}, f32[16,64]{1,0:T(8,128)}, f32[16,64]{1,0:T(8,128)}, ...), branch_computations={%region_0.1_spmd, %region_1.2_spmd} | conditional | bytes 1845392 | solution.py:411
  0.0 0.0 copy-start.15
  0.0 3.1 %project.5 = f32[4,3,128,128]{3,2,1,0:T(8,128)S(1)} custom-call(bf16[256,2048]{1,0:T(8,128)(2,1)} %get-tuple-element.239.tok_hbm, bf16[3,2048,256]{2,1,0:T(8,128)(2,1)} %get-tuple-element.240.w_hbm), custom_call_target="tpu_custom_call" | custom-call | tf_op jit(solution)/shard_map/cond/branch_1_fun/project/pallas_call | solution.py:80
  3.1 15.2 %all_to_all.40.part_ref = f32[4,3,128,128]{3,2,1,0:T(8,128)S(1)} all-to-all(f32[4,3,128,128]{3,2,1,0:T(8,128)S(1)} %project.5), channel_id=1, replica_groups=mesh['far'=8,'near'=16,'chan'=4] {'chan'}, dimensions={0} | all-to-all | bytes 1572864 | tf_op jit(solution)/shard_map/cond/branch_1_fun/all_to_all | solution.py:400
  18.3 0.0 copy-done
  18.3 0.0 copy-done.5
  18.3 0.0 copy-done.10
  18.3 0.0 copy-done.15
  18.3 0.3 local.5
  18.6 17.6 %all_to_all.41.got_ref = f32[16,7,2,128]{3,2,1,0:T(2,128)S(1)} all-to-all(f32[16,7,2,128]{3,2,1,0:T(2,128)S(1)} %get-tuple-element.245), channel_id=1, replica_groups=mesh['far'=8,'near'=16,'chan'=4] {'near'}, dimensions={0} | all-to-all | bytes 229376 | tf_op jit(solution)/shard_map/cond/branch_1_fun/all_to_all | solution.py:402
  36.2 0.1 near_sums.5
  36.3 0.1 first_sum.1
  36.4 0.5 %conditional.14 = ((f32[320,128]{1,0:T(8,128)S(1)}, f32[128,128]{1,0:T(8,128)S(1)})) conditional(s32[]{:T(128)} %convert_element_type.30, () %tuple.102, f32[320,128]{1,0:T(8,128)S(1)} %get-tuple-element.429), branch_computations={%region_10.11_spmd, %region_11.12_spmd} | conditional | bytes 8 | solution.py:443
  36.4 0.5 %within.6 = (f32[320,128]{1,0:T(8,128)S(1)}, f32[128,128]{1,0:T(8,128)S(1)}) custom-call(f32[320,128]{1,0:T(8,128)S(1)} %keep_ref), custom_call_target="tpu_custom_call" | custom-call | tf_op jit(solution)/shard_map/cond/branch_1_fun/within/pallas_call | solution.py:191
  37.0 9.6 %conditional.16 = ((f32[16,128]{1,0:T(8,128)S(1)}, f32[16,128]{1,0:T(8,128)S(1)}, f32[24,128]{1,0:T(8,128)S(1)}, f32[320,128]{1,0:T(8,128)S(1)}, f32[128,128]{1,0:T(8,128)S(1)}, /*index=5*/f32[16,128]{1,0:T(8,128)S(1)})) conditional(s32[]{:T(128)} %convert_element_type.32, () %tuple.105, (s32[]{:T(128)}, f32[16,128]{1,0:T(8,128)S(1)}, pred[]{:T(512)}, ...), branch_computations={%region_16.17_spmd, %region_17.20_spmd} | conditional | flops 4099 | bytes 1943865 | solution.py:437
  37.0 0.7 %collective-permute-start.5 = (f32[16,128]{1,0:T(8,128)S(1)}, f32[16,128]{1,0:T(8,128)S(1)}, u32[]{:S(2)}, u32[]{:S(2)}) collective-permute-start(f32[16,128]{1,0:T(8,128)S(1)} %get-tuple-element.458), channel_id=1, source_target_pairs={{320,452},{324,448},{328,460},{332,456},{336,468},{340,464},{344,4... | collective-permute-start | bytes 24584 | tf_op jit(solution)/shard_map/cond/branch_1_fun/ppermute | solution.py:427
  37.7 1.9 %collective-permute-start.6 = (f32[16,128]{1,0:T(8,128)S(1)}, f32[16,128]{1,0:T(8,128)S(1)}, u32[]{:S(2)}, u32[]{:S(2)}) collective-permute-start(f32[16,128]{1,0:T(8,128)S(1)} %get-tuple-element.457), channel_id=1, source_target_pairs={{320,388},{324,384},{328,396},{332,392},{336,404},{340,400},{344,4... | collective-permute-start | bytes 24584 | tf_op jit(solution)/shard_map/cond/branch_1_fun/ppermute | solution.py:431
  39.6 0.0 collective-permute-done.5.refs_0_
  39.6 6.8 %collective-permute-done.6.refs_1_.refs_6_ = f32[16,128]{1,0:T(8,128)S(1)} collective-permute-done((f32[16,128]{1,0:T(8,128)S(1)}, f32[16,128]{1,0:T(8,128)S(1)}, u32[]{:S(2)}, u32[]{:S(2)}) %collective-permute-start.6) | collective-permute-done | bytes 8224 | tf_op jit(solution)/shard_map/cond/branch_1_fun/ppermute | solution.py:431
  46.5 0.1 hop.7
  46.6 0.3 conditional.17
  46.6 0.3 finish.6
  46.9 0.0 copy-start.20
  46.9 0.6 %copy-done.20 = bf16[64,256]{1,0:T(8,128)(2,1)} copy-done((bf16[64,256]{1,0:T(8,128)(2,1)}, bf16[64,256]{1,0:T(8,128)(2,1)S(1)}, u32[]{:S(2)}) %copy-start.20) | copy-done | bytes 32792
  (13 shorter events, 0.1 us)
Async XLA Ops:
  0.0 18.3 %copy-start = (f32[16,64]{1,0:T(8,128)S(1)}, f32[16,64]{1,0:T(8,128)}, u32[]{:S(2)}) copy-start(f32[16,64]{1,0:T(8,128)} %get-tuple-element.243.rates_ref) | copy-start | bytes 12292 | tf_op jit(solution)/shard_map/cond
  0.0 18.3 %copy-start.5 = (f32[16,64]{1,0:T(8,128)S(1)}, f32[16,64]{1,0:T(8,128)}, u32[]{:S(2)}) copy-start(f32[16,64]{1,0:T(8,128)} %get-tuple-element.242.residue_ref) | copy-start | bytes 12292 | tf_op jit(solution)/shard_map/cond
  0.0 18.3 %copy-start.10 = (f32[3,3,64]{2,1,0:T(4,128)S(1)}, f32[3,3,64]{2,1,0:T(4,128)}, u32[]{:S(2)}) copy-start(f32[3,3,64]{2,1,0:T(4,128)} %get-tuple-element.241.short_ref) | copy-start | bytes 6916 | tf_op jit(solution)/shard_map/cond
  0.0 18.3 %copy-start.15 = (f32[1,64]{1,0:T(1,128)S(1)}, f32[1,64]{1,0:T(1,128)}, u32[]{:S(2)}) copy-start(f32[1,64]{1,0:T(1,128)} %get-tuple-element.244.skip_ref) | copy-start | bytes 772 | tf_op jit(solution)/shard_map/cond
  37.0 2.6 %collective-permute-start.5 = (f32[16,128]{1,0:T(8,128)S(1)}, f32[16,128]{1,0:T(8,128)S(1)}, u32[]{:S(2)}, u32[]{:S(2)}) collective-permute-start(f32[16,128]{1,0:T(8,128)S(1)} %get-tuple-element.458), channel_id=1, source_target_pairs={{320,452},{324,448},{328,460},{332,456},{336,468},{340,464},{344,4... | collective-permute-start | bytes 24584 | tf_op jit(solution)/shard_map/cond/branch_1_fun/ppermute | solution.py:427
  37.7 8.8 %collective-permute-start.6 = (f32[16,128]{1,0:T(8,128)S(1)}, f32[16,128]{1,0:T(8,128)S(1)}, u32[]{:S(2)}, u32[]{:S(2)}) collective-permute-start(f32[16,128]{1,0:T(8,128)S(1)} %get-tuple-element.457), channel_id=1, source_target_pairs={{320,388},{324,384},{328,396},{332,392},{336,404},{340,400},{344,4... | collective-permute-start | bytes 24584 | tf_op jit(solution)/shard_map/cond/branch_1_fun/ppermute | solution.py:431
  46.9 0.6 %copy-start.20 = (bf16[64,256]{1,0:T(8,128)(2,1)}, bf16[64,256]{1,0:T(8,128)(2,1)S(1)}, u32[]{:S(2)}) copy-start(bf16[64,256]{1,0:T(8,128)(2,1)S(1)} %get-tuple-element.559) | copy-start | bytes 98308

commit v11 on v9

--- a/solution.py
+++ b/solution.py
@@ -408,7 +408,7 @@
     results = [None]
     for k in range(1, far_count, 2):
         sums = int(k + 1 < far_count)
-        full = k != 3
+        full = k > 3
 
         two = jnp.where(far == k - 1, row, total)
 

time: 48 us -> 48 us (level)
  no operation moved by 1% of the time
where the time goes in v11:
time: 48 us; the launch traced here: 47.8 us
  blocking collectives  33.1 us (69%)
  waiting for transfers between devices  6.82 us (14%)
  Pallas kernels  4.43 us (9%)
  starting transfers between devices  2.58 us (5%)
  local copies, waits for them, and re-layouts  0.63 us (1%)
    all_to_all x1, blocking collectives, row_of_shards(): lax.all_to_all(send, 'near', 0, 0, tiled=True)  17.9 us
    all_to_all x1, blocking collectives, row_of_shards(): parts = lax.all_to_all(project(tokens, weight), 'chan', 0, 0, tiled=True)  15.2 us
    ppermute x1, waiting for transfers between devices, odd_row(): extra = [lax.ppermute(two, ('far', 'near'), steps)]  6.82 us
    pallas_call x1, Pallas kernels, project(): pl.pallas_call(project_kernel, in_specs=[HBM, HBM], out_shape=pltpu.VMEM(...  3.06 us
    ppermute x1, starting transfers between devices, odd_row(): extra = [lax.ppermute(two, ('far', 'near'), steps)]  1.92 us
  transfers between devices with their start and end apart: 2, of which 1 were waited for; matrix products, arithmetic and copies ran while one was open for 0% of the time, Pallas kernels for 0%

profile of v11, /device:TPU:385, one launch (start us, length us, event | category | flops | bytes accessed | tf_op | source)
XLA Modules:
  0.0 47.8 jit_solution(9322630277436967234)
XLA Ops:
  0.0 36.6 %conditional.11 = ((f32[16,128]{1,0:T(8,128)S(1)}, f32[24,128]{1,0:T(8,128)S(1)}, f32[320,128]{1,0:T(8,128)S(1)})) conditional(s32[]{:T(128)} %convert_element_type.30, () %tuple.95, (bf16[256,2048]{1,0:T(8,128)(2,1)}, bf16[3,2048,256]{2,1,0:T(8,128)(2,1)}, f32[3,3,64]{2,1,0:T(4,128)}, f32[16,64]{1,0:T(8,128)}, f32[16,64]{1,0:T(8,128)}, ...), branch_computations={%region_0.1_spmd, %region_1.2_spmd} | conditional | bytes 1878160 | solution.py:401
  0.0 0.0 copy-start.15
  0.0 3.1 %project.5 = f32[4,3,128,128]{3,2,1,0:T(8,128)S(1)} custom-call(bf16[256,2048]{1,0:T(8,128)(2,1)} %get-tuple-element.237.tok_hbm, bf16[3,2048,256]{2,1,0:T(8,128)(2,1)} %get-tuple-element.238.w_hbm), custom_call_target="tpu_custom_call" | custom-call | tf_op jit(solution)/shard_map/cond/branch_1_fun/project/pallas_call | solution.py:80
  3.1 15.2 %all_to_all.40.part_ref = f32[4,3,128,128]{3,2,1,0:T(8,128)S(1)} all-to-all(f32[4,3,128,128]{3,2,1,0:T(8,128)S(1)} %project.5), channel_id=1, replica_groups=mesh['far'=8,'near'=16,'chan'=4] {'chan'}, dimensions={0} | all-to-all | bytes 1572864 | tf_op jit(solution)/shard_map/cond/branch_1_fun/all_to_all | solution.py:390
  18.3 0.0 copy-done
  18.3 0.0 copy-done.5
  18.3 0.0 copy-done.10
  18.3 0.0 copy-done.15
  18.3 0.3 local.5
  18.6 17.9 %all_to_all.41.got_ref = f32[16,16,128]{2,1,0:T(8,128)S(1)} all-to-all(f32[16,16,128]{2,1,0:T(8,128)S(1)} %get-tuple-element.243), channel_id=1, replica_groups=mesh['far'=8,'near'=16,'chan'=4] {'near'}, dimensions={0} | all-to-all | bytes 262144 | tf_op jit(solution)/shard_map/cond/branch_1_fun/all_to_all | solution.py:392
  36.5 0.1 near_sums.5
  36.7 0.1 first_sum.1
  36.7 0.5 %conditional.14 = ((f32[320,128]{1,0:T(8,128)S(1)}, f32[128,128]{1,0:T(8,128)S(1)})) conditional(s32[]{:T(128)} %convert_element_type.30, () %tuple.101, f32[320,128]{1,0:T(8,128)S(1)} %get-tuple-element.420), branch_computations={%region_10.11_spmd, %region_11.12_spmd} | conditional | bytes 8 | solution.py:433
  36.8 0.5 within.5
  37.3 9.6 %conditional.16 = ((f32[16,128]{1,0:T(8,128)S(1)}, f32[16,128]{1,0:T(8,128)S(1)}, f32[24,128]{1,0:T(8,128)S(1)}, f32[320,128]{1,0:T(8,128)S(1)}, f32[128,128]{1,0:T(8,128)S(1)}, /*index=5*/f32[16,128]{1,0:T(8,128)S(1)})) conditional(s32[]{:T(128)} %convert_element_type.32, () %tuple.104, (s32[]{:T(128)}, f32[16,128]{1,0:T(8,128)S(1)}, pred[]{:T(512)}, ...), branch_computations={%region_16.17_spmd, %region_17.20_spmd} | conditional | flops 4099 | bytes 1976633 | solution.py:427
  37.3 0.7 %collective-permute-start.5 = (f32[16,128]{1,0:T(8,128)S(1)}, f32[16,128]{1,0:T(8,128)S(1)}, u32[]{:S(2)}, u32[]{:S(2)}) collective-permute-start(f32[16,128]{1,0:T(8,128)S(1)} %get-tuple-element.448), channel_id=1, source_target_pairs={{320,452},{324,448},{328,460},{332,456},{336,468},{340,464},{344,4... | collective-permute-start | bytes 24584 | tf_op jit(solution)/shard_map/cond/branch_1_fun/ppermute | solution.py:417
  38.0 1.9 %collective-permute-start.6 = (f32[16,128]{1,0:T(8,128)S(1)}, f32[16,128]{1,0:T(8,128)S(1)}, u32[]{:S(2)}, u32[]{:S(2)}) collective-permute-start(f32[16,128]{1,0:T(8,128)S(1)} %get-tuple-element.447), channel_id=1, source_target_pairs={{320,388},{324,384},{328,396},{332,392},{336,404},{340,400},{344,4... | collective-permute-start | bytes 24584 | tf_op jit(solution)/shard_map/cond/branch_1_fun/ppermute | solution.py:421
  40.0 0.0 collective-permute-done.5.refs_0_
  40.0 6.8 %collective-permute-done.6.refs_1_.refs_6_ = f32[16,128]{1,0:T(8,128)S(1)} collective-permute-done((f32[16,128]{1,0:T(8,128)S(1)}, f32[16,128]{1,0:T(8,128)S(1)}, u32[]{:S(2)}, u32[]{:S(2)}) %collective-permute-start.6) | collective-permute-done | bytes 8224 | tf_op jit(solution)/shard_map/cond/branch_1_fun/ppermute | solution.py:421
  46.8 0.1 hop.7
  46.9 0.3 conditional.17
  46.9 0.3 finish.6
  47.2 0.0 copy-start.20
  47.2 0.6 %copy-done.20 = bf16[64,256]{1,0:T(8,128)(2,1)} copy-done((bf16[64,256]{1,0:T(8,128)(2,1)}, bf16[64,256]{1,0:T(8,128)(2,1)S(1)}, u32[]{:S(2)}) %copy-start.20) | copy-done | bytes 32792
  (13 shorter events, 0.1 us)
Async XLA Ops:
  0.0 18.3 %copy-start = (f32[16,64]{1,0:T(8,128)S(1)}, f32[16,64]{1,0:T(8,128)}, u32[]{:S(2)}) copy-start(f32[16,64]{1,0:T(8,128)} %get-tuple-element.241.rates_ref) | copy-start | bytes 12292 | tf_op jit(solution)/shard_map/cond
  0.0 18.3 %copy-start.5 = (f32[16,64]{1,0:T(8,128)S(1)}, f32[16,64]{1,0:T(8,128)}, u32[]{:S(2)}) copy-start(f32[16,64]{1,0:T(8,128)} %get-tuple-element.240.residue_ref) | copy-start | bytes 12292 | tf_op jit(solution)/shard_map/cond
  0.0 18.3 %copy-start.10 = (f32[3,3,64]{2,1,0:T(4,128)S(1)}, f32[3,3,64]{2,1,0:T(4,128)}, u32[]{:S(2)}) copy-start(f32[3,3,64]{2,1,0:T(4,128)} %get-tuple-element.239.short_ref) | copy-start | bytes 6916 | tf_op jit(solution)/shard_map/cond
  0.0 18.3 %copy-start.15 = (f32[1,64]{1,0:T(1,128)S(1)}, f32[1,64]{1,0:T(1,128)}, u32[]{:S(2)}) copy-start(f32[1,64]{1,0:T(1,128)} %get-tuple-element.242.skip_ref) | copy-start | bytes 772 | tf_op jit(solution)/shard_map/cond
  37.3 2.6 %collective-permute-start.5 = (f32[16,128]{1,0:T(8,128)S(1)}, f32[16,128]{1,0:T(8,128)S(1)}, u32[]{:S(2)}, u32[]{:S(2)}) collective-permute-start(f32[16,128]{1,0:T(8,128)S(1)} %get-tuple-element.448), channel_id=1, source_target_pairs={{320,452},{324,448},{328,460},{332,456},{336,468},{340,464},{344,4... | collective-permute-start | bytes 24584 | tf_op jit(solution)/shard_map/cond/branch_1_fun/ppermute | solution.py:417
  38.0 8.8 %collective-permute-start.6 = (f32[16,128]{1,0:T(8,128)S(1)}, f32[16,128]{1,0:T(8,128)S(1)}, u32[]{:S(2)}, u32[]{:S(2)}) collective-permute-start(f32[16,128]{1,0:T(8,128)S(1)} %get-tuple-element.447), channel_id=1, source_target_pairs={{320,388},{324,384},{328,396},{332,392},{336,404},{340,400},{344,4... | collective-permute-start | bytes 24584 | tf_op jit(solution)/shard_map/cond/branch_1_fun/ppermute | solution.py:421
  47.2 0.6 %copy-start.20 = (bf16[64,256]{1,0:T(8,128)(2,1)}, bf16[64,256]{1,0:T(8,128)(2,1)S(1)}, u32[]{:S(2)}) copy-start(bf16[64,256]{1,0:T(8,128)(2,1)S(1)} %get-tuple-element.545) | copy-start | bytes 98308

commit v12 on v11

--- a/solution.py
+++ b/solution.py
@@ -417,7 +417,7 @@
             sources = [lax.ppermute(block, ("far", "near"), crossed(max(k - 2, 0), k))]
             extra = []
             if k > 1:
-                steps = crossed(k - 2, k - 1) + crossed(k - 1, k)
+                steps = crossed(k - 2, k - 1) + [((k - 1) * NEAR + i, k * NEAR + i) for i in range(NEAR)]
                 extra = [lax.ppermute(two, ("far", "near"), steps)]
                 sources += extra
             return hop(shard_rows, sums, sources, *work_of(far == k, full), *extra)

time: 48 us -> 48 us (level)
  no operation moved by 1% of the time
where the time goes in v12:
time: 48 us; the launch traced here: 47.8 us
  blocking collectives  33.1 us (69%)
  waiting for transfers between devices  6.82 us (14%)
  Pallas kernels  4.43 us (9%)
  starting transfers between devices  2.58 us (5%)
  local copies, waits for them, and re-layouts  0.63 us (1%)
    all_to_all x1, blocking collectives, row_of_shards(): lax.all_to_all(send, 'near', 0, 0, tiled=True)  17.9 us
    all_to_all x1, blocking collectives, row_of_shards(): parts = lax.all_to_all(project(tokens, weight), 'chan', 0, 0, tiled=True)  15.2 us
    ppermute x1, waiting for transfers between devices, odd_row(): extra = [lax.ppermute(two, ('far', 'near'), steps)]  6.82 us
    pallas_call x1, Pallas kernels, project(): pl.pallas_call(project_kernel, in_specs=[HBM, HBM], out_shape=pltpu.VMEM(...  3.06 us
    ppermute x1, starting transfers between devices, odd_row(): extra = [lax.ppermute(two, ('far', 'near'), steps)]  1.92 us
  transfers between devices with their start and end apart: 2, of which 1 were waited for; matrix products, arithmetic and copies ran while one was open for 0% of the time, Pallas kernels for 0%

profile of v12, /device:TPU:385, one launch (start us, length us, event | category | flops | bytes accessed | tf_op | source)
XLA Modules:
  0.0 47.8 jit_solution(5873577704058245425)
XLA Ops:
  0.0 36.6 %conditional.11 = ((f32[16,128]{1,0:T(8,128)S(1)}, f32[24,128]{1,0:T(8,128)S(1)}, f32[320,128]{1,0:T(8,128)S(1)})) conditional(s32[]{:T(128)} %convert_element_type.30, () %tuple.95, (bf16[256,2048]{1,0:T(8,128)(2,1)}, bf16[3,2048,256]{2,1,0:T(8,128)(2,1)}, f32[3,3,64]{2,1,0:T(4,128)}, f32[16,64]{1,0:T(8,128)}, f32[16,64]{1,0:T(8,128)}, ...), branch_computations={%region_0.1_spmd, %region_1.2_spmd} | conditional | bytes 1878160 | solution.py:401
  0.0 0.0 copy-start.15
  0.0 3.1 %project.5 = f32[4,3,128,128]{3,2,1,0:T(8,128)S(1)} custom-call(bf16[256,2048]{1,0:T(8,128)(2,1)} %get-tuple-element.237.tok_hbm, bf16[3,2048,256]{2,1,0:T(8,128)(2,1)} %get-tuple-element.238.w_hbm), custom_call_target="tpu_custom_call" | custom-call | tf_op jit(solution)/shard_map/cond/branch_1_fun/project/pallas_call | solution.py:80
  3.1 15.2 %all_to_all.40.part_ref = f32[4,3,128,128]{3,2,1,0:T(8,128)S(1)} all-to-all(f32[4,3,128,128]{3,2,1,0:T(8,128)S(1)} %project.5), channel_id=1, replica_groups=mesh['far'=8,'near'=16,'chan'=4] {'chan'}, dimensions={0} | all-to-all | bytes 1572864 | tf_op jit(solution)/shard_map/cond/branch_1_fun/all_to_all | solution.py:390
  18.3 0.0 copy-done
  18.3 0.0 copy-done.5
  18.3 0.0 copy-done.10
  18.3 0.0 copy-done.15
  18.3 0.3 local.5
  18.6 17.9 %all_to_all.41.got_ref = f32[16,16,128]{2,1,0:T(8,128)S(1)} all-to-all(f32[16,16,128]{2,1,0:T(8,128)S(1)} %get-tuple-element.243), channel_id=1, replica_groups=mesh['far'=8,'near'=16,'chan'=4] {'near'}, dimensions={0} | all-to-all | bytes 262144 | tf_op jit(solution)/shard_map/cond/branch_1_fun/all_to_all | solution.py:392
  36.5 0.1 near_sums.5
  36.7 0.1 first_sum.1
  36.7 0.5 %conditional.14 = ((f32[320,128]{1,0:T(8,128)S(1)}, f32[128,128]{1,0:T(8,128)S(1)})) conditional(s32[]{:T(128)} %convert_element_type.30, () %tuple.101, f32[320,128]{1,0:T(8,128)S(1)} %get-tuple-element.420), branch_computations={%region_10.11_spmd, %region_11.12_spmd} | conditional | bytes 8 | solution.py:433
  36.8 0.5 within.5
  37.3 9.6 %conditional.16 = ((f32[16,128]{1,0:T(8,128)S(1)}, f32[16,128]{1,0:T(8,128)S(1)}, f32[24,128]{1,0:T(8,128)S(1)}, f32[320,128]{1,0:T(8,128)S(1)}, f32[128,128]{1,0:T(8,128)S(1)}, /*index=5*/f32[16,128]{1,0:T(8,128)S(1)})) conditional(s32[]{:T(128)} %convert_element_type.32, () %tuple.104, (s32[]{:T(128)}, f32[16,128]{1,0:T(8,128)S(1)}, pred[]{:T(512)}, ...), branch_computations={%region_16.17_spmd, %region_17.20_spmd} | conditional | flops 4099 | bytes 1976633 | solution.py:427
  37.3 0.7 %collective-permute-start.5 = (f32[16,128]{1,0:T(8,128)S(1)}, f32[16,128]{1,0:T(8,128)S(1)}, u32[]{:S(2)}, u32[]{:S(2)}) collective-permute-start(f32[16,128]{1,0:T(8,128)S(1)} %get-tuple-element.448), channel_id=1, source_target_pairs={{320,452},{324,448},{328,460},{332,456},{336,468},{340,464},{344,4... | collective-permute-start | bytes 24584 | tf_op jit(solution)/shard_map/cond/branch_1_fun/ppermute | solution.py:417
  38.0 1.9 %collective-permute-start.6 = (f32[16,128]{1,0:T(8,128)S(1)}, f32[16,128]{1,0:T(8,128)S(1)}, u32[]{:S(2)}, u32[]{:S(2)}) collective-permute-start(f32[16,128]{1,0:T(8,128)S(1)} %get-tuple-element.447), channel_id=1, source_target_pairs={{320,388},{324,384},{328,396},{332,392},{336,404},{340,400},{344,4... | collective-permute-start | bytes 24584 | tf_op jit(solution)/shard_map/cond/branch_1_fun/ppermute | solution.py:421
  40.0 0.0 collective-permute-done.5.refs_0_
  40.0 6.8 %collective-permute-done.6.refs_1_.refs_6_ = f32[16,128]{1,0:T(8,128)S(1)} collective-permute-done((f32[16,128]{1,0:T(8,128)S(1)}, f32[16,128]{1,0:T(8,128)S(1)}, u32[]{:S(2)}, u32[]{:S(2)}) %collective-permute-start.6) | collective-permute-done | bytes 8224 | tf_op jit(solution)/shard_map/cond/branch_1_fun/ppermute | solution.py:421
  46.8 0.1 hop.7
  46.9 0.3 conditional.17
  46.9 0.3 finish.6
  47.2 0.0 copy-start.20
  47.2 0.6 %copy-done.20 = bf16[64,256]{1,0:T(8,128)(2,1)} copy-done((bf16[64,256]{1,0:T(8,128)(2,1)}, bf16[64,256]{1,0:T(8,128)(2,1)S(1)}, u32[]{:S(2)}) %copy-start.20) | copy-done | bytes 32792
  (13 shorter events, 0.1 us)
Async XLA Ops:
  0.0 18.3 %copy-start = (f32[16,64]{1,0:T(8,128)S(1)}, f32[16,64]{1,0:T(8,128)}, u32[]{:S(2)}) copy-start(f32[16,64]{1,0:T(8,128)} %get-tuple-element.241.rates_ref) | copy-start | bytes 12292 | tf_op jit(solution)/shard_map/cond
  0.0 18.3 %copy-start.5 = (f32[16,64]{1,0:T(8,128)S(1)}, f32[16,64]{1,0:T(8,128)}, u32[]{:S(2)}) copy-start(f32[16,64]{1,0:T(8,128)} %get-tuple-element.240.residue_ref) | copy-start | bytes 12292 | tf_op jit(solution)/shard_map/cond
  0.0 18.3 %copy-start.10 = (f32[3,3,64]{2,1,0:T(4,128)S(1)}, f32[3,3,64]{2,1,0:T(4,128)}, u32[]{:S(2)}) copy-start(f32[3,3,64]{2,1,0:T(4,128)} %get-tuple-element.239.short_ref) | copy-start | bytes 6916 | tf_op jit(solution)/shard_map/cond
  0.0 18.3 %copy-start.15 = (f32[1,64]{1,0:T(1,128)S(1)}, f32[1,64]{1,0:T(1,128)}, u32[]{:S(2)}) copy-start(f32[1,64]{1,0:T(1,128)} %get-tuple-element.242.skip_ref) | copy-start | bytes 772 | tf_op jit(solution)/shard_map/cond
  37.3 2.6 %collective-permute-start.5 = (f32[16,128]{1,0:T(8,128)S(1)}, f32[16,128]{1,0:T(8,128)S(1)}, u32[]{:S(2)}, u32[]{:S(2)}) collective-permute-start(f32[16,128]{1,0:T(8,128)S(1)} %get-tuple-element.448), channel_id=1, source_target_pairs={{320,452},{324,448},{328,460},{332,456},{336,468},{340,464},{344,4... | collective-permute-start | bytes 24584 | tf_op jit(solution)/shard_map/cond/branch_1_fun/ppermute | solution.py:417
  38.0 8.8 %collective-permute-start.6 = (f32[16,128]{1,0:T(8,128)S(1)}, f32[16,128]{1,0:T(8,128)S(1)}, u32[]{:S(2)}, u32[]{:S(2)}) collective-permute-start(f32[16,128]{1,0:T(8,128)S(1)} %get-tuple-element.447), channel_id=1, source_target_pairs={{320,388},{324,384},{328,396},{332,392},{336,404},{340,400},{344,4... | collective-permute-start | bytes 24584 | tf_op jit(solution)/shard_map/cond/branch_1_fun/ppermute | solution.py:421
  47.2 0.6 %copy-start.20 = (bf16[64,256]{1,0:T(8,128)(2,1)}, bf16[64,256]{1,0:T(8,128)(2,1)S(1)}, u32[]{:S(2)}) copy-start(bf16[64,256]{1,0:T(8,128)(2,1)S(1)} %get-tuple-element.545) | copy-start | bytes 98308

commit v13 on v9

--- a/solution.py
+++ b/solution.py
@@ -413,12 +413,14 @@
         two = jnp.where(far == k - 1, row, total)
 
         def odd_row(k=k, total=total, two=two, sums=sums, full=full):
-            block = jnp.where(far == max(k - 2, 0), total, none)
+            final = k + 1 == far_count
+            block = total if final else jnp.where(far == max(k - 2, 0), total, none)
             sources = [lax.ppermute(block, ("far", "near"), crossed(max(k - 2, 0), k))]
             extra = []
             if k > 1:
                 steps = crossed(k - 2, k - 1) + crossed(k - 1, k)
-                extra = [lax.ppermute(two, ("far", "near"), steps)]
+                both = jnp.where(far == k - 1, row, total) if final else two
+                extra = [lax.ppermute(both, ("far", "near"), steps)]
                 sources += extra
             return hop(shard_rows, sums, sources, *work_of(far == k, full), *extra)
 

time: 48 us -> 48 us (level)
  the two profiles are of different devices: /device:TPU:385 before, /device:TPU:449 now
where the time goes in v13:
time: 48 us; the launch traced here: 47.8 us
  blocking collectives  33.1 us (69%)
  waiting for transfers between devices  6.82 us (14%)
  Pallas kernels  4.41 us (9%)
  starting transfers between devices  2.58 us (5%)
  local copies, waits for them, and re-layouts  0.63 us (1%)
    all_to_all x1, blocking collectives, row_of_shards(): lax.all_to_all(send, 'near', 0, 0, tiled=True)  17.9 us
    all_to_all x1, blocking collectives, row_of_shards(): parts = lax.all_to_all(project(tokens, weight), 'chan', 0, 0, tiled=True)  15.2 us
    ppermute x1, waiting for transfers between devices, odd_row(): sources = [lax.ppermute(block, ('far', 'near'), crossed(max(k - 2, 0), k))]  6.38 us
    pallas_call x1, Pallas kernels, project(): pl.pallas_call(project_kernel, in_specs=[HBM, HBM], out_shape=pltpu.VMEM(...  3.04 us
    ppermute x1, starting transfers between devices, odd_row(): extra = [lax.ppermute(both, ('far', 'near'), steps)]  1.29 us
    ppermute x1, starting transfers between devices, odd_row(): sources = [lax.ppermute(block, ('far', 'near'), crossed(max(k - 2, 0), k))]  1.29 us
  transfers between devices with their start and end apart: 2, of which 2 were waited for; matrix products, arithmetic and copies ran while one was open for 0% of the time, Pallas kernels for 8%

profile of v13, /device:TPU:449, one launch (start us, length us, event | category | flops | bytes accessed | tf_op | source)
XLA Modules:
  0.0 47.8 jit_solution(15926265973957339520)
XLA Ops:
  0.0 0.1 first_sum.1
  0.2 46.7 %conditional.16 = ((f32[16,128]{1,0:T(8,128)S(1)}, f32[16,128]{1,0:T(8,128)S(1)}, f32[24,128]{1,0:T(8,128)S(1)}, f32[320,128]{1,0:T(8,128)S(1)}, f32[128,128]{1,0:T(8,128)S(1)}, /*index=5*/f32[16,128]{1,0:T(8,128)S(1)})) conditional(s32[]{:T(128)} %convert_element_type.32, () %tuple.109, (f32[16,128]{1,0:T(8,128)S(1)}, s32[]{:T(128)}, ...), branch_computations={%region_16.17_spmd, %region_17.20_spmd} | conditional | flops 2051 | bytes 1968440 | solution.py:429
  0.2 1.3 %collective-permute-start.6 = (f32[16,128]{1,0:T(8,128)S(1)}, f32[16,128]{1,0:T(8,128)S(1)}, u32[]{:S(2)}, u32[]{:S(2)}) collective-permute-start(f32[16,128]{1,0:T(8,128)S(1)} %broadcast_select_fusion.5), channel_id=1, source_target_pairs={{320,388},{324,384},{328,396},{332,392},{336,404},{340,400},{344,4... | collective-permute-start | bytes 24584 | tf_op jit(solution)/shard_map/cond/branch_1_fun/ppermute | solution.py:423
  1.5 1.3 %collective-permute-start.5 = (f32[16,128]{1,0:T(8,128)S(1)}, f32[16,128]{1,0:T(8,128)S(1)}, u32[]{:S(2)}, u32[]{:S(2)}) collective-permute-start(f32[16,128]{1,0:T(8,128)S(1)} %get-tuple-element.337), channel_id=1, source_target_pairs={{320,452},{324,448},{328,460},{332,456},{336,468},{340,464},{344,4... | collective-permute-start | bytes 24584 | tf_op jit(solution)/shard_map/cond/branch_1_fun/ppermute | solution.py:418
  2.8 37.1 %conditional.3 = ((f32[16,128]{1,0:T(8,128)S(1)}, f32[24,128]{1,0:T(8,128)S(1)}, f32[320,128]{1,0:T(8,128)S(1)}, f32[128,128]{1,0:T(8,128)S(1)})) conditional(s32[]{:T(128)} %convert_element_type.22, () %tuple.78, (bf16[256,2048]{1,0:T(8,128)(2,1)}, bf16[3,2048,256]{2,1,0:T(8,128)(2,1)}, f32[3,3,64]{2,1,0:T(4,128)}, f32[16,64]{1,0:T(8,128)}, ...), branch_computations={%region_18.18_spmd, %region_19.19_spmd} | conditional | bytes 1878168 | solution.py:401
  2.8 0.0 copy-start.4
  2.8 0.0 copy-start.9
  2.9 0.0 copy-start.14
  2.9 0.0 copy-start.19
  2.9 3.0 %project.9 = f32[4,3,128,128]{3,2,1,0:T(8,128)S(1)} custom-call(bf16[256,2048]{1,0:T(8,128)(2,1)} %get-tuple-element.323.tok_hbm, bf16[3,2048,256]{2,1,0:T(8,128)(2,1)} %get-tuple-element.324.w_hbm), custom_call_target="tpu_custom_call" | custom-call | tf_op jit(solution)/shard_map/cond/branch_1_fun/cond/branch_1_fun/project/pallas_call | solution.py:80
  5.9 15.2 %all_to_all.48.part_ref = f32[4,3,128,128]{3,2,1,0:T(8,128)S(1)} all-to-all(f32[4,3,128,128]{3,2,1,0:T(8,128)S(1)} %project.9), channel_id=1, replica_groups=mesh['far'=8,'near'=16,'chan'=4] {'chan'}, dimensions={0} | all-to-all | bytes 1572864 | tf_op jit(solution)/shard_map/cond/branch_1_fun/cond/branch_1_fun/all_to_all | solution.py:390
  21.1 0.0 copy-done.4
  21.1 0.0 copy-done.9
  21.1 0.3 local.9
  21.4 17.9 %all_to_all.49.got_ref = f32[16,16,128]{2,1,0:T(8,128)S(1)} all-to-all(f32[16,16,128]{2,1,0:T(8,128)S(1)} %get-tuple-element.329), channel_id=1, replica_groups=mesh['far'=8,'near'=16,'chan'=4] {'near'}, dimensions={0} | all-to-all | bytes 262144 | tf_op jit(solution)/shard_map/cond/branch_1_fun/cond/branch_1_fun/all_to_all | solution.py:392
  39.4 0.1 near_sums.9
  39.5 0.5 within.8
  40.0 0.4 collective-permute-done.6.refs_1_.refs_6_
  40.4 6.4 %collective-permute-done.5.refs_0_ = f32[16,128]{1,0:T(8,128)S(1)} collective-permute-done((f32[16,128]{1,0:T(8,128)S(1)}, f32[16,128]{1,0:T(8,128)S(1)}, u32[]{:S(2)}, u32[]{:S(2)}) %collective-permute-start.5) | collective-permute-done | bytes 8224 | tf_op jit(solution)/shard_map/cond/branch_1_fun/ppermute | solution.py:418
  46.8 0.1 hop.7
  46.9 0.3 conditional.17
  46.9 0.3 finish.10
  47.2 0.0 copy-start.20
  47.2 0.6 %copy-done.20 = bf16[64,256]{1,0:T(8,128)(2,1)} copy-done((bf16[64,256]{1,0:T(8,128)(2,1)}, bf16[64,256]{1,0:T(8,128)(2,1)S(1)}, u32[]{:S(2)}) %copy-start.20) | copy-done | bytes 32792
  (13 shorter events, 0.1 us)
Async XLA Ops:
  0.2 40.2 %collective-permute-start.6 = (f32[16,128]{1,0:T(8,128)S(1)}, f32[16,128]{1,0:T(8,128)S(1)}, u32[]{:S(2)}, u32[]{:S(2)}) collective-permute-start(f32[16,128]{1,0:T(8,128)S(1)} %broadcast_select_fusion.5), channel_id=1, source_target_pairs={{320,388},{324,384},{328,396},{332,392},{336,404},{340,400},{344,4... | collective-permute-start | bytes 24584 | tf_op jit(solution)/shard_map/cond/branch_1_fun/ppermute | solution.py:423
  1.5 45.3 %collective-permute-start.5 = (f32[16,128]{1,0:T(8,128)S(1)}, f32[16,128]{1,0:T(8,128)S(1)}, u32[]{:S(2)}, u32[]{:S(2)}) collective-permute-start(f32[16,128]{1,0:T(8,128)S(1)} %get-tuple-element.337), channel_id=1, source_target_pairs={{320,452},{324,448},{328,460},{332,456},{336,468},{340,464},{344,4... | collective-permute-start | bytes 24584 | tf_op jit(solution)/shard_map/cond/branch_1_fun/ppermute | solution.py:418
  2.8 18.3 %copy-start.4 = (f32[16,64]{1,0:T(8,128)S(1)}, f32[16,64]{1,0:T(8,128)}, u32[]{:S(2)}) copy-start(f32[16,64]{1,0:T(8,128)} %get-tuple-element.327.rates_ref) | copy-start | bytes 12292 | tf_op jit(solution)/shard_map/cond/branch_1_fun/cond
  2.8 18.3 %copy-start.9 = (f32[16,64]{1,0:T(8,128)S(1)}, f32[16,64]{1,0:T(8,128)}, u32[]{:S(2)}) copy-start(f32[16,64]{1,0:T(8,128)} %get-tuple-element.326.residue_ref) | copy-start | bytes 12292 | tf_op jit(solution)/shard_map/cond/branch_1_fun/cond
  2.9 18.3 %copy-start.14 = (f32[3,3,64]{2,1,0:T(4,128)S(1)}, f32[3,3,64]{2,1,0:T(4,128)}, u32[]{:S(2)}) copy-start(f32[3,3,64]{2,1,0:T(4,128)} %get-tuple-element.325.short_ref) | copy-start | bytes 6916 | tf_op jit(solution)/shard_map/cond/branch_1_fun/cond
  2.9 18.3 %copy-start.19 = (f32[1,64]{1,0:T(1,128)S(1)}, f32[1,64]{1,0:T(1,128)}, u32[]{:S(2)}) copy-start(f32[1,64]{1,0:T(1,128)} %get-tuple-element.328.skip_ref) | copy-start | bytes 772 | tf_op jit(solution)/shard_map/cond/branch_1_fun/cond
  47.2 0.6 %copy-start.20 = (bf16[64,256]{1,0:T(8,128)(2,1)}, bf16[64,256]{1,0:T(8,128)(2,1)S(1)}, u32[]{:S(2)}) copy-start(bf16[64,256]{1,0:T(8,128)(2,1)S(1)} %get-tuple-element.553) | copy-start | bytes 98308
